TPU v7x, 1024 devices: a whole 8x8x8 slice. The times are simulated.
1024 devices in a mesh: dp: 256 (over z, x, y_hi), tensor: 4 (over y_lo, core).
Axes of the slice: x: 8, y: 8 (y_hi: 4, y_lo: 2; y = y_hi * 2 + y_lo), z: 8, core: 2. Of those that a mesh axis runs over, the one named last changes fastest.
Arguments:
- picture_averaged_vectors: bfloat16 [49152, 1152], P('dp'), may hold values from -6 to 6
- picture_mapping_matrix: bfloat16 [1152, 1152], P(None, 'tensor'), may hold values from -0.1875 to 0.1875
- caption_averaged_vectors: bfloat16 [49152, 1152], P('dp'), may hold values from -6 to 6
- caption_mapping_matrix: bfloat16 [1152, 1152], P(None, 'tensor'), may hold values from -0.1875 to 0.1875
- sharpness_factor: float32 [1], replicated, may hold values from 3 to 8
- offset_term: float32 [1], replicated, may hold values from -4 to -1
- paired_caption_index: int32 [49152], P('dp'), may hold values from 0 to 49151, as said below
Outputs:
- img_grad: float32 [49152, 1152], P('dp', 'tensor')
- txt_grad: float32 [49152, 1152], P('dp', 'tensor')
Inputs may be any that keep to these rules, and one draw needn't show every extreme that they name: paired_caption_index[i] lies in the same aligned block of 192 rows as i, and each text is matched by exactly one image.
All inputs are finite; a program needn't handle non-finite values.
Results may differ from a plain program's by a relative error of at most 0.0041.
Values may be sent and summed in bfloat16 or wider, within the bound.
No kernel may reach another device: no remote copies, remote signals or barrier semaphores. Data moves between devices by JAX's collectives and lax.ppermute only.
A program may use at most 32 MiB of HBM per device.

v0:
```python
import jax
import jax.numpy as jnp
from jax import lax
from jax.sharding import PartitionSpec as P

SPAN = 8


def passed_along(block, axis, distance):
    devices = range(lax.axis_size(axis))
    route = [((i - distance) % len(devices), i) for i in devices]
    return lax.ppermute(block, axis, route)


def pair_weight(logits, sign):
    return (-16.0 * sign * jax.nn.sigmoid(-sign * logits)).astype(jnp.bfloat16)


def shards(
    picture_averaged_vectors,
    picture_mapping_matrix,
    caption_averaged_vectors,
    caption_mapping_matrix,
    sharpness_factor,
    offset_term,
    paired_caption_index,
):
    rows = picture_averaged_vectors.shape[0]
    similarity_multiplier = sharpness_factor[0]
    offset = offset_term[0]
    img_emb = jnp.dot(
        picture_averaged_vectors, picture_mapping_matrix, preferred_element_type=jnp.float32
    )
    txt_emb = jnp.dot(
        caption_averaged_vectors, caption_mapping_matrix, preferred_element_type=jnp.float32
    )
    sq_img, sq_txt = lax.psum(
        (jnp.sum(img_emb * img_emb, axis=1), jnp.sum(txt_emb * txt_emb, axis=1)), "tensor"
    )
    inv_img = lax.rsqrt(sq_img + 1e-06)
    inv_txt = lax.rsqrt(sq_txt + 1e-06)
    img_unit = img_emb * inv_img[:, None]
    txt_unit = txt_emb * inv_txt[:, None]
    img_low = img_unit.astype(jnp.bfloat16)
    txt_low = txt_unit.astype(jnp.bfloat16)
    first_row = lax.axis_index("dp") * rows
    contract_rows = (((0,), (0,)), ((), ()))
    local_column_span = txt_low.shape[1]
    local_ids = first_row + jnp.arange(rows, dtype=jnp.int32)
    own_sign = jnp.where(paired_caption_index[:, None] == local_ids[None, :], 1.0, -1.0).astype(
        jnp.float32
    )

    def visit(step, carry):
        block, block_grad, image_partial_sum = carry
        partial_value = jnp.dot(img_low, block.T, preferred_element_type=jnp.float32)
        logits = similarity_multiplier * lax.psum(partial_value, "tensor") + offset
        sign = jnp.where(step == 0, own_sign, -1.0)
        weight = pair_weight(logits, sign)
        image_partial_sum = image_partial_sum + jnp.dot(
            weight, block, preferred_element_type=jnp.float32
        )
        block_grad = block_grad + lax.dot_general(
            weight, img_low, contract_rows, preferred_element_type=jnp.float32
        )
        block = passed_along(block, "dp", -1)
        block_grad = passed_along(block_grad, "dp", -1)
        return (block, block_grad, image_partial_sum)

    start = (
        txt_low,
        jnp.zeros((rows, local_column_span), jnp.float32),
        jnp.zeros((rows, local_column_span), jnp.float32),
    )
    block, block_grad, image_partial_sum = lax.fori_loop(0, SPAN, visit, start)
    txt_sum = passed_along(block_grad, "dp", SPAN)
    img_dunit = similarity_multiplier * image_partial_sum
    txt_dunit = similarity_multiplier * txt_sum
    inner_img = jnp.sum(img_unit * img_dunit, axis=1)
    inner_txt = jnp.sum(txt_unit * txt_dunit, axis=1)
    inner_img, inner_txt = lax.psum((inner_img, inner_txt), "tensor")
    img_demb = inv_img[:, None] * (img_dunit - img_unit * inner_img[:, None])
    txt_demb = inv_txt[:, None] * (txt_dunit - txt_unit * inner_txt[:, None])
    highest = lax.Precision.HIGHEST
    img_part = jnp.dot(img_demb, picture_mapping_matrix.astype(jnp.float32).T, precision=highest)
    txt_part = jnp.dot(txt_demb, caption_mapping_matrix.astype(jnp.float32).T, precision=highest)
    img_grad, txt_grad = (
        lax.psum_scatter(img_part, "tensor", scatter_dimension=1, tiled=True),
        lax.psum_scatter(txt_part, "tensor", scatter_dimension=1, tiled=True),
    )
    return (img_grad, txt_grad)


def solution(mesh):
    in_specs = (
        P("dp", None),
        P(None, "tensor"),
        P("dp", None),
        P(None, "tensor"),
        P(),
        P(),
        P("dp"),
    )
    out_specs = (P("dp", "tensor"), P("dp", "tensor"))
    return jax.shard_map(shards, mesh=mesh, in_specs=in_specs, out_specs=out_specs, check_vma=False)
```

profile of v0, /device:TPU:1, one launch (start us, length us, event | category | flops | bytes accessed | tf_op | source)
XLA Modules:
  0.0 762.1 jit_solution(8412767829885105334)
XLA Ops:
  11.2 19.2 %all-reduce.1 = (f32[192]{0:T(256)S(1)}, f32[192]{0:T(256)S(1)}) all-reduce(f32[192]{0:T(256)S(1)} %get-tuple-element.200, f32[192]{0:T(256)S(1)} %get-tuple-element.202), channel_id=1, replica_groups=mesh['dp'=256,'tensor'=4] {'tensor'}, use_global_device_ids=true, to_apply=%region_3.0 | all-reduce | flops 384 | bytes 3072 | tf_op jit(solution)/shard_map/psum | solution.py:37
  30.7 633.7 %while.18 = (s32[]{:T(128)}, bf16[192,288]{1,0:T(8,128)(2,1)S(1)}, f32[192,288]{1,0:T(8,128)S(1)}, f32[192,288]{1,0:T(8,128)S(1)}, f32[]{:T(128)}, /*index=5*/bf...) while((s32[]{:T(128)}, bf16[192,288]{1,0:T(8,128)(2,1)S(1)}, ...), condition=%wide.region_6.7_spmd.clone, body=%wide.region_4.6_spmd.clone.sunk | while | flops 64862208 | bytes 4893980 | solution.py:75
  31.7 11.0 %collective-permute-start = (bf16[192,288]{1,0:T(8,128)(2,1)S(1)}, bf16[192,288]{1,0:T(8,128)(2,1)S(1)}, u32[]{:S(2)}, u32[]{:S(2)}) collective-permute-start(bf16[192,288]{1,0:T(8,128)(2,1)S(1)} %copy.19), channel_id=1, source_target_pairs={{4,0},{8,4},{12,8},{16,12},{20,16},{24,20},{28,24},{32,28},{36,32}... | collective-permute-start | bytes 331784 | tf_op jit(solution)/shard_map/while/body/eval_jaxpr/ppermute | solution.py:12
  42.8 46.0 %all-reduce.4.cloned.1.call-done = f32[192,192]{1,0:T(8,128)} async-done(((f32[192,192]{1,0:T(8,128)}), f32[192,192]{1,0:T(8,128)}) %all-reduce.4.cloned.1.call-update) | async-done | bytes 147472 | tf_op jit(solution)/shard_map/while/body/eval_jaxpr/psum | solution.py:57
  91.4 9.9 %collective-permute-start.1 = (f32[192,288]{1,0:T(8,128)S(1)}, f32[192,288]{1,0:T(8,128)S(1)}, u32[]{:S(2)}, u32[]{:S(2)}) collective-permute-start(f32[192,288]{1,0:T(8,128)S(1)} %convolution_add_fusion.4), channel_id=1, source_target_pairs={{4,0},{8,4},{12,8},{16,12},{20,16},{24,20},{28,24},{32,28},{36,32}... | collective-permute-start | bytes 663560 | tf_op jit(solution)/shard_map/while/body/eval_jaxpr/ppermute | solution.py:12
  111.4 11.5 %collective-permute-start = (bf16[192,288]{1,0:T(8,128)(2,1)S(1)}, bf16[192,288]{1,0:T(8,128)(2,1)S(1)}, u32[]{:S(2)}, u32[]{:S(2)}) collective-permute-start(bf16[192,288]{1,0:T(8,128)(2,1)S(1)} %copy.19), channel_id=1, source_target_pairs={{4,0},{8,4},{12,8},{16,12},{20,16},{24,20},{28,24},{32,28},{36,32}... | collective-permute-start | bytes 331784 | tf_op jit(solution)/shard_map/while/body/eval_jaxpr/ppermute | solution.py:12
  122.9 45.1 %all-reduce.4.cloned.1.call-done = f32[192,192]{1,0:T(8,128)} async-done(((f32[192,192]{1,0:T(8,128)}), f32[192,192]{1,0:T(8,128)}) %all-reduce.4.cloned.1.call-update) | async-done | bytes 147472 | tf_op jit(solution)/shard_map/while/body/eval_jaxpr/psum | solution.py:57
  170.7 9.9 %collective-permute-start.1 = (f32[192,288]{1,0:T(8,128)S(1)}, f32[192,288]{1,0:T(8,128)S(1)}, u32[]{:S(2)}, u32[]{:S(2)}) collective-permute-start(f32[192,288]{1,0:T(8,128)S(1)} %convolution_add_fusion.4), channel_id=1, source_target_pairs={{4,0},{8,4},{12,8},{16,12},{20,16},{24,20},{28,24},{32,28},{36,32}... | collective-permute-start | bytes 663560 | tf_op jit(solution)/shard_map/while/body/eval_jaxpr/ppermute | solution.py:12
  190.7 11.5 %collective-permute-start = (bf16[192,288]{1,0:T(8,128)(2,1)S(1)}, bf16[192,288]{1,0:T(8,128)(2,1)S(1)}, u32[]{:S(2)}, u32[]{:S(2)}) collective-permute-start(bf16[192,288]{1,0:T(8,128)(2,1)S(1)} %copy.19), channel_id=1, source_target_pairs={{4,0},{8,4},{12,8},{16,12},{20,16},{24,20},{28,24},{32,28},{36,32}... | collective-permute-start | bytes 331784 | tf_op jit(solution)/shard_map/while/body/eval_jaxpr/ppermute | solution.py:12
  202.2 45.1 %all-reduce.4.cloned.1.call-done = f32[192,192]{1,0:T(8,128)} async-done(((f32[192,192]{1,0:T(8,128)}), f32[192,192]{1,0:T(8,128)}) %all-reduce.4.cloned.1.call-update) | async-done | bytes 147472 | tf_op jit(solution)/shard_map/while/body/eval_jaxpr/psum | solution.py:57
  249.9 9.9 %collective-permute-start.1 = (f32[192,288]{1,0:T(8,128)S(1)}, f32[192,288]{1,0:T(8,128)S(1)}, u32[]{:S(2)}, u32[]{:S(2)}) collective-permute-start(f32[192,288]{1,0:T(8,128)S(1)} %convolution_add_fusion.4), channel_id=1, source_target_pairs={{4,0},{8,4},{12,8},{16,12},{20,16},{24,20},{28,24},{32,28},{36,32}... | collective-permute-start | bytes 663560 | tf_op jit(solution)/shard_map/while/body/eval_jaxpr/ppermute | solution.py:12
  261.5 7.5 collective-permute-done.1
  270.0 11.4 %collective-permute-start = (bf16[192,288]{1,0:T(8,128)(2,1)S(1)}, bf16[192,288]{1,0:T(8,128)(2,1)S(1)}, u32[]{:S(2)}, u32[]{:S(2)}) collective-permute-start(bf16[192,288]{1,0:T(8,128)(2,1)S(1)} %copy.19), channel_id=1, source_target_pairs={{4,0},{8,4},{12,8},{16,12},{20,16},{24,20},{28,24},{32,28},{36,32}... | collective-permute-start | bytes 331784 | tf_op jit(solution)/shard_map/while/body/eval_jaxpr/ppermute | solution.py:12
  281.4 44.8 %all-reduce.4.cloned.1.call-done = f32[192,192]{1,0:T(8,128)} async-done(((f32[192,192]{1,0:T(8,128)}), f32[192,192]{1,0:T(8,128)}) %all-reduce.4.cloned.1.call-update) | async-done | bytes 147472 | tf_op jit(solution)/shard_map/while/body/eval_jaxpr/psum | solution.py:57
  328.9 9.9 %collective-permute-start.1 = (f32[192,288]{1,0:T(8,128)S(1)}, f32[192,288]{1,0:T(8,128)S(1)}, u32[]{:S(2)}, u32[]{:S(2)}) collective-permute-start(f32[192,288]{1,0:T(8,128)S(1)} %convolution_add_fusion.4), channel_id=1, source_target_pairs={{4,0},{8,4},{12,8},{16,12},{20,16},{24,20},{28,24},{32,28},{36,32}... | collective-permute-start | bytes 663560 | tf_op jit(solution)/shard_map/while/body/eval_jaxpr/ppermute | solution.py:12
  348.9 11.5 %collective-permute-start = (bf16[192,288]{1,0:T(8,128)(2,1)S(1)}, bf16[192,288]{1,0:T(8,128)(2,1)S(1)}, u32[]{:S(2)}, u32[]{:S(2)}) collective-permute-start(bf16[192,288]{1,0:T(8,128)(2,1)S(1)} %copy.19), channel_id=1, source_target_pairs={{4,0},{8,4},{12,8},{16,12},{20,16},{24,20},{28,24},{32,28},{36,32}... | collective-permute-start | bytes 331784 | tf_op jit(solution)/shard_map/while/body/eval_jaxpr/ppermute | solution.py:12
  360.4 44.8 %all-reduce.4.cloned.1.call-done = f32[192,192]{1,0:T(8,128)} async-done(((f32[192,192]{1,0:T(8,128)}), f32[192,192]{1,0:T(8,128)}) %all-reduce.4.cloned.1.call-update) | async-done | bytes 147472 | tf_op jit(solution)/shard_map/while/body/eval_jaxpr/psum | solution.py:57
  407.8 9.9 %collective-permute-start.1 = (f32[192,288]{1,0:T(8,128)S(1)}, f32[192,288]{1,0:T(8,128)S(1)}, u32[]{:S(2)}, u32[]{:S(2)}) collective-permute-start(f32[192,288]{1,0:T(8,128)S(1)} %convolution_add_fusion.4), channel_id=1, source_target_pairs={{4,0},{8,4},{12,8},{16,12},{20,16},{24,20},{28,24},{32,28},{36,32}... | collective-permute-start | bytes 663560 | tf_op jit(solution)/shard_map/while/body/eval_jaxpr/ppermute | solution.py:12
  419.4 7.5 collective-permute-done.1
  427.9 11.4 %collective-permute-start = (bf16[192,288]{1,0:T(8,128)(2,1)S(1)}, bf16[192,288]{1,0:T(8,128)(2,1)S(1)}, u32[]{:S(2)}, u32[]{:S(2)}) collective-permute-start(bf16[192,288]{1,0:T(8,128)(2,1)S(1)} %copy.19), channel_id=1, source_target_pairs={{4,0},{8,4},{12,8},{16,12},{20,16},{24,20},{28,24},{32,28},{36,32}... | collective-permute-start | bytes 331784 | tf_op jit(solution)/shard_map/while/body/eval_jaxpr/ppermute | solution.py:12
  439.3 44.9 %all-reduce.4.cloned.1.call-done = f32[192,192]{1,0:T(8,128)} async-done(((f32[192,192]{1,0:T(8,128)}), f32[192,192]{1,0:T(8,128)}) %all-reduce.4.cloned.1.call-update) | async-done | bytes 147472 | tf_op jit(solution)/shard_map/while/body/eval_jaxpr/psum | solution.py:57
  486.8 9.9 %collective-permute-start.1 = (f32[192,288]{1,0:T(8,128)S(1)}, f32[192,288]{1,0:T(8,128)S(1)}, u32[]{:S(2)}, u32[]{:S(2)}) collective-permute-start(f32[192,288]{1,0:T(8,128)S(1)} %convolution_add_fusion.4), channel_id=1, source_target_pairs={{4,0},{8,4},{12,8},{16,12},{20,16},{24,20},{28,24},{32,28},{36,32}... | collective-permute-start | bytes 663560 | tf_op jit(solution)/shard_map/while/body/eval_jaxpr/ppermute | solution.py:12
  506.8 11.4 %collective-permute-start = (bf16[192,288]{1,0:T(8,128)(2,1)S(1)}, bf16[192,288]{1,0:T(8,128)(2,1)S(1)}, u32[]{:S(2)}, u32[]{:S(2)}) collective-permute-start(bf16[192,288]{1,0:T(8,128)(2,1)S(1)} %copy.19), channel_id=1, source_target_pairs={{4,0},{8,4},{12,8},{16,12},{20,16},{24,20},{28,24},{32,28},{36,32}... | collective-permute-start | bytes 331784 | tf_op jit(solution)/shard_map/while/body/eval_jaxpr/ppermute | solution.py:12
  518.3 45.2 %all-reduce.4.cloned.1.call-done = f32[192,192]{1,0:T(8,128)} async-done(((f32[192,192]{1,0:T(8,128)}), f32[192,192]{1,0:T(8,128)}) %all-reduce.4.cloned.1.call-update) | async-done | bytes 147472 | tf_op jit(solution)/shard_map/while/body/eval_jaxpr/psum | solution.py:57
  566.1 9.9 %collective-permute-start.1 = (f32[192,288]{1,0:T(8,128)S(1)}, f32[192,288]{1,0:T(8,128)S(1)}, u32[]{:S(2)}, u32[]{:S(2)}) collective-permute-start(f32[192,288]{1,0:T(8,128)S(1)} %convolution_add_fusion.4), channel_id=1, source_target_pairs={{4,0},{8,4},{12,8},{16,12},{20,16},{24,20},{28,24},{32,28},{36,32}... | collective-permute-start | bytes 663560 | tf_op jit(solution)/shard_map/while/body/eval_jaxpr/ppermute | solution.py:12
  586.1 11.4 %collective-permute-start = (bf16[192,288]{1,0:T(8,128)(2,1)S(1)}, bf16[192,288]{1,0:T(8,128)(2,1)S(1)}, u32[]{:S(2)}, u32[]{:S(2)}) collective-permute-start(bf16[192,288]{1,0:T(8,128)(2,1)S(1)} %copy.19), channel_id=1, source_target_pairs={{4,0},{8,4},{12,8},{16,12},{20,16},{24,20},{28,24},{32,28},{36,32}... | collective-permute-start | bytes 331784 | tf_op jit(solution)/shard_map/while/body/eval_jaxpr/ppermute | solution.py:12
  597.5 45.2 %all-reduce.4.cloned.1.call-done = f32[192,192]{1,0:T(8,128)} async-done(((f32[192,192]{1,0:T(8,128)}), f32[192,192]{1,0:T(8,128)}) %all-reduce.4.cloned.1.call-update) | async-done | bytes 147472 | tf_op jit(solution)/shard_map/while/body/eval_jaxpr/psum | solution.py:57
  645.3 9.9 %collective-permute-start.1 = (f32[192,288]{1,0:T(8,128)S(1)}, f32[192,288]{1,0:T(8,128)S(1)}, u32[]{:S(2)}, u32[]{:S(2)}) collective-permute-start(f32[192,288]{1,0:T(8,128)S(1)} %convolution_add_fusion.4), channel_id=1, source_target_pairs={{4,0},{8,4},{12,8},{16,12},{20,16},{24,20},{28,24},{32,28},{36,32}... | collective-permute-start | bytes 663560 | tf_op jit(solution)/shard_map/while/body/eval_jaxpr/ppermute | solution.py:12
  669.5 13.1 %collective-permute-done.2 = f32[192,288]{1,0:T(8,128)S(1)} collective-permute-done((f32[192,288]{1,0:T(8,128)S(1)}, f32[192,288]{1,0:T(8,128)S(1)}, u32[]{:S(2)}, u32[]{:S(2)}) %collective-permute-start.2) | collective-permute-done | bytes 221216 | tf_op jit(solution)/shard_map/ppermute | solution.py:12
  682.8 7.8 %all-reduce = (f32[192]{0:T(256)S(1)}, f32[192]{0:T(256)S(1)}) all-reduce(f32[192]{0:T(256)S(1)} %multiply_reduce_fusion.1, f32[192]{0:T(256)S(1)} %multiply_reduce_fusion), channel_id=1, replica_groups=mesh['dp'=256,'tensor'=4] {'tensor'}, use_global_device_ids=true, to_apply=%region_8.9 | all-reduce | flops 384 | bytes 3072 | tf_op jit(solution)/shard_map/psum | solution.py:81
  695.5 23.9 %reduce-scatter.7.cloned.1.call-done = f32[288,192]{1,0:T(8,128)} async-done(((f32[1152,192]{1,0:T(8,128)}), f32[288,192]{1,0:T(8,128)}) %reduce-scatter.7.cloned.1.call-update) | async-done | bytes 221200
  721.2 31.7 %reduce-scatter.9.cloned.1.call-done = f32[288,192]{1,0:T(8,128)} async-done(((f32[1152,192]{1,0:T(8,128)}), f32[288,192]{1,0:T(8,128)}) %reduce-scatter.9.cloned.1.call-update) | async-done | bytes 221200
  (105 shorter events, 103.0 us)
Async XLA Ops:
  10.7 20.0 %copy-start.4 = (s32[192]{0:T(256)S(1)}, s32[192]{0:T(256)}, u32[]{:S(2)}) copy-start(s32[192]{0:T(256)} %param.15) | copy-start | bytes 2308
  30.7 58.1 %all-reduce.4.cloned.1.call-start = ((), (), s32[]{:S(2)}) async-start(), calls=%async_computation.4 | async-start | bytes 393216 | tf_op jit(solution)/shard_map/while/body/eval_jaxpr/psum | solution.py:57
  31.7 71.3 %collective-permute-start = (bf16[192,288]{1,0:T(8,128)(2,1)S(1)}, bf16[192,288]{1,0:T(8,128)(2,1)S(1)}, u32[]{:S(2)}, u32[]{:S(2)}) collective-permute-start(bf16[192,288]{1,0:T(8,128)(2,1)S(1)} %copy.19), channel_id=1, source_target_pairs={{4,0},{8,4},{12,8},{16,12},{20,16},{24,20},{28,24},{32,28},{36,32}... | collective-permute-start | bytes 331784 | tf_op jit(solution)/shard_map/while/body/eval_jaxpr/ppermute | solution.py:12
  88.8 12.6 %copy-start.3 = (f32[192,192]{1,0:T(8,128)S(1)}, f32[192,192]{1,0:T(8,128)}, u32[]{:S(2)}) copy-start(f32[192,192]{1,0:T(8,128)} %all-reduce.4.cloned.1.call-done) | copy-start | bytes 442372 | tf_op jit(solution)/shard_map/while
  91.4 19.1 %collective-permute-start.1 = (f32[192,288]{1,0:T(8,128)S(1)}, f32[192,288]{1,0:T(8,128)S(1)}, u32[]{:S(2)}, u32[]{:S(2)}) collective-permute-start(f32[192,288]{1,0:T(8,128)S(1)} %convolution_add_fusion.4), channel_id=1, source_target_pairs={{4,0},{8,4},{12,8},{16,12},{20,16},{24,20},{28,24},{32,28},{36,32}... | collective-permute-start | bytes 663560 | tf_op jit(solution)/shard_map/while/body/eval_jaxpr/ppermute | solution.py:12
  110.5 57.6 %all-reduce.4.cloned.1.call-start = ((), (), s32[]{:S(2)}) async-start(), calls=%async_computation.4 | async-start | bytes 393216 | tf_op jit(solution)/shard_map/while/body/eval_jaxpr/psum | solution.py:57
  111.4 70.8 %collective-permute-start = (bf16[192,288]{1,0:T(8,128)(2,1)S(1)}, bf16[192,288]{1,0:T(8,128)(2,1)S(1)}, u32[]{:S(2)}, u32[]{:S(2)}) collective-permute-start(bf16[192,288]{1,0:T(8,128)(2,1)S(1)} %copy.19), channel_id=1, source_target_pairs={{4,0},{8,4},{12,8},{16,12},{20,16},{24,20},{28,24},{32,28},{36,32}... | collective-permute-start | bytes 331784 | tf_op jit(solution)/shard_map/while/body/eval_jaxpr/ppermute | solution.py:12
  168.0 12.6 %copy-start.3 = (f32[192,192]{1,0:T(8,128)S(1)}, f32[192,192]{1,0:T(8,128)}, u32[]{:S(2)}) copy-start(f32[192,192]{1,0:T(8,128)} %all-reduce.4.cloned.1.call-done) | copy-start | bytes 442372 | tf_op jit(solution)/shard_map/while
  170.7 19.1 %collective-permute-start.1 = (f32[192,288]{1,0:T(8,128)S(1)}, f32[192,288]{1,0:T(8,128)S(1)}, u32[]{:S(2)}, u32[]{:S(2)}) collective-permute-start(f32[192,288]{1,0:T(8,128)S(1)} %convolution_add_fusion.4), channel_id=1, source_target_pairs={{4,0},{8,4},{12,8},{16,12},{20,16},{24,20},{28,24},{32,28},{36,32}... | collective-permute-start | bytes 663560 | tf_op jit(solution)/shard_map/while/body/eval_jaxpr/ppermute | solution.py:12
  189.7 57.6 %all-reduce.4.cloned.1.call-start = ((), (), s32[]{:S(2)}) async-start(), calls=%async_computation.4 | async-start | bytes 393216 | tf_op jit(solution)/shard_map/while/body/eval_jaxpr/psum | solution.py:57
  190.7 70.8 %collective-permute-start = (bf16[192,288]{1,0:T(8,128)(2,1)S(1)}, bf16[192,288]{1,0:T(8,128)(2,1)S(1)}, u32[]{:S(2)}, u32[]{:S(2)}) collective-permute-start(bf16[192,288]{1,0:T(8,128)(2,1)S(1)} %copy.19), channel_id=1, source_target_pairs={{4,0},{8,4},{12,8},{16,12},{20,16},{24,20},{28,24},{32,28},{36,32}... | collective-permute-start | bytes 331784 | tf_op jit(solution)/shard_map/while/body/eval_jaxpr/ppermute | solution.py:12
  249.9 19.1 %collective-permute-start.1 = (f32[192,288]{1,0:T(8,128)S(1)}, f32[192,288]{1,0:T(8,128)S(1)}, u32[]{:S(2)}, u32[]{:S(2)}) collective-permute-start(f32[192,288]{1,0:T(8,128)S(1)} %convolution_add_fusion.4), channel_id=1, source_target_pairs={{4,0},{8,4},{12,8},{16,12},{20,16},{24,20},{28,24},{32,28},{36,32}... | collective-permute-start | bytes 663560 | tf_op jit(solution)/shard_map/while/body/eval_jaxpr/ppermute | solution.py:12
  269.0 57.2 %all-reduce.4.cloned.1.call-start = ((), (), s32[]{:S(2)}) async-start(), calls=%async_computation.4 | async-start | bytes 393216 | tf_op jit(solution)/shard_map/while/body/eval_jaxpr/psum | solution.py:57
  270.0 70.5 %collective-permute-start = (bf16[192,288]{1,0:T(8,128)(2,1)S(1)}, bf16[192,288]{1,0:T(8,128)(2,1)S(1)}, u32[]{:S(2)}, u32[]{:S(2)}) collective-permute-start(bf16[192,288]{1,0:T(8,128)(2,1)S(1)} %copy.19), channel_id=1, source_target_pairs={{4,0},{8,4},{12,8},{16,12},{20,16},{24,20},{28,24},{32,28},{36,32}... | collective-permute-start | bytes 331784 | tf_op jit(solution)/shard_map/while/body/eval_jaxpr/ppermute | solution.py:12
  326.2 12.6 %copy-start.3 = (f32[192,192]{1,0:T(8,128)S(1)}, f32[192,192]{1,0:T(8,128)}, u32[]{:S(2)}) copy-start(f32[192,192]{1,0:T(8,128)} %all-reduce.4.cloned.1.call-done) | copy-start | bytes 442372 | tf_op jit(solution)/shard_map/while
  328.9 19.1 %collective-permute-start.1 = (f32[192,288]{1,0:T(8,128)S(1)}, f32[192,288]{1,0:T(8,128)S(1)}, u32[]{:S(2)}, u32[]{:S(2)}) collective-permute-start(f32[192,288]{1,0:T(8,128)S(1)} %convolution_add_fusion.4), channel_id=1, source_target_pairs={{4,0},{8,4},{12,8},{16,12},{20,16},{24,20},{28,24},{32,28},{36,32}... | collective-permute-start | bytes 663560 | tf_op jit(solution)/shard_map/while/body/eval_jaxpr/ppermute | solution.py:12
  347.9 57.3 %all-reduce.4.cloned.1.call-start = ((), (), s32[]{:S(2)}) async-start(), calls=%async_computation.4 | async-start | bytes 393216 | tf_op jit(solution)/shard_map/while/body/eval_jaxpr/psum | solution.py:57
  348.9 70.5 %collective-permute-start = (bf16[192,288]{1,0:T(8,128)(2,1)S(1)}, bf16[192,288]{1,0:T(8,128)(2,1)S(1)}, u32[]{:S(2)}, u32[]{:S(2)}) collective-permute-start(bf16[192,288]{1,0:T(8,128)(2,1)S(1)} %copy.19), channel_id=1, source_target_pairs={{4,0},{8,4},{12,8},{16,12},{20,16},{24,20},{28,24},{32,28},{36,32}... | collective-permute-start | bytes 331784 | tf_op jit(solution)/shard_map/while/body/eval_jaxpr/ppermute | solution.py:12
  405.2 12.6 %copy-start.3 = (f32[192,192]{1,0:T(8,128)S(1)}, f32[192,192]{1,0:T(8,128)}, u32[]{:S(2)}) copy-start(f32[192,192]{1,0:T(8,128)} %all-reduce.4.cloned.1.call-done) | copy-start | bytes 442372 | tf_op jit(solution)/shard_map/while
  407.8 19.1 %collective-permute-start.1 = (f32[192,288]{1,0:T(8,128)S(1)}, f32[192,288]{1,0:T(8,128)S(1)}, u32[]{:S(2)}, u32[]{:S(2)}) collective-permute-start(f32[192,288]{1,0:T(8,128)S(1)} %convolution_add_fusion.4), channel_id=1, source_target_pairs={{4,0},{8,4},{12,8},{16,12},{20,16},{24,20},{28,24},{32,28},{36,32}... | collective-permute-start | bytes 663560 | tf_op jit(solution)/shard_map/while/body/eval_jaxpr/ppermute | solution.py:12
  426.9 57.3 %all-reduce.4.cloned.1.call-start = ((), (), s32[]{:S(2)}) async-start(), calls=%async_computation.4 | async-start | bytes 393216 | tf_op jit(solution)/shard_map/while/body/eval_jaxpr/psum | solution.py:57
  427.9 70.5 %collective-permute-start = (bf16[192,288]{1,0:T(8,128)(2,1)S(1)}, bf16[192,288]{1,0:T(8,128)(2,1)S(1)}, u32[]{:S(2)}, u32[]{:S(2)}) collective-permute-start(bf16[192,288]{1,0:T(8,128)(2,1)S(1)} %copy.19), channel_id=1, source_target_pairs={{4,0},{8,4},{12,8},{16,12},{20,16},{24,20},{28,24},{32,28},{36,32}... | collective-permute-start | bytes 331784 | tf_op jit(solution)/shard_map/while/body/eval_jaxpr/ppermute | solution.py:12
  486.8 19.1 %collective-permute-start.1 = (f32[192,288]{1,0:T(8,128)S(1)}, f32[192,288]{1,0:T(8,128)S(1)}, u32[]{:S(2)}, u32[]{:S(2)}) collective-permute-start(f32[192,288]{1,0:T(8,128)S(1)} %convolution_add_fusion.4), channel_id=1, source_target_pairs={{4,0},{8,4},{12,8},{16,12},{20,16},{24,20},{28,24},{32,28},{36,32}... | collective-permute-start | bytes 663560 | tf_op jit(solution)/shard_map/while/body/eval_jaxpr/ppermute | solution.py:12
  505.9 57.6 %all-reduce.4.cloned.1.call-start = ((), (), s32[]{:S(2)}) async-start(), calls=%async_computation.4 | async-start | bytes 393216 | tf_op jit(solution)/shard_map/while/body/eval_jaxpr/psum | solution.py:57
  506.8 70.8 %collective-permute-start = (bf16[192,288]{1,0:T(8,128)(2,1)S(1)}, bf16[192,288]{1,0:T(8,128)(2,1)S(1)}, u32[]{:S(2)}, u32[]{:S(2)}) collective-permute-start(bf16[192,288]{1,0:T(8,128)(2,1)S(1)} %copy.19), channel_id=1, source_target_pairs={{4,0},{8,4},{12,8},{16,12},{20,16},{24,20},{28,24},{32,28},{36,32}... | collective-permute-start | bytes 331784 | tf_op jit(solution)/shard_map/while/body/eval_jaxpr/ppermute | solution.py:12
  566.1 19.1 %collective-permute-start.1 = (f32[192,288]{1,0:T(8,128)S(1)}, f32[192,288]{1,0:T(8,128)S(1)}, u32[]{:S(2)}, u32[]{:S(2)}) collective-permute-start(f32[192,288]{1,0:T(8,128)S(1)} %convolution_add_fusion.4), channel_id=1, source_target_pairs={{4,0},{8,4},{12,8},{16,12},{20,16},{24,20},{28,24},{32,28},{36,32}... | collective-permute-start | bytes 663560 | tf_op jit(solution)/shard_map/while/body/eval_jaxpr/ppermute | solution.py:12
  585.1 57.6 %all-reduce.4.cloned.1.call-start = ((), (), s32[]{:S(2)}) async-start(), calls=%async_computation.4 | async-start | bytes 393216 | tf_op jit(solution)/shard_map/while/body/eval_jaxpr/psum | solution.py:57
  586.1 70.8 %collective-permute-start = (bf16[192,288]{1,0:T(8,128)(2,1)S(1)}, bf16[192,288]{1,0:T(8,128)(2,1)S(1)}, u32[]{:S(2)}, u32[]{:S(2)}) collective-permute-start(bf16[192,288]{1,0:T(8,128)(2,1)S(1)} %copy.19), channel_id=1, source_target_pairs={{4,0},{8,4},{12,8},{16,12},{20,16},{24,20},{28,24},{32,28},{36,32}... | collective-permute-start | bytes 331784 | tf_op jit(solution)/shard_map/while/body/eval_jaxpr/ppermute | solution.py:12
  645.3 19.1 %collective-permute-start.1 = (f32[192,288]{1,0:T(8,128)S(1)}, f32[192,288]{1,0:T(8,128)S(1)}, u32[]{:S(2)}, u32[]{:S(2)}) collective-permute-start(f32[192,288]{1,0:T(8,128)S(1)} %convolution_add_fusion.4), channel_id=1, source_target_pairs={{4,0},{8,4},{12,8},{16,12},{20,16},{24,20},{28,24},{32,28},{36,32}... | collective-permute-start | bytes 663560 | tf_op jit(solution)/shard_map/while/body/eval_jaxpr/ppermute | solution.py:12
  664.4 55.0 %reduce-scatter.7.cloned.1.call-start = ((), (), s32[]{:S(2)}) async-start(), calls=%async_computation.2 | async-start | bytes 1474560
  664.4 18.2 %collective-permute-start.2 = (f32[192,288]{1,0:T(8,128)S(1)}, f32[192,288]{1,0:T(8,128)S(1)}, u32[]{:S(2)}, u32[]{:S(2)}) collective-permute-start(f32[192,288]{1,0:T(8,128)S(1)} %get-tuple-element.143), channel_id=1, source_target_pairs={{992,0},{996,4},{1000,8},{1004,12},{1008,16},{1012,20},{1016,24},{... | collective-permute-start | bytes 663560 | tf_op jit(solution)/shard_map/ppermute | solution.py:12
  693.0 59.9 %reduce-scatter.9.cloned.1.call-start = ((), (), s32[]{:S(2)}) async-start(), calls=%async_computation.3 | async-start | bytes 1474560
  (7 other events, 56.6 us)
Sparse Core Ops, SparseCore 0:
  35.6 53.1 all-reduce.3
  115.4 52.6 all-reduce.3
  194.6 52.6 all-reduce.3
  273.6 52.6 all-reduce.3
  352.5 52.6 all-reduce.3
  431.5 52.6 all-reduce.3
  510.8 52.6 all-reduce.3
  590.0 52.6 all-reduce.3
Sparse Core Ops, SparseCore 1:
  693.0 26.2 reduce-scatter.6
  722.7 30.2 reduce-scatter.8
where the time goes:
time: 763 us; the launch traced here: 762 us
  waiting for transfers between devices  490 us (64%)
  starting transfers between devices  175 us (23%)
  matrix products  48.1 us (6%)
  blocking collectives  27 us (4%)
  between operations  16.2 us (2%)
    psum x8, waiting for transfers between devices, visit(): logits = similarity_multiplier * lax.psum(partial_value, 'tensor') + offset  361 us
    ppermute x17, starting transfers between devices, passed_along(): return lax.ppermute(block, axis, route)  175 us
    ppermute x17, waiting for transfers between devices, passed_along(): return lax.ppermute(block, axis, route)  73 us
    unnamed x4, waiting for transfers between devices  55.6 us
    dot_general x8, matrix products, visit(): lax.dot_general(weight, img_low, contract_rows, preferred_element_type=jn...  20.9 us
    psum x1, blocking collectives, shards(): lax.psum((jnp.sum(img_emb * img_emb, axis=1), jnp.sum(txt_emb * txt_emb,...  19.2 us
  transfers between devices with their start and end apart: 27, of which 19 were waited for; matrix products, arithmetic and copies ran while one was open for 5% of the time, Pallas kernels for 0%

commit v1 on v0

v1 whole, which is shorter than its diff:
```python
import jax
import jax.numpy as jnp
from jax import lax
from jax.sharding import PartitionSpec as P

AXES = ("dp", "tensor")
ROUND = 4


def exchange(block, groups, source):
    route = []
    for n in range(groups):
        for t in range(4):
            m, u = source(n, t)
            route.append(((m % groups) * 4 + u, n * 4 + t))
    return lax.ppermute(block, AXES, route)


def neighbour(n, t):
    return [(n + 3, 2), (n - 1, 3), (n + 1, 0), (n - 3, 1)][t]


def relay(n, t):
    return (n - 1, t) if t < 2 else (n + 1, t)


def beyond(n, t):
    return (n + ROUND, t) if t % 2 == 0 else (n - ROUND, t)


def chip_swap(n, t):
    return (n, t ^ 2)


def core_swap(n, t):
    return (n, t ^ 1)


def shards(
    picture_averaged_vectors,
    picture_mapping_matrix,
    caption_averaged_vectors,
    caption_mapping_matrix,
    sharpness_factor,
    offset_term,
    paired_caption_index,
):
    f32, bf16 = jnp.float32, jnp.bfloat16
    groups = lax.axis_size("dp")
    rows = picture_averaged_vectors.shape[0]
    half = rows // 2
    span = picture_mapping_matrix.shape[1]
    scale = sharpness_factor[0]
    offset = offset_term[0]
    t = lax.axis_index("tensor")
    core0 = t % 2 == 0
    chip0 = t < 2

    img_emb = jnp.dot(
        picture_averaged_vectors, picture_mapping_matrix, preferred_element_type=f32
    )
    txt_emb = jnp.dot(
        caption_averaged_vectors, caption_mapping_matrix, preferred_element_type=f32
    )
    squares = jnp.concatenate(
        [jnp.sum(img_emb * img_emb, axis=1), jnp.sum(txt_emb * txt_emb, axis=1)]
    )
    inv = lax.rsqrt(lax.psum(squares, "tensor") + 1e-06)
    inv_img, inv_txt = inv[:rows], inv[rows:]
    img_unit = img_emb * inv_img[:, None]
    txt_unit = txt_emb * inv_txt[:, None]
    img_low = img_unit.astype(bf16)
    txt_low = txt_unit.astype(bf16)
    img_rest = (img_unit - img_low.astype(f32)).astype(bf16)
    txt_rest = (txt_unit - txt_low.astype(f32)).astype(bf16)

    def by_core(a, b):
        return jnp.where(core0, a, b), jnp.where(core0, b, a)

    def by_chip(mine, other):
        return jnp.where(chip0, mine, other), jnp.where(chip0, other, mine)

    fixed_part, moving_part = by_core(img_low, txt_low)
    own = jnp.concatenate([fixed_part, moving_part])
    other = exchange(own, groups, chip_swap)
    first, second = by_chip(own, other)
    pair = jnp.concatenate([first, second], axis=1)
    peer = exchange(pair, groups, core_swap)

    def whole(mine, theirs):
        return jnp.concatenate(
            [mine[:, :span], theirs[:, :span], mine[:, span:], theirs[:, span:]], axis=1
        )

    fixed = whole(pair[:rows], peer[rows:])
    moving = whole(pair[rows:], peer[:rows])
    own_half = jnp.where(chip0, moving[:half], moving[half:])

    near = exchange(moving, groups, neighbour)
    far_own = exchange(own_half, groups, beyond)

    rest_mine, rest_theirs = by_core(img_rest, txt_rest)
    rest_peer = exchange(rest_theirs, groups, core_swap)
    rest_chip = jnp.concatenate([rest_mine, rest_peer], axis=1)
    rest_other = exchange(rest_chip, groups, chip_swap)
    rest = jnp.concatenate(by_chip(rest_chip, rest_other), axis=1)
    matrix_mine, matrix_theirs = by_core(picture_mapping_matrix, caption_mapping_matrix)
    matrix_peer = exchange(matrix_theirs, groups, core_swap)

    near_half = jnp.where(chip0, near[:half], near[half:])
    opposite = exchange(near_half, groups, relay)
    far_near = exchange(near, groups, beyond)
    far_opposite = exchange(opposite, groups, beyond)

    def products(block):
        return scale * lax.dot_general(
            fixed, block, (((1,), (1,)), ((), ())), preferred_element_type=f32
        ) + offset

    def pull(weight, block):
        return jnp.dot(weight.astype(bf16), block, preferred_element_type=f32)

    def unmatched(block):
        return pull(16.0 * jax.nn.sigmoid(products(block)), block)

    first_row = lax.axis_index("dp") * rows
    ids = first_row + jnp.arange(rows, dtype=jnp.int32)
    half_ids = jnp.where(chip0, ids[:half], ids[half:])
    half_index = jnp.where(chip0, paired_caption_index[:half], paired_caption_index[half:])
    matched = jnp.where(
        core0,
        paired_caption_index[:, None] == half_ids[None, :],
        ids[:, None] == half_index[None, :],
    )
    sign = jnp.where(matched, 1.0, -1.0).astype(f32)
    total = pull(-16.0 * sign * jax.nn.sigmoid(-sign * products(own_half)), own_half)
    total = total + unmatched(far_own)
    total = total + unmatched(near)
    total = total + unmatched(opposite)
    total = total + unmatched(far_near)
    total = total + unmatched(far_opposite)

    unit = fixed.astype(f32) + rest.astype(f32)
    across = total - unit * jnp.sum(unit * total, axis=1, keepdims=True)
    keep, give = by_chip(across[:, : 2 * span], across[:, 2 * span :])
    got = exchange(give.astype(bf16), groups, chip_swap)
    inv_fixed = jnp.where(core0, inv_img, inv_txt)
    demb = (scale * inv_fixed)[:, None] * (keep + got.astype(f32))
    demb_high = demb.astype(bf16)
    demb_rest = (demb - demb_high.astype(f32)).astype(bf16)
    matrix = jnp.concatenate([matrix_mine, matrix_peer], axis=1)
    by_columns = (((1,), (1,)), ((), ()))
    part = lax.dot_general(
        demb_high, matrix, by_columns, preferred_element_type=f32
    ) + lax.dot_general(demb_rest, matrix, by_columns, preferred_element_type=f32)
    keep, give = by_chip(part[:, : 2 * span], part[:, 2 * span :])
    got = exchange(give.astype(bf16), groups, chip_swap)
    grad = keep + got.astype(f32)
    mine, theirs = by_core(grad[:, :span], grad[:, span:])
    peer_grad = exchange(theirs, groups, core_swap)
    return by_core(mine, peer_grad)


def solution(mesh):
    in_specs = (
        P("dp", None),
        P(None, "tensor"),
        P("dp", None),
        P(None, "tensor"),
        P(),
        P(),
        P("dp"),
    )
    out_specs = (P("dp", "tensor"), P("dp", "tensor"))
    return jax.shard_map(shards, mesh=mesh, in_specs=in_specs, out_specs=out_specs, check_vma=False)
```

time: 763 us -> 122 us (0.16)
  waiting for transfers between devices: 490 us -> 43 us
  starting transfers between devices: 175 us -> 31.3 us
  matrix products: 48.1 us -> 16.1 us
  between operations: 16.2 us -> 2.44 us
  blocking collectives: 27 us -> 19.2 us
  other arithmetic: 0.58 us -> 8.37 us
    psum x8 -> x0, waiting for transfers between devices: 361 us -> none  [visit(): logits = similarity_multiplier * lax.psum(partial_value, 'tensor') + offset]
    ppermute x17 -> x13, starting transfers between devices: 175 us -> 31.3 us  [exchange(): return lax.ppermute(block, AXES, route)]
    unnamed x4 -> x0, waiting for transfers between devices: 55.6 us -> none
    ppermute x17 -> x13, waiting for transfers between devices: 73 us -> 43 us  [exchange(): return lax.ppermute(block, AXES, route)]
    dot_general x24 -> x8, matrix products: 41.2 us -> 13.9 us  [the longest x6 10.5 us: pull(): return jnp.dot(weight.astype(bf16), block, preferred_element_type=f32)]
    psum x2 -> x1, blocking collectives: 27 us -> 19.2 us  [shards(): inv = lax.rsqrt(lax.psum(squares, 'tensor') + 1e-06)]
  transfers between devices with their start and end apart: 27 -> 13, of which waited for: 19 -> 8; matrix products, arithmetic and copies ran while one was open for 5% -> 15% of each run, Pallas kernels for 0% -> 0%
where the time goes in v1:
time: 122 us; the launch traced here: 121 us
  waiting for transfers between devices  43 us (35%)
  starting transfers between devices  31.3 us (26%)
  blocking collectives  19.2 us (16%)
  matrix products  16.1 us (13%)
  other arithmetic  8.37 us (7%)
  between operations  2.44 us (2%)
    ppermute x13, waiting for transfers between devices, exchange(): return lax.ppermute(block, AXES, route)  43 us
    ppermute x13, starting transfers between devices, exchange(): return lax.ppermute(block, AXES, route)  31.3 us
    psum x1, blocking collectives, shards(): inv = lax.rsqrt(lax.psum(squares, 'tensor') + 1e-06)  19.2 us
    dot_general x6, matrix products, pull(): return jnp.dot(weight.astype(bf16), block, preferred_element_type=f32)  10.5 us
    select_n x4, other arithmetic, by_core(): return (jnp.where(core0, a, b), jnp.where(core0, b, a))  2.53 us
  transfers between devices with their start and end apart: 13, of which 8 were waited for; matrix products, arithmetic and copies ran while one was open for 15% of the time, Pallas kernels for 0%

profile of v1, /device:TPU:1, one launch (start us, length us, event | category | flops | bytes accessed | tf_op | source)
XLA Modules:
  0.0 121.4 jit_solution(2898868049901186987)
XLA Ops:
  1.6 1.6 %multiply_reduce_fusion.1 = (f32[192]{0:T(256)S(1)}, f32[192,288]{1,0:T(8,128)S(1)}) fusion(bf16[192,1152]{1,0:T(8,128)(2,1)S(1)} %copy-done, bf16[1152,288]{0,1:T(8,128)(2,1)} %param.10), kind=kOutput, calls=%fused_computation.75 | convolution fusion | flops 127512384 | bytes 1327872 | tf_op jit(solution)/shard_map/dot_general | solution.py:62
  3.9 19.2 %psum.7 = f32[384]{0:T(512)S(1)} all-reduce(f32[384]{0:T(512)S(1)} %pad_maximum_fusion.7), channel_id=1, replica_groups=mesh['dp'=256,'tensor'=4] {'tensor'}, use_global_device_ids=true, to_apply=%region_2.3 | all-reduce | flops 384 | bytes 3072 | tf_op jit(solution)/shard_map/psum | solution.py:68
  23.4 2.0 %collective-permute-start = (bf16[384,288]{1,0:T(8,128)(2,1)S(1)}, bf16[384,288]{1,0:T(8,128)(2,1)S(1)}, u32[]{:S(2)}, u32[]{:S(2)}) collective-permute-start(bf16[384,288]{1,0:T(8,128)(2,1)S(1)} %pad_maximum_fusion.5), channel_id=1, source_target_pairs={{2,0},{3,1},{0,2},{1,3},{6,4},{7,5},{4,6},{5,7},{10,8},{11,9},{8,1... | collective-permute-start | bytes 663560 | tf_op jit(solution)/shard_map/ppermute | solution.py:16
  25.4 2.6 %collective-permute-start.7 = (bf16[192,288]{1,0:T(8,128)(2,1)S(1)}, bf16[192,288]{1,0:T(8,128)(2,1)S(1)}, u32[]{:S(2)}, u32[]{:S(2)}) collective-permute-start(bf16[192,288]{1,0:T(8,128)(2,1)S(1)} %get-tuple-element.7), channel_id=1, source_target_pairs={{1,0},{0,1},{3,2},{2,3},{5,4},{4,5},{7,6},{6,7},{9,8},{8,9},{11,10... | collective-permute-start | bytes 331784 | tf_op jit(solution)/shard_map/ppermute | solution.py:16
  28.0 1.2 %broadcast_select_fusion.1 = (bf16[1152,288]{0,1:T(8,128)(2,1)}, bf16[1152,288]{0,1:T(8,128)(2,1)}) fusion(bf16[1152,288]{0,1:T(8,128)(2,1)S(1)} %copy-done.2, bf16[1152,288]{0,1:T(8,128)(2,1)S(1)} %copy-done.3, pred[]{:T(512)S(6)} %eq.16), kind=kLoop, calls=%fused_computation.64 | loop fusion | flops 663552 | bytes 2654209 | tf_op jit(solution)/shard_map/jit(_where)/select_n | solution.py:78
  29.2 1.9 %collective-permute-start.10 = (bf16[1152,288]{0,1:T(8,128)(2,1)}, bf16[1152,288]{0,1:T(8,128)(2,1)}, u32[]{:S(2)}, u32[]{:S(2)}) collective-permute-start(bf16[1152,288]{0,1:T(8,128)(2,1)} %get-tuple-element.3), channel_id=1, source_target_pairs={{1,0},{0,1},{3,2},{2,3},{5,4},{4,5},{7,6},{6,7},{9,8},{8,9},{11,10... | collective-permute-start | bytes 1990664 | tf_op jit(solution)/shard_map/ppermute | solution.py:16
  31.2 1.9 %collective-permute-done = bf16[384,288]{1,0:T(8,128)(2,1)S(1)} collective-permute-done((bf16[384,288]{1,0:T(8,128)(2,1)S(1)}, bf16[384,288]{1,0:T(8,128)(2,1)S(1)}, u32[]{:S(2)}, u32[]{:S(2)}) %collective-permute-start) | collective-permute-done | bytes 221216 | tf_op jit(solution)/shard_map/ppermute | solution.py:16
  33.4 3.5 %collective-permute-start.1 = (bf16[384,576]{1,0:T(8,128)(2,1)S(1)}, bf16[384,576]{1,0:T(8,128)(2,1)S(1)}, u32[]{:S(2)}, u32[]{:S(2)}) collective-permute-start(bf16[384,576]{1,0:T(8,128)(2,1)S(1)} %pad_maximum_fusion.3), channel_id=1, source_target_pairs={{1,0},{0,1},{3,2},{2,3},{5,4},{4,5},{7,6},{6,7},{9,8},{8,9},{11,10... | collective-permute-start | bytes 1327112 | tf_op jit(solution)/shard_map/ppermute | solution.py:16
  38.5 2.0 %collective-permute-start.8 = (bf16[192,576]{1,0:T(8,128)(2,1)}, bf16[192,576]{1,0:T(8,128)(2,1)}, u32[]{:S(2)}, u32[]{:S(2)}) collective-permute-start(bf16[192,576]{1,0:T(8,128)(2,1)} %pad_maximum_fusion.6), channel_id=1, source_target_pairs={{2,0},{3,1},{0,2},{1,3},{6,4},{7,5},{4,6},{5,7},{10,8},{11,9},{8,1... | collective-permute-start | bytes 663560 | tf_op jit(solution)/shard_map/ppermute | solution.py:16
  41.1 1.9 %collective-permute-start.3 = (bf16[192,1152]{1,0:T(8,128)(2,1)S(1)}, bf16[192,1152]{1,0:T(8,128)(2,1)S(1)}, u32[]{:S(2)}, u32[]{:S(2)}) collective-permute-start(bf16[192,1152]{1,0:T(8,128)(2,1)S(1)} %concatenate.28), channel_id=1, source_target_pairs={{14,0},{1023,1},{4,2},{1013,3},{18,4},{3,5},{8,6},{1017,7},{22,8},... | collective-permute-start | bytes 1327112 | tf_op jit(solution)/shard_map/ppermute | solution.py:16
  43.0 1.9 %collective-permute-start.2 = (bf16[96,1152]{1,0:T(8,128)(2,1)S(1)}, bf16[96,1152]{1,0:T(8,128)(2,1)S(1)}, u32[]{:S(2)}, u32[]{:S(2)}) collective-permute-start(bf16[96,1152]{1,0:T(8,128)(2,1)S(1)} %slice_select_fusion.3), channel_id=1, source_target_pairs={{16,0},{1009,1},{18,2},{1011,3},{20,4},{1013,5},{22,6},{1015,7},{2... | collective-permute-start | bytes 663560 | tf_op jit(solution)/shard_map/ppermute | solution.py:16
  44.9 3.3 %collective-permute-done.8 = bf16[192,576]{1,0:T(8,128)(2,1)} collective-permute-done((bf16[192,576]{1,0:T(8,128)(2,1)}, bf16[192,576]{1,0:T(8,128)(2,1)}, u32[]{:S(2)}, u32[]{:S(2)}) %collective-permute-start.8) | collective-permute-done | bytes 221216 | tf_op jit(solution)/shard_map/ppermute | solution.py:16
  48.2 1.8 %broadcast_select_fusion.5 = (bf16[192,576]{1,0:T(8,128)(2,1)S(1)}, bf16[192,576]{1,0:T(8,128)(2,1)}) fusion(bf16[192,576]{1,0:T(8,128)(2,1)} %collective-permute-done.8, pred[]{:T(512)S(6)} %lt.10, bf16[192,288]{1,0:T(8,128)(2,1)S(1)} %collective-permute-done.7, bf16[192,288]{1,0:T(8,128)(2,1)S(1)} %get-tuple-element.6), kind=kLoop, calls=%fused_computation.85 | loop fusion | flops 663552 | bytes 884737 | tf_op jit(solution)/shard_map/jit(_where)/select_n | solution.py:81
  50.3 9.9 %collective-permute-done.2 = bf16[96,1152]{1,0:T(8,128)(2,1)S(1)} collective-permute-done((bf16[96,1152]{1,0:T(8,128)(2,1)S(1)}, bf16[96,1152]{1,0:T(8,128)(2,1)S(1)}, u32[]{:S(2)}, u32[]{:S(2)}) %collective-permute-start.2) | collective-permute-done | bytes 221216 | tf_op jit(solution)/shard_map/ppermute | solution.py:16
  61.7 1.9 %collective-permute-start.4 = (bf16[96,1152]{1,0:T(8,128)(2,1)}, bf16[96,1152]{1,0:T(8,128)(2,1)}, u32[]{:S(2)}, u32[]{:S(2)}) collective-permute-start(bf16[96,1152]{1,0:T(8,128)(2,1)} %slice_select_fusion.2), channel_id=1, source_target_pairs={{1020,0},{1021,1},{6,2},{7,3},{0,4},{1,5},{10,6},{11,7},{4,8},{5,9... | collective-permute-start | bytes 663560 | tf_op jit(solution)/shard_map/ppermute | solution.py:16
  63.6 1.7 %convolution_add_fusion.3 = f32[192,1152]{1,0:T(8,128)S(1)} fusion(f32[192,1152]{1,0:T(8,128)S(1)} %fusion.47, bf16[96,1152]{1,0:T(8,128)(2,1)} %copy-done.6, bf16[192,1152]{1,0:T(8,128)(2,1)S(1)} %concatenate.27, f32[]{:T(128)} %bitcast.31, f32[]{:T(128)} %bitcast.25, s32[96]{0:T(128)S(1)} %get-tuple-element.31, s32[96]{0:T(128)S(1)} %get-tuple-element.32, ...), kind=kOutput, calls=%fused_computation.5 | convolution fusion | flops 85413888 | bytes 2435337 | tf_op jit(solution)/shard_map/dot_general | solution.py:121
  65.3 1.9 %collective-permute-start.5 = (bf16[192,1152]{1,0:T(8,128)(2,1)S(1)}, bf16[192,1152]{1,0:T(8,128)(2,1)}, u32[]{:S(2)}, u32[]{:S(2)}) collective-permute-start(bf16[192,1152]{1,0:T(8,128)(2,1)S(1)} %collective-permute-done.3), channel_id=1, source_target_pairs={{16,0},{1009,1},{18,2},{1011,3},{20,4},{1013,5},{22,6},{1015,7},{2... | collective-permute-start | bytes 1327112 | tf_op jit(solution)/shard_map/ppermute | solution.py:16
  67.2 11.1 %collective-permute-done.4 = bf16[96,1152]{1,0:T(8,128)(2,1)} collective-permute-done((bf16[96,1152]{1,0:T(8,128)(2,1)}, bf16[96,1152]{1,0:T(8,128)(2,1)}, u32[]{:S(2)}, u32[]{:S(2)}) %collective-permute-start.4) | collective-permute-done | bytes 221216 | tf_op jit(solution)/shard_map/ppermute | solution.py:16
  78.4 1.9 %collective-permute-start.6 = (bf16[96,1152]{1,0:T(8,128)(2,1)}, bf16[96,1152]{1,0:T(8,128)(2,1)}, u32[]{:S(2)}, u32[]{:S(2)}) collective-permute-start(bf16[96,1152]{1,0:T(8,128)(2,1)} %collective-permute-done.4), channel_id=1, source_target_pairs={{16,0},{1009,1},{18,2},{1011,3},{20,4},{1013,5},{22,6},{1015,7},{2... | collective-permute-start | bytes 663560 | tf_op jit(solution)/shard_map/ppermute | solution.py:16
  80.3 1.7 %fusion.46 = f32[192,1152]{1,0:T(8,128)S(1)} fusion(bf16[96,1152]{1,0:T(8,128)(2,1)} %collective-permute-done.4, bf16[192,1152]{1,0:T(8,128)(2,1)S(1)} %concatenate.27, f32[]{:T(128)} %bitcast.35, f32[]{:T(128)} %bitcast.29), kind=kOutput, calls=%fused_computation.57 | convolution fusion | flops 85063680 | bytes 1548296 | tf_op jit(solution)/shard_map/dot_general | solution.py:121
  82.0 1.7 %fusion.1 = f32[192,1152]{1,0:T(8,128)} fusion(f32[192,1152]{1,0:T(8,128)S(1)} %fusion.46, f32[192,1152]{1,0:T(8,128)S(1)} %convolution_add_fusion.3, bf16[192,1152]{1,0:T(8,128)(2,1)S(1)} %collective-permute-done.3, bf16[192,1152]{1,0:T(8,128)(2,1)S(1)} %concatenate.27, f32[]{:T(128)} %bitcast.32, f32[]{:T(128)} %bitcast.26), kind=kOutput, calls=%fused_computation.4 | convolution fusion | flops 170569728 | bytes 3538952 | tf_op jit(solution)/shard_map/dot_general | solution.py:121
  83.7 5.0 %collective-permute-done.6 = bf16[96,1152]{1,0:T(8,128)(2,1)} collective-permute-done((bf16[96,1152]{1,0:T(8,128)(2,1)}, bf16[96,1152]{1,0:T(8,128)(2,1)}, u32[]{:S(2)}, u32[]{:S(2)}) %collective-permute-start.6) | collective-permute-done | bytes 221216 | tf_op jit(solution)/shard_map/ppermute | solution.py:16
  88.7 1.8 %fusion.45 = f32[192,1152]{1,0:T(8,128)S(1)} fusion(bf16[96,1152]{1,0:T(8,128)(2,1)} %collective-permute-done.6, bf16[192,1152]{1,0:T(8,128)(2,1)S(1)} %concatenate.27, f32[]{:T(128)} %bitcast.34, f32[]{:T(128)} %bitcast.28), kind=kOutput, calls=%fused_computation.56 | convolution fusion | flops 85063680 | bytes 1548296 | tf_op jit(solution)/shard_map/dot_general | solution.py:121
  90.5 3.0 %multiply_reduce_fusion = (f32[192]{0:T(256)S(1)}, f32[192,1152]{1,0:T(8,128)}) fusion(bf16[192,1152]{1,0:T(8,128)(2,1)S(1)} %concatenate.27, bf16[192,576]{1,0:T(8,128)(2,1)} %get-tuple-element.13, bf16[192,576]{1,0:T(8,128)(2,1)S(1)} %get-tuple-element.12, f32[192,1152]{1,0:T(8,128)S(1)} %fusion.45, f32[192,1152]{1,0:T(8,128)S(1)} %copy-done.1, ...), kind=kOutput, calls=%fused_computation.60 | convolution fusion | flops 172339008 | bytes 3982088 | tf_op jit(solution)/shard_map/dot_general | solution.py:121
  93.4 1.5 %multiply_subtract_fusion = f32[192,1152]{1,0:T(8,128)S(1)} fusion(f32[192,1152]{1,0:T(8,128)} %get-tuple-element.30, bf16[192,1152]{1,0:T(8,128)(2,1)S(1)} %concatenate.27, f32[192]{0:T(256)S(1)} %get-tuple-element.29, bf16[192,576]{1,0:T(8,128)(2,1)S(1)} %copy-done.5, bf16[192,576]{1,0:T(8,128)(2,1)S(1)} %get-tuple-element.12), kind=kLoop, calls=%fused_computation.59 | loop fusion | flops 1769472 | bytes 2654976 | tf_op jit(solution)/shard_map/sub | solution.py:144
  95.1 1.9 %collective-permute-start.9 = (bf16[192,576]{1,0:T(8,128)(2,1)S(1)}, bf16[192,576]{1,0:T(8,128)(2,1)S(1)}, u32[]{:S(2)}, u32[]{:S(2)}) collective-permute-start(bf16[192,576]{1,0:T(8,128)(2,1)S(1)} %select_convert_fusion.1), channel_id=1, source_target_pairs={{2,0},{3,1},{0,2},{1,3},{6,4},{7,5},{4,6},{5,7},{10,8},{11,9},{8,1... | collective-permute-start | bytes 663560 | tf_op jit(solution)/shard_map/ppermute | solution.py:16
  97.0 5.8 %collective-permute-done.9 = bf16[192,576]{1,0:T(8,128)(2,1)S(1)} collective-permute-done((bf16[192,576]{1,0:T(8,128)(2,1)S(1)}, bf16[192,576]{1,0:T(8,128)(2,1)S(1)}, u32[]{:S(2)}, u32[]{:S(2)}) %collective-permute-start.9) | collective-permute-done | bytes 221216 | tf_op jit(solution)/shard_map/ppermute | solution.py:16
  102.8 1.7 %fusion.48 = f32[192,1152]{1,0:T(8,128)S(1)} fusion(bf16[1152,288]{0,1:T(8,128)(2,1)} %collective-permute-done.10, bf16[1152,288]{0,1:T(8,128)(2,1)S(1)} %copy-done.4, bf16[192,576]{1,0:T(8,128)(2,1)S(1)} %collective-permute-done.9, f32[192,1152]{1,0:T(8,128)S(1)} %multiply_subtract_fusion, f32[192]{0:T(256)S(1)} %get-tuple-element.22, pred[]{:T(512)S(6)} %lt.10), kind=kOutput, calls=%fused_computation.62 | convolution fusion | flops 258342912 | bytes 3441665 | tf_op jit(solution)/shard_map/dot_general | solution.py:155
  104.5 1.7 %convolution_add_fusion = f32[192,1152]{1,0:T(8,128)S(1)} fusion(f32[192,1152]{1,0:T(8,128)S(1)} %fusion.48, bf16[1152,288]{0,1:T(8,128)(2,1)} %collective-permute-done.10, bf16[1152,288]{0,1:T(8,128)(2,1)S(1)} %copy-done.4, bf16[192,576]{1,0:T(8,128)(2,1)S(1)} %collective-permute-done.9, f32[192,1152]{1,0:T(8,128)S(1)} %multiply_subtract_fusion, ...), kind=kOutput, calls=%fused_computation | convolution fusion | flops 258232320 | bytes 4326401 | tf_op jit(solution)/shard_map/dot_general | solution.py:153
  106.4 2.2 %collective-permute-start.11 = (bf16[192,576]{1,0:T(8,128)(2,1)S(1)}, bf16[192,576]{1,0:T(8,128)(2,1)S(1)}, u32[]{:S(2)}, u32[]{:S(2)}) collective-permute-start(bf16[192,576]{1,0:T(8,128)(2,1)S(1)} %select_convert_fusion), channel_id=1, source_target_pairs={{2,0},{3,1},{0,2},{1,3},{6,4},{7,5},{4,6},{5,7},{10,8},{11,9},{8,1... | collective-permute-start | bytes 663560 | tf_op jit(solution)/shard_map/ppermute | solution.py:16
  108.6 4.7 %collective-permute-done.11 = bf16[192,576]{1,0:T(8,128)(2,1)S(1)} collective-permute-done((bf16[192,576]{1,0:T(8,128)(2,1)S(1)}, bf16[192,576]{1,0:T(8,128)(2,1)S(1)}, u32[]{:S(2)}, u32[]{:S(2)}) %collective-permute-start.11) | collective-permute-done | bytes 221216 | tf_op jit(solution)/shard_map/ppermute | solution.py:16
  113.7 5.6 %collective-permute-start.12 = (f32[192,288]{1,0:T(8,128)S(1)}, f32[192,288]{1,0:T(8,128)S(1)}, u32[]{:S(2)}, u32[]{:S(2)}) collective-permute-start(f32[192,288]{1,0:T(8,128)S(1)} %slice_select_fusion), channel_id=1, source_target_pairs={{1,0},{0,1},{3,2},{2,3},{5,4},{4,5},{7,6},{6,7},{9,8},{8,9},{11,10... | collective-permute-start | bytes 663560 | tf_op jit(solution)/shard_map/ppermute | solution.py:16
  (47 shorter events, 7.3 us)
Async XLA Ops:
  0.6 1.0 copy-start
  0.6 2.6 %copy-start.7 = (bf16[192,1152]{1,0:T(8,128)(2,1)S(1)}, bf16[192,1152]{1,0:T(8,128)(2,1)}, u32[]{:S(2)}) copy-start(bf16[192,1152]{1,0:T(8,128)(2,1)} %param.7) | copy-start | bytes 1327108
  0.7 2.6 %copy-start.2 = (bf16[1152,288]{0,1:T(8,128)(2,1)S(1)}, bf16[1152,288]{0,1:T(8,128)(2,1)}, u32[]{:S(2)}) copy-start(bf16[1152,288]{0,1:T(8,128)(2,1)} %param.8) | copy-start | bytes 1990660
  23.2 4.8 %copy-start.3 = (bf16[1152,288]{0,1:T(8,128)(2,1)S(1)}, bf16[1152,288]{0,1:T(8,128)(2,1)}, u32[]{:S(2)}) copy-start(bf16[1152,288]{0,1:T(8,128)(2,1)} %param.10) | copy-start | bytes 1990660
  23.4 9.7 %collective-permute-start = (bf16[384,288]{1,0:T(8,128)(2,1)S(1)}, bf16[384,288]{1,0:T(8,128)(2,1)S(1)}, u32[]{:S(2)}, u32[]{:S(2)}) collective-permute-start(bf16[384,288]{1,0:T(8,128)(2,1)S(1)} %pad_maximum_fusion.5), channel_id=1, source_target_pairs={{2,0},{3,1},{0,2},{1,3},{6,4},{7,5},{4,6},{5,7},{10,8},{11,9},{8,1... | collective-permute-start | bytes 663560 | tf_op jit(solution)/shard_map/ppermute | solution.py:16
  25.4 12.2 %collective-permute-start.7 = (bf16[192,288]{1,0:T(8,128)(2,1)S(1)}, bf16[192,288]{1,0:T(8,128)(2,1)S(1)}, u32[]{:S(2)}, u32[]{:S(2)}) collective-permute-start(bf16[192,288]{1,0:T(8,128)(2,1)S(1)} %get-tuple-element.7), channel_id=1, source_target_pairs={{1,0},{0,1},{3,2},{2,3},{5,4},{4,5},{7,6},{6,7},{9,8},{8,9},{11,10... | collective-permute-start | bytes 331784 | tf_op jit(solution)/shard_map/ppermute | solution.py:16
  29.2 67.8 %collective-permute-start.10 = (bf16[1152,288]{0,1:T(8,128)(2,1)}, bf16[1152,288]{0,1:T(8,128)(2,1)}, u32[]{:S(2)}, u32[]{:S(2)}) collective-permute-start(bf16[1152,288]{0,1:T(8,128)(2,1)} %get-tuple-element.3), channel_id=1, source_target_pairs={{1,0},{0,1},{3,2},{2,3},{5,4},{4,5},{7,6},{6,7},{9,8},{8,9},{11,10... | collective-permute-start | bytes 1990664 | tf_op jit(solution)/shard_map/ppermute | solution.py:16
  31.2 5.7 %copy-start.8 = (s32[192]{0:T(256)S(1)}, s32[192]{0:T(256)}, u32[]{:S(2)}) copy-start(s32[192]{0:T(256)} %param.13) | copy-start | bytes 2308
  33.4 7.2 %collective-permute-start.1 = (bf16[384,576]{1,0:T(8,128)(2,1)S(1)}, bf16[384,576]{1,0:T(8,128)(2,1)S(1)}, u32[]{:S(2)}, u32[]{:S(2)}) collective-permute-start(bf16[384,576]{1,0:T(8,128)(2,1)S(1)} %pad_maximum_fusion.3), channel_id=1, source_target_pairs={{1,0},{0,1},{3,2},{2,3},{5,4},{4,5},{7,6},{6,7},{9,8},{8,9},{11,10... | collective-permute-start | bytes 1327112 | tf_op jit(solution)/shard_map/ppermute | solution.py:16
  38.5 9.8 %collective-permute-start.8 = (bf16[192,576]{1,0:T(8,128)(2,1)}, bf16[192,576]{1,0:T(8,128)(2,1)}, u32[]{:S(2)}, u32[]{:S(2)}) collective-permute-start(bf16[192,576]{1,0:T(8,128)(2,1)} %pad_maximum_fusion.6), channel_id=1, source_target_pairs={{2,0},{3,1},{0,2},{1,3},{6,4},{7,5},{4,6},{5,7},{10,8},{11,9},{8,1... | collective-permute-start | bytes 663560 | tf_op jit(solution)/shard_map/ppermute | solution.py:16
  41.1 9.3 %copy-start.6 = (bf16[96,1152]{1,0:T(8,128)(2,1)}, bf16[96,1152]{1,0:T(8,128)(2,1)S(1)}, u32[]{:S(2)}) copy-start(bf16[96,1152]{1,0:T(8,128)(2,1)S(1)} %slice_select_fusion.3) | copy-start | bytes 663556
  41.1 19.9 %collective-permute-start.3 = (bf16[192,1152]{1,0:T(8,128)(2,1)S(1)}, bf16[192,1152]{1,0:T(8,128)(2,1)S(1)}, u32[]{:S(2)}, u32[]{:S(2)}) collective-permute-start(bf16[192,1152]{1,0:T(8,128)(2,1)S(1)} %concatenate.28), channel_id=1, source_target_pairs={{14,0},{1023,1},{4,2},{1013,3},{18,4},{3,5},{8,6},{1017,7},{22,8},... | collective-permute-start | bytes 1327112 | tf_op jit(solution)/shard_map/ppermute | solution.py:16
  43.0 17.3 %collective-permute-start.2 = (bf16[96,1152]{1,0:T(8,128)(2,1)S(1)}, bf16[96,1152]{1,0:T(8,128)(2,1)S(1)}, u32[]{:S(2)}, u32[]{:S(2)}) collective-permute-start(bf16[96,1152]{1,0:T(8,128)(2,1)S(1)} %slice_select_fusion.3), channel_id=1, source_target_pairs={{16,0},{1009,1},{18,2},{1011,3},{20,4},{1013,5},{22,6},{1015,7},{2... | collective-permute-start | bytes 663560 | tf_op jit(solution)/shard_map/ppermute | solution.py:16
  61.7 16.7 %collective-permute-start.4 = (bf16[96,1152]{1,0:T(8,128)(2,1)}, bf16[96,1152]{1,0:T(8,128)(2,1)}, u32[]{:S(2)}, u32[]{:S(2)}) collective-permute-start(bf16[96,1152]{1,0:T(8,128)(2,1)} %slice_select_fusion.2), channel_id=1, source_target_pairs={{1020,0},{1021,1},{6,2},{7,3},{0,4},{1,5},{10,6},{11,7},{4,8},{5,9... | collective-permute-start | bytes 663560 | tf_op jit(solution)/shard_map/ppermute | solution.py:16
  65.3 25.1 %collective-permute-start.5 = (bf16[192,1152]{1,0:T(8,128)(2,1)S(1)}, bf16[192,1152]{1,0:T(8,128)(2,1)}, u32[]{:S(2)}, u32[]{:S(2)}) collective-permute-start(bf16[192,1152]{1,0:T(8,128)(2,1)S(1)} %collective-permute-done.3), channel_id=1, source_target_pairs={{16,0},{1009,1},{18,2},{1011,3},{20,4},{1013,5},{22,6},{1015,7},{2... | collective-permute-start | bytes 1327112 | tf_op jit(solution)/shard_map/ppermute | solution.py:16
  78.4 10.3 %collective-permute-start.6 = (bf16[96,1152]{1,0:T(8,128)(2,1)}, bf16[96,1152]{1,0:T(8,128)(2,1)}, u32[]{:S(2)}, u32[]{:S(2)}) collective-permute-start(bf16[96,1152]{1,0:T(8,128)(2,1)} %collective-permute-done.4), channel_id=1, source_target_pairs={{16,0},{1009,1},{18,2},{1011,3},{20,4},{1013,5},{22,6},{1015,7},{2... | collective-permute-start | bytes 663560 | tf_op jit(solution)/shard_map/ppermute | solution.py:16
  88.7 1.8 %copy-start.1 = (f32[192,1152]{1,0:T(8,128)S(1)}, f32[192,1152]{1,0:T(8,128)}, u32[]{:S(2)}) copy-start(f32[192,1152]{1,0:T(8,128)} %fusion.1) | copy-start | bytes 2654212
  90.5 3.0 %copy-start.5 = (bf16[192,576]{1,0:T(8,128)(2,1)S(1)}, bf16[192,576]{1,0:T(8,128)(2,1)}, u32[]{:S(2)}) copy-start(bf16[192,576]{1,0:T(8,128)(2,1)} %get-tuple-element.13) | copy-start | bytes 663556
  93.4 9.4 %copy-start.4 = (bf16[1152,288]{0,1:T(8,128)(2,1)S(1)}, bf16[1152,288]{0,1:T(8,128)(2,1)}, u32[]{:S(2)}) copy-start(bf16[1152,288]{0,1:T(8,128)(2,1)} %get-tuple-element.2) | copy-start | bytes 1990660
  95.1 7.7 %collective-permute-start.9 = (bf16[192,576]{1,0:T(8,128)(2,1)S(1)}, bf16[192,576]{1,0:T(8,128)(2,1)S(1)}, u32[]{:S(2)}, u32[]{:S(2)}) collective-permute-start(bf16[192,576]{1,0:T(8,128)(2,1)S(1)} %select_convert_fusion.1), channel_id=1, source_target_pairs={{2,0},{3,1},{0,2},{1,3},{6,4},{7,5},{4,6},{5,7},{10,8},{11,9},{8,1... | collective-permute-start | bytes 663560 | tf_op jit(solution)/shard_map/ppermute | solution.py:16
  106.4 6.9 %collective-permute-start.11 = (bf16[192,576]{1,0:T(8,128)(2,1)S(1)}, bf16[192,576]{1,0:T(8,128)(2,1)S(1)}, u32[]{:S(2)}, u32[]{:S(2)}) collective-permute-start(bf16[192,576]{1,0:T(8,128)(2,1)S(1)} %select_convert_fusion), channel_id=1, source_target_pairs={{2,0},{3,1},{0,2},{1,3},{6,4},{7,5},{4,6},{5,7},{10,8},{11,9},{8,1... | collective-permute-start | bytes 663560 | tf_op jit(solution)/shard_map/ppermute | solution.py:16
  113.7 6.8 %collective-permute-start.12 = (f32[192,288]{1,0:T(8,128)S(1)}, f32[192,288]{1,0:T(8,128)S(1)}, u32[]{:S(2)}, u32[]{:S(2)}) collective-permute-start(f32[192,288]{1,0:T(8,128)S(1)} %slice_select_fusion), channel_id=1, source_target_pairs={{1,0},{0,1},{3,2},{2,3},{5,4},{4,5},{7,6},{6,7},{9,8},{8,9},{11,10... | collective-permute-start | bytes 663560 | tf_op jit(solution)/shard_map/ppermute | solution.py:16

commit v2 on v1

v2 whole, which is shorter than its diff:
```python
import jax
import jax.numpy as jnp
from jax import lax
from jax.experimental import pallas as pl
from jax.experimental.pallas import tpu as pltpu
from jax.sharding import PartitionSpec as P

AXES = ("dp", "tensor")
ROUND = 4
LANES = 128
F32, BF16 = jnp.float32, jnp.bfloat16
BY_COLUMNS = (((1,), (1,)), ((), ()))


def exchange(block, groups, source):
    route = []
    for n in range(groups):
        for t in range(4):
            m, u = source(n, t)
            route.append(((m % groups) * 4 + u, n * 4 + t))
    return lax.ppermute(block, AXES, route)


def neighbour(n, t):
    return [(n + 3, 2), (n - 1, 3), (n + 1, 0), (n - 3, 1)][t]


def relay(n, t):
    return (n - 1, t) if t < 2 else (n + 1, t)


def beyond(n, t):
    return (n + ROUND, t) if t % 2 == 0 else (n - ROUND, t)


def chip_swap(n, t):
    return (n, t ^ 2)


def core_swap(n, t):
    return (n, t ^ 1)


def cross_swap(n, t):
    return (n, t ^ 3)


def call(kernel, outs, *operands, scratch=(), flops=0):
    specs = [
        pl.BlockSpec(memory_space=pltpu.SMEM if x.ndim == 1 else pltpu.VMEM) for x in operands
    ]
    moved = sum(x.size * x.dtype.itemsize for x in operands)
    return pl.pallas_call(
        kernel,
        cost_estimate=pl.CostEstimate(flops=flops, bytes_accessed=moved, transcendentals=0),
        out_shape=[jax.ShapeDtypeStruct(shape, dtype) for shape, dtype in outs],
        in_specs=specs,
        out_specs=[pl.BlockSpec(memory_space=pltpu.VMEM)] * len(outs),
        scratch_shapes=[pltpu.VMEM(shape, dtype) for shape, dtype in scratch],
        compiler_params=pltpu.CompilerParams(vmem_limit_bytes=24 * 2**20),
    )(*operands)


def packed_rows(rows, columns):
    whole, rest = columns // LANES, columns % LANES
    return rows * whole + (rows * rest) // LANES


def pack(ref, at, value):
    rows, columns = value.shape
    whole, rest = columns // LANES, columns % LANES
    for i in range(whole):
        ref[at + i * rows : at + (i + 1) * rows, :] = value[:, i * LANES : (i + 1) * LANES]
    if rest:
        side = LANES // rest
        short = rows // side
        at = at + whole * rows
        ref[at : at + short, :] = jnp.concatenate(
            [value[i * short : (i + 1) * short, whole * LANES :] for i in range(side)], axis=1
        )


def unpack(ref, at, rows, columns):
    whole, rest = columns // LANES, columns % LANES
    tiles = [ref[at + i * rows : at + (i + 1) * rows, :] for i in range(whole)]
    if rest:
        side = LANES // rest
        short = rows // side
        last = ref[at + whole * rows : at + whole * rows + short, :]
        tiles.append(
            jnp.concatenate([last[:, i * rest : (i + 1) * rest] for i in range(side)], axis=0)
        )
    return jnp.concatenate(tiles, axis=1)


def beside(parts, axis):
    cut = parts[0].shape[axis] // LANES * LANES
    size = parts[0].shape[axis]
    return jnp.concatenate(
        [lax.slice_in_dim(x, 0, cut, axis=axis) for x in parts]
        + [lax.slice_in_dim(x, cut, size, axis=axis) for x in parts],
        axis=axis,
    )


def unit_parts(place, img, txt, own, fixed, moving, rest_mine, rest_theirs):
    rows, span = img.shape
    core0 = place[0] == 0
    a, b = img[...], txt[...]
    keep, travel = jnp.where(core0, a, b), jnp.where(core0, b, a)
    keep_low, travel_low = keep.astype(BF16), travel.astype(BF16)
    fixed[...] = keep_low
    moving[...] = travel_low
    rest_mine[...] = (keep - keep_low.astype(F32)).astype(BF16)
    rest_theirs[...] = (travel - travel_low.astype(F32)).astype(BF16)
    pack(own, 0, keep_low)
    pack(own, packed_rows(rows, span), travel_low)


def pair_up(place, fixed, moving, got, pair):
    rows, span = fixed.shape
    chip0 = place[1] == 0
    second = packed_rows(rows, span)
    for i, ref in enumerate((fixed, moving)):
        own, other = ref[...], unpack(got, i * second, rows, span)
        first, last = jnp.where(chip0, own, other), jnp.where(chip0, other, own)
        pair[i * rows : (i + 1) * rows, :] = beside([first, last], 1)


def whole_width(place, pair, peer, fixed, own_half, other_half):
    rows = fixed.shape[0]
    half = rows // 2
    span = pair.shape[1] // 2
    cut = span // LANES * LANES
    chip0 = place[1] == 0

    def widened(i):
        mine = pair[i * rows : (i + 1) * rows, :]
        theirs = peer[(1 - i) * rows : (2 - i) * rows, :]
        end = cut + span
        return jnp.concatenate(
            [mine[:, :cut], theirs[:, :cut], mine[:, cut : 2 * cut], theirs[:, cut : 2 * cut]]
            + [mine[:, 2 * cut : end], theirs[:, 2 * cut : end], mine[:, end:], theirs[:, end:]],
            axis=1,
        )

    fixed[...] = widened(0)
    moving = widened(1)
    top, bottom = moving[:half], moving[half:]
    own_half[...] = jnp.where(chip0, top, bottom)
    other_half[...] = jnp.where(chip0, bottom, top)


def pull(factors, fixed, block, sign=None):
    logits = factors[0] * lax.dot_general(
        fixed, block, BY_COLUMNS, preferred_element_type=F32
    ) + factors[1]
    if sign is None:
        weight = 16.0 * jax.nn.sigmoid(logits)
    else:
        weight = -16.0 * sign * jax.nn.sigmoid(-sign * logits)
    return jnp.dot(weight.astype(BF16), block, preferred_element_type=F32)


def first_sum(factors, fixed, sign, own_half, total):
    total[...] = pull(factors, fixed[...], own_half[...], sign[...])


def next_sum(factors, fixed, before, *refs):
    block = jnp.concatenate([x[...] for x in refs[:-1]], axis=0)
    refs[-1][...] = before[...] + pull(factors, fixed[...], block)


def on_diagonal(rows):
    shape = (rows, rows)
    return lax.broadcasted_iota(jnp.int32, shape, 0) == lax.broadcasted_iota(jnp.int32, shape, 1)


def last_sum(place, factors, fixed, before, far_opposite, inv, keep, inner_kept, give):
    rows, width = fixed.shape
    span = width // 4
    cut = span // LANES * LANES
    chip0 = place[1] == 0
    a = fixed[...]
    total = before[...] + pull(factors, a, far_opposite[...])
    unit = a.astype(F32)
    by_row = factors[0] * inv[...]
    inner = jnp.sum(unit * total, axis=1, keepdims=True) * by_row
    across = total * by_row - unit * inner
    middle = 4 * cut + 2 * (span - cut)
    first = jnp.concatenate([across[:, : 2 * cut], across[:, 4 * cut : middle]], axis=1)
    last = jnp.concatenate([across[:, 2 * cut : 4 * cut], across[:, middle:]], axis=1)
    keep[...] = jnp.where(chip0, first, last)
    inner_kept[...] = inner
    pack(give, 0, jnp.where(chip0, last, first).astype(BF16))
    at = packed_rows(rows, 2 * span)
    line = jnp.sum(jnp.where(on_diagonal(rows), inner, 0.0), axis=0, keepdims=True)
    give[at : at + 16, :] = jnp.broadcast_to(line[:, :LANES], (16, LANES)).astype(BF16)
    give[at + 16 : at + 32, :] = jnp.broadcast_to(line[:, rows - LANES :], (16, LANES)).astype(BF16)


def finish_sum(kept, inner_kept, got, rest_mine, rest_peer, stacked):
    rows, width = kept.shape
    at = packed_rows(rows, width)
    start, end = got[at : at + 1, :], got[at + 16 : at + 17, :]
    line = jnp.concatenate([start, end[:, 2 * LANES - rows :]], axis=1).astype(F32)
    other = jnp.sum(jnp.where(on_diagonal(rows), line, 0.0), axis=1, keepdims=True)
    rest = beside([rest_mine[...], rest_peer[...]], 1).astype(F32)
    demb = kept[...] + unpack(got, 0, rows, width).astype(F32) - rest * (inner_kept[...] + other)
    high = demb.astype(BF16)
    stacked[:rows, :] = high
    stacked[rows:, :] = (demb - high.astype(F32)).astype(BF16)


def through_matrix(
    place, kept, inner_kept, got, rest_mine, rest_peer, mine, peer, to_chip, to_cross, to_core, keep, stacked
):
    rows, width = kept.shape
    span = width // 2
    finish_sum(kept, inner_kept, got, rest_mine, rest_peer, stacked)
    matrix = beside([mine[...], peer[...]], 0)
    part = jnp.dot(stacked[...], matrix, preferred_element_type=F32)
    part = part[:rows] + part[rows:]
    spans = [part[:, u * span : (u + 1) * span] for u in range(4)]
    for t in range(4):

        @pl.when(2 * place[1] + place[0] == t)
        def _(t=t):
            pack(to_chip, 0, spans[t ^ 2].astype(BF16))
            pack(to_cross, 0, spans[t ^ 3].astype(BF16))
            pack(to_core, 0, spans[t ^ 1].astype(BF16))
            keep[...] = spans[t]


def last_add(place, from_chip, from_cross, from_core, kept, img, txt):
    rows, span = kept.shape
    core0 = place[0] == 0
    mine = kept[...] + unpack(from_chip, 0, rows, span).astype(F32)
    theirs = unpack(from_core, 0, rows, span).astype(F32)
    theirs = theirs + unpack(from_cross, 0, rows, span).astype(F32)
    img[...] = jnp.where(core0, mine, theirs)
    txt[...] = jnp.where(core0, theirs, mine)


def shards(
    picture_averaged_vectors,
    picture_mapping_matrix,
    caption_averaged_vectors,
    caption_mapping_matrix,
    sharpness_factor,
    offset_term,
    paired_caption_index,
):
    groups = lax.axis_size("dp")
    rows = picture_averaged_vectors.shape[0]
    half = rows // 2
    span = picture_mapping_matrix.shape[1]
    width = 4 * span
    t = lax.axis_index("tensor")
    core0 = t % 2 == 0
    chip0 = t < 2
    place = jnp.stack([t % 2, t // 2]).astype(jnp.int32)
    factors = jnp.concatenate([sharpness_factor, offset_term])

    img_emb = jnp.dot(
        picture_averaged_vectors, picture_mapping_matrix, preferred_element_type=F32
    )
    txt_emb = jnp.dot(
        caption_averaged_vectors, caption_mapping_matrix, preferred_element_type=F32
    )
    squares = jnp.concatenate(
        [jnp.sum(img_emb * img_emb, axis=1), jnp.sum(txt_emb * txt_emb, axis=1)]
    )
    inv = lax.rsqrt(lax.psum(squares, "tensor") + 1e-06)
    inv_img, inv_txt = inv[:rows], inv[rows:]
    img_unit = img_emb * inv_img[:, None]
    txt_unit = txt_emb * inv_txt[:, None]
    piece = ((rows, span), BF16)
    own, fixed_own, moving_own, rest_mine, rest_theirs = call(
        unit_parts,
        [((2 * packed_rows(rows, span), LANES), BF16)] + [piece] * 4,
        place,
        img_unit,
        txt_unit,
    )
    other = exchange(own, groups, chip_swap)
    rest_peer = exchange(rest_theirs, groups, core_swap)
    img_matrix, txt_matrix, _ = lax.optimization_barrier(
        (picture_mapping_matrix.T, caption_mapping_matrix.T, own)
    )
    matrix_mine = jnp.where(core0, img_matrix, txt_matrix)
    matrix_theirs = jnp.where(core0, txt_matrix, img_matrix)
    matrix_peer = exchange(matrix_theirs, groups, core_swap)
    (pair,) = call(pair_up, [((2 * rows, 2 * span), BF16)], place, fixed_own, moving_own, other)
    peer = exchange(pair, groups, core_swap)
    peer, matrix_peer = lax.optimization_barrier((peer, matrix_peer))
    fixed, own_half, other_half = call(
        whole_width,
        [((rows, width), BF16), ((half, width), BF16), ((half, width), BF16)],
        place,
        pair,
        peer,
    )

    inv_fixed = jnp.where(core0, inv_img, inv_txt)[:, None]

    first_row = lax.axis_index("dp") * rows
    ids = first_row + jnp.arange(rows, dtype=jnp.int32)
    half_ids = jnp.where(chip0, ids[:half], ids[half:])
    half_index = jnp.where(chip0, paired_caption_index[:half], paired_caption_index[half:])
    matched = jnp.where(
        core0,
        paired_caption_index[:, None] == half_ids[None, :],
        ids[:, None] == half_index[None, :],
    )
    sign = jnp.where(matched, 1.0, -1.0).astype(F32)

    sums = [((rows, width), F32)]
    near_relayed = exchange(other_half, groups, neighbour)
    near_other = exchange(own_half, groups, neighbour)
    (total,) = call(first_sum, sums, factors, fixed, sign, own_half)
    near_relayed, total = lax.optimization_barrier((near_relayed, total))
    opposite = exchange(near_relayed, groups, relay)
    far_own = exchange(own_half, groups, beyond)
    far_relayed = exchange(near_relayed, groups, beyond)
    far_other = exchange(near_other, groups, beyond)
    far_opposite = exchange(opposite, groups, beyond)
    nearer = (near_relayed, near_other, opposite)
    (total,) = call(
        next_sum, sums, factors, fixed, total, *nearer, far_own, far_relayed, far_other
    )
    keep, inner_kept, give = call(
        last_sum,
        [
            ((rows, 2 * span), F32),
            ((rows, 1), F32),
            ((packed_rows(rows, 2 * span) + 32, LANES), BF16),
        ],
        place,
        factors,
        fixed,
        total,
        far_opposite,
        inv_fixed,
    )
    got = exchange(give, groups, chip_swap)
    part = ((rows, span), F32)
    sent = ((packed_rows(rows, span), LANES), BF16)
    to_chip, to_cross, to_core, keep = call(
        through_matrix,
        [sent, sent, sent, part],
        place,
        keep,
        inner_kept,
        got,
        rest_mine,
        rest_peer,
        matrix_mine,
        matrix_peer,
        scratch=[((2 * rows, 2 * span), BF16)],
    )
    from_chip = exchange(to_chip, groups, chip_swap)
    from_cross = exchange(to_cross, groups, cross_swap)
    from_core = exchange(to_core, groups, core_swap)
    return tuple(call(last_add, [part, part], place, from_chip, from_cross, from_core, keep))


def solution(mesh):
    in_specs = (
        P("dp", None),
        P(None, "tensor"),
        P("dp", None),
        P(None, "tensor"),
        P(),
        P(),
        P("dp"),
    )
    out_specs = (P("dp", "tensor"), P("dp", "tensor"))
    return jax.shard_map(shards, mesh=mesh, in_specs=in_specs, out_specs=out_specs, check_vma=False)
```

time: 122 us -> 106 us (0.87)
  matrix products: 16.1 us -> 2.28 us
  Pallas kernels: 0 us -> 11.3 us
  waiting for transfers between devices: 43 us -> 32 us
  other arithmetic: 8.37 us -> 1.63 us
  starting transfers between devices: 31.3 us -> 34.7 us
    dot_general x8 -> x0, matrix products: 13.9 us -> none  [the longest x6 10.5 us: pull(): return jnp.dot(weight.astype(bf16), block, preferred_element_type=f32)]
    pallas_call x0 -> x8, Pallas kernels: none -> 11.3 us  [call(): pl.pallas_call(kernel, cost_estimate=pl.CostEstimate(flops=flops, bytes_a...]
    ppermute x13 -> x15, waiting for transfers between devices: 43 us -> 32 us  [exchange(): return lax.ppermute(block, AXES, route)]
    select_n x8 -> x3, other arithmetic: 5.19 us -> 1.18 us  [the longest x1 0.99 us: shards(): matrix_mine = jnp.where(core0, img_matrix, txt_matrix)]
    ppermute x13 -> x15, starting transfers between devices: 31.3 us -> 34.7 us  [exchange(): return lax.ppermute(block, AXES, route)]
    sub x1 -> x0, other arithmetic: 1.48 us -> none  [shards(): across = total - unit * jnp.sum(unit * total, axis=1, keepdims=True)]
    unnamed x18, local copies, waits for them, and re-layouts: 0.26 us -> 1.7 us
  transfers between devices with their start and end apart: 13 -> 15, of which waited for: 8 -> 9; matrix products, arithmetic and copies ran while one was open for 15% -> 1% of each run, Pallas kernels for 0% -> 4%
where the time goes in v2:
time: 106 us; the launch traced here: 105 us
  starting transfers between devices  34.7 us (33%)
  waiting for transfers between devices  32 us (30%)
  blocking collectives  19.1 us (18%)
  Pallas kernels  11.3 us (11%)
  matrix products  2.28 us (2%)
  between operations  2.25 us (2%)
  local copies, waits for them, and re-layouts  1.82 us (2%)
  other arithmetic  1.63 us (2%)
    ppermute x15, starting transfers between devices, exchange(): return lax.ppermute(block, AXES, route)  34.7 us
    ppermute x15, waiting for transfers between devices, exchange(): return lax.ppermute(block, AXES, route)  32 us
    psum x1, blocking collectives, shards(): inv = lax.rsqrt(lax.psum(squares, 'tensor') + 1e-06)  19.1 us
    pallas_call x8, Pallas kernels, call(): pl.pallas_call(kernel, cost_estimate=pl.CostEstimate(flops=flops, bytes_a...  11.3 us
  transfers between devices with their start and end apart: 15, of which 9 were waited for; matrix products, arithmetic and copies ran while one was open for 1% of the time, Pallas kernels for 4%

profile of v2, /device:TPU:1, one launch (start us, length us, event | category | flops | bytes accessed | tf_op | source)
XLA Modules:
  0.0 105.1 jit_solution(18398651576381964780)
XLA Ops:
  0.7 1.0 copy-done
  1.7 1.7 %multiply_reduce_fusion = (f32[192]{0:T(256)S(1)}, f32[192,288]{1,0:T(8,128)S(1)}) fusion(bf16[192,1152]{1,0:T(8,128)(2,1)S(1)} %copy-done, bf16[1152,288]{0,1:T(8,128)(2,1)} %param.10), kind=kOutput, calls=%fused_computation.2 | convolution fusion | flops 127512384 | bytes 1327872 | tf_op jit(solution)/shard_map/dot_general | solution.py:268
  4.0 19.1 %psum.7 = f32[384]{0:T(512)S(1)} all-reduce(f32[384]{0:T(512)S(1)} %pad_maximum_fusion), channel_id=1, replica_groups=mesh['dp'=256,'tensor'=4] {'tensor'}, use_global_device_ids=true, to_apply=%region_2.3 | all-reduce | flops 384 | bytes 3072 | tf_op jit(solution)/shard_map/psum | solution.py:274
  24.2 2.0 %collective-permute-start = (bf16[864,128]{1,0:T(8,128)(2,1)S(1)}, bf16[864,128]{1,0:T(8,128)(2,1)S(1)}, u32[]{:S(2)}, u32[]{:S(2)}) collective-permute-start(bf16[864,128]{1,0:T(8,128)(2,1)S(1)} %get-tuple-element.25), channel_id=1, source_target_pairs={{2,0},{3,1},{0,2},{1,3},{6,4},{7,5},{4,6},{5,7},{10,8},{11,9},{8,1... | collective-permute-start | bytes 663560 | tf_op jit(solution)/shard_map/ppermute | solution.py:21
  26.2 1.0 broadcast_select_fusion
  27.2 2.5 %collective-permute-start.2 = (bf16[288,1152]{1,0:T(8,128)(2,1)}, bf16[288,1152]{1,0:T(8,128)(2,1)S(1)}, u32[]{:S(2)}, u32[]{:S(2)}) collective-permute-start(bf16[288,1152]{1,0:T(8,128)(2,1)} %get-tuple-element.45), channel_id=1, source_target_pairs={{1,0},{0,1},{3,2},{2,3},{5,4},{4,5},{7,6},{6,7},{9,8},{8,9},{11,10... | collective-permute-start | bytes 1990664 | tf_op jit(solution)/shard_map/ppermute | solution.py:21
  31.1 1.2 %collective-permute-done.got = bf16[864,128]{1,0:T(8,128)(2,1)S(1)} collective-permute-done((bf16[864,128]{1,0:T(8,128)(2,1)S(1)}, bf16[864,128]{1,0:T(8,128)(2,1)S(1)}, u32[]{:S(2)}, u32[]{:S(2)}) %collective-permute-start) | collective-permute-done | bytes 221216 | tf_op jit(solution)/shard_map/ppermute | solution.py:21
  33.0 3.5 %collective-permute-start.1 = (bf16[384,576]{1,0:T(8,128)(2,1)S(1)}, bf16[384,576]{1,0:T(8,128)(2,1)S(1)}, u32[]{:S(2)}, u32[]{:S(2)}) collective-permute-start(bf16[384,576]{1,0:T(8,128)(2,1)S(1)} %shard_map.87.pair), channel_id=1, source_target_pairs={{1,0},{0,1},{3,2},{2,3},{5,4},{4,5},{7,6},{6,7},{9,8},{8,9},{11,10... | collective-permute-start | bytes 1327112 | tf_op jit(solution)/shard_map/ppermute | solution.py:21
  38.8 1.9 %collective-permute-start.3 = (bf16[96,1152]{1,0:T(8,128)(2,1)S(1)}, bf16[96,1152]{1,0:T(8,128)(2,1)}, u32[]{:S(2)}, u32[]{:S(2)}) collective-permute-start(bf16[96,1152]{1,0:T(8,128)(2,1)S(1)} %get-tuple-element.30), channel_id=1, source_target_pairs={{14,0},{1023,1},{4,2},{1013,3},{18,4},{3,5},{8,6},{1017,7},{22,8},... | collective-permute-start | bytes 663560 | tf_op jit(solution)/shard_map/ppermute | solution.py:21
  40.8 1.9 %collective-permute-start.4 = (bf16[96,1152]{1,0:T(8,128)(2,1)S(1)}, bf16[96,1152]{1,0:T(8,128)(2,1)}, u32[]{:S(2)}, u32[]{:S(2)}) collective-permute-start(bf16[96,1152]{1,0:T(8,128)(2,1)S(1)} %get-tuple-element.31.own_half), channel_id=1, source_target_pairs={{14,0},{1023,1},{4,2},{1013,3},{18,4},{3,5},{8,6},{1017,7},{22,8},... | collective-permute-start | bytes 663560 | tf_op jit(solution)/shard_map/ppermute | solution.py:21
  42.8 1.2 %shard_map.89.before = f32[192,1152]{1,0:T(8,128)S(1)} custom-call(f32[2]{0:T(128)S(1)} %pad_maximum_fusion.1.factors, bf16[192,1152]{1,0:T(8,128)(2,1)S(1)} %get-tuple-element.29.fixed, f32[192,96]{1,0:T(8,128)S(1)} %select_select_fusion.sign, bf16[96,1152]{1,0:T(8,128)(2,1)S(1)} %get-tuple-element.31.own_half), custom_call_target="tpu_custom_call" | custom-call | bytes 737288 | tf_op jit(solution)/shard_map/pallas_call | solution.py:53
  43.9 8.8 %collective-permute-done.3.refs_0_ = bf16[96,1152]{1,0:T(8,128)(2,1)} collective-permute-done((bf16[96,1152]{1,0:T(8,128)(2,1)S(1)}, bf16[96,1152]{1,0:T(8,128)(2,1)}, u32[]{:S(2)}, u32[]{:S(2)}) %collective-permute-start.3) | collective-permute-done | bytes 221216 | tf_op jit(solution)/shard_map/ppermute | solution.py:21
  52.7 1.9 %collective-permute-start.5 = (bf16[96,1152]{1,0:T(8,128)(2,1)}, bf16[96,1152]{1,0:T(8,128)(2,1)}, u32[]{:S(2)}, u32[]{:S(2)}) collective-permute-start(bf16[96,1152]{1,0:T(8,128)(2,1)} %collective-permute-done.3.refs_0_), channel_id=1, source_target_pairs={{1020,0},{1021,1},{6,2},{7,3},{0,4},{1,5},{10,6},{11,7},{4,8},{5,9... | collective-permute-start | bytes 663560 | tf_op jit(solution)/shard_map/ppermute | solution.py:21
  54.6 1.9 %collective-permute-start.6 = (bf16[96,1152]{1,0:T(8,128)(2,1)S(1)}, bf16[96,1152]{1,0:T(8,128)(2,1)}, u32[]{:S(2)}, u32[]{:S(2)}) collective-permute-start(bf16[96,1152]{1,0:T(8,128)(2,1)S(1)} %get-tuple-element.31.own_half), channel_id=1, source_target_pairs={{16,0},{1009,1},{18,2},{1011,3},{20,4},{1013,5},{22,6},{1015,7},{2... | collective-permute-start | bytes 663560 | tf_op jit(solution)/shard_map/ppermute | solution.py:21
  56.6 1.9 %collective-permute-start.7 = (bf16[96,1152]{1,0:T(8,128)(2,1)}, bf16[96,1152]{1,0:T(8,128)(2,1)}, u32[]{:S(2)}, u32[]{:S(2)}) collective-permute-start(bf16[96,1152]{1,0:T(8,128)(2,1)} %collective-permute-done.3.refs_0_), channel_id=1, source_target_pairs={{16,0},{1009,1},{18,2},{1011,3},{20,4},{1013,5},{22,6},{1015,7},{2... | collective-permute-start | bytes 663560 | tf_op jit(solution)/shard_map/ppermute | solution.py:21
  58.5 1.9 %collective-permute-start.8 = (bf16[96,1152]{1,0:T(8,128)(2,1)}, bf16[96,1152]{1,0:T(8,128)(2,1)}, u32[]{:S(2)}, u32[]{:S(2)}) collective-permute-start(bf16[96,1152]{1,0:T(8,128)(2,1)} %collective-permute-done.4.refs_1_), channel_id=1, source_target_pairs={{16,0},{1009,1},{18,2},{1011,3},{20,4},{1013,5},{22,6},{1015,7},{2... | collective-permute-start | bytes 663560 | tf_op jit(solution)/shard_map/ppermute | solution.py:21
  60.4 10.3 %collective-permute-done.5.refs_2_ = bf16[96,1152]{1,0:T(8,128)(2,1)} collective-permute-done((bf16[96,1152]{1,0:T(8,128)(2,1)}, bf16[96,1152]{1,0:T(8,128)(2,1)}, u32[]{:S(2)}, u32[]{:S(2)}) %collective-permute-start.5) | collective-permute-done | bytes 221216 | tf_op jit(solution)/shard_map/ppermute | solution.py:21
  70.7 1.9 %collective-permute-start.9 = (bf16[96,1152]{1,0:T(8,128)(2,1)}, bf16[96,1152]{1,0:T(8,128)(2,1)}, u32[]{:S(2)}, u32[]{:S(2)}) collective-permute-start(bf16[96,1152]{1,0:T(8,128)(2,1)} %collective-permute-done.5.refs_2_), channel_id=1, source_target_pairs={{16,0},{1009,1},{18,2},{1011,3},{20,4},{1013,5},{22,6},{1015,7},{2... | collective-permute-start | bytes 663560 | tf_op jit(solution)/shard_map/ppermute | solution.py:21
  72.8 2.0 %collective-permute-done.8.refs_5_ = bf16[96,1152]{1,0:T(8,128)(2,1)} collective-permute-done((bf16[96,1152]{1,0:T(8,128)(2,1)}, bf16[96,1152]{1,0:T(8,128)(2,1)}, u32[]{:S(2)}, u32[]{:S(2)}) %collective-permute-start.8) | collective-permute-done | bytes 221216 | tf_op jit(solution)/shard_map/ppermute | solution.py:21
  74.8 2.6 %shard_map.90.before = f32[192,1152]{1,0:T(8,128)S(1)} custom-call(f32[2]{0:T(128)S(1)} %pad_maximum_fusion.1.factors, bf16[192,1152]{1,0:T(8,128)(2,1)S(1)} %get-tuple-element.29.fixed, f32[192,1152]{1,0:T(8,128)S(1)} %shard_map.89.before, bf16[96,1152]{1,0:T(8,128)(2,1)} %collective-permute-done.3.refs_0_, ...), custom_call_target="tpu_custom_call" | custom-call | bytes 2654216 | tf_op jit(solution)/shard_map/pallas_call | solution.py:53
  77.4 3.6 %collective-permute-done.9.far_opposite = bf16[96,1152]{1,0:T(8,128)(2,1)} collective-permute-done((bf16[96,1152]{1,0:T(8,128)(2,1)}, bf16[96,1152]{1,0:T(8,128)(2,1)}, u32[]{:S(2)}, u32[]{:S(2)}) %collective-permute-start.9) | collective-permute-done | bytes 221216 | tf_op jit(solution)/shard_map/ppermute | solution.py:21
  81.0 2.0 %shard_map.91 = (f32[192,576]{1,0:T(8,128)S(1)}, f32[192,1]{1,0:T(8,128)S(1)}, bf16[896,128]{1,0:T(8,128)(2,1)S(1)}) custom-call(s32[2]{0:T(128)S(1)} %pad_add_fusion.place, f32[2]{0:T(128)S(1)} %pad_maximum_fusion.1.factors, bf16[192,1152]{1,0:T(8,128)(2,1)S(1)} %get-tuple-element.29.fixed, f32[192,1152]{1,0:T(8,128)S(1)} %shard_map.90.before, ...), custom_call_target="tpu_custom_call" | custom-call | bytes 1549072 | tf_op jit(solution)/shard_map/pallas_call | solution.py:53
  83.0 1.9 %collective-permute-start.10 = (bf16[896,128]{1,0:T(8,128)(2,1)S(1)}, bf16[896,128]{1,0:T(8,128)(2,1)S(1)}, u32[]{:S(2)}, u32[]{:S(2)}) collective-permute-start(bf16[896,128]{1,0:T(8,128)(2,1)S(1)} %get-tuple-element.36), channel_id=1, source_target_pairs={{2,0},{3,1},{0,2},{1,3},{6,4},{7,5},{4,6},{5,7},{10,8},{11,9},{8,1... | collective-permute-start | bytes 688136 | tf_op jit(solution)/shard_map/ppermute | solution.py:21
  84.9 2.5 %collective-permute-start.11 = (bf16[192,288]{1,0:T(8,128)(2,1)S(1)}, bf16[192,288]{1,0:T(8,128)(2,1)S(1)}, u32[]{:S(2)}, u32[]{:S(2)}) collective-permute-start(bf16[192,288]{1,0:T(8,128)(2,1)S(1)} %copy-done.4), channel_id=1, source_target_pairs={{1,0},{0,1},{3,2},{2,3},{5,4},{4,5},{7,6},{6,7},{9,8},{8,9},{11,10... | collective-permute-start | bytes 331784 | tf_op jit(solution)/shard_map/ppermute | solution.py:21
  87.4 1.0 collective-permute-done.11.rest_peer
  88.4 3.1 %collective-permute-done.10.got = bf16[896,128]{1,0:T(8,128)(2,1)S(1)} collective-permute-done((bf16[896,128]{1,0:T(8,128)(2,1)S(1)}, bf16[896,128]{1,0:T(8,128)(2,1)S(1)}, u32[]{:S(2)}, u32[]{:S(2)}) %collective-permute-start.10) | collective-permute-done | bytes 229408 | tf_op jit(solution)/shard_map/ppermute | solution.py:21
  91.5 2.0 %shard_map.92 = (bf16[432,128]{1,0:T(8,128)(2,1)S(1)}, bf16[432,128]{1,0:T(8,128)(2,1)S(1)}, bf16[432,128]{1,0:T(8,128)(2,1)S(1)}, f32[192,288]{1,0:T(8,128)S(1)}) custom-call(s32[2]{0:T(128)S(1)} %pad_add_fusion.place, f32[192,576]{1,0:T(8,128)S(1)} %get-tuple-element.34.kept, f32[192,1]{1,0:T(8,128)S(1)} %get-tuple-element.35.inner_kept, ...), custom_call_target="tpu_custom_call" | custom-call | bytes 2220808 | tf_op jit(solution)/shard_map/pallas_call | solution.py:53
  93.5 2.2 %collective-permute-start.12 = (bf16[432,128]{1,0:T(8,128)(2,1)S(1)}, bf16[432,128]{1,0:T(8,128)(2,1)S(1)}, u32[]{:S(2)}, u32[]{:S(2)}) collective-permute-start(bf16[432,128]{1,0:T(8,128)(2,1)S(1)} %get-tuple-element.40), channel_id=1, source_target_pairs={{2,0},{3,1},{0,2},{1,3},{6,4},{7,5},{4,6},{5,7},{10,8},{11,9},{8,1... | collective-permute-start | bytes 331784 | tf_op jit(solution)/shard_map/ppermute | solution.py:21
  95.7 4.6 %collective-permute-start.13 = (bf16[432,128]{1,0:T(8,128)(2,1)S(1)}, bf16[432,128]{1,0:T(8,128)(2,1)S(1)}, u32[]{:S(2)}, u32[]{:S(2)}) collective-permute-start(bf16[432,128]{1,0:T(8,128)(2,1)S(1)} %get-tuple-element.41), channel_id=1, source_target_pairs={{3,0},{2,1},{1,2},{0,3},{7,4},{6,5},{5,6},{4,7},{11,8},{10,9},{9,1... | collective-permute-start | bytes 331784 | tf_op jit(solution)/shard_map/ppermute | solution.py:21
  100.4 1.9 %collective-permute-start.14 = (bf16[432,128]{1,0:T(8,128)(2,1)S(1)}, bf16[432,128]{1,0:T(8,128)(2,1)S(1)}, u32[]{:S(2)}, u32[]{:S(2)}) collective-permute-start(bf16[432,128]{1,0:T(8,128)(2,1)S(1)} %get-tuple-element.42), channel_id=1, source_target_pairs={{1,0},{0,1},{3,2},{2,3},{5,4},{4,5},{7,6},{6,7},{9,8},{8,9},{11,10... | collective-permute-start | bytes 331784 | tf_op jit(solution)/shard_map/ppermute | solution.py:21
  102.3 1.4 %collective-permute-done.13.from_cross = bf16[432,128]{1,0:T(8,128)(2,1)S(1)} collective-permute-done((bf16[432,128]{1,0:T(8,128)(2,1)S(1)}, bf16[432,128]{1,0:T(8,128)(2,1)S(1)}, u32[]{:S(2)}, u32[]{:S(2)}) %collective-permute-start.13) | collective-permute-done | bytes 110624 | tf_op jit(solution)/shard_map/ppermute | solution.py:21
  103.7 1.5 %shard_map.93 = (f32[192,288]{1,0:T(8,128)}, f32[192,288]{1,0:T(8,128)}) custom-call(s32[2]{0:T(128)S(1)} %pad_add_fusion.place, bf16[432,128]{1,0:T(8,128)(2,1)S(1)} %collective-permute-done.12.from_chip, bf16[432,128]{1,0:T(8,128)(2,1)S(1)} %collective-permute-done.13.from_cross, bf16[432,128]{1,0:T(8,128)(2,1)S(1)} %collective-permute-done.14.from_core, ...), custom_call_target="tpu_custom_call" | custom-call | bytes 552968 | tf_op jit(solution)/shard_map/pallas_call | solution.py:53
  (38 shorter events, 4.8 us)
Async XLA Ops:
  0.6 1.0 copy-start
  1.6 1.7 %copy-start.6 = (bf16[1152,288]{0,1:T(8,128)(2,1)S(1)}, bf16[1152,288]{0,1:T(8,128)(2,1)}, u32[]{:S(2)}) copy-start(bf16[1152,288]{0,1:T(8,128)(2,1)} %param.8) | copy-start | bytes 1990660
  1.7 1.7 %copy-start.7 = (bf16[192,1152]{1,0:T(8,128)(2,1)S(1)}, bf16[192,1152]{1,0:T(8,128)(2,1)}, u32[]{:S(2)}) copy-start(bf16[192,1152]{1,0:T(8,128)(2,1)} %param.7) | copy-start | bytes 1327108
  23.3 2.9 %copy-start.5 = (bf16[1152,288]{0,1:T(8,128)(2,1)S(1)}, bf16[1152,288]{0,1:T(8,128)(2,1)}, u32[]{:S(2)}) copy-start(bf16[1152,288]{0,1:T(8,128)(2,1)} %param.10) | copy-start | bytes 1990660
  24.2 3.1 %copy-start.1 = (bf16[192,288]{1,0:T(8,128)(2,1)}, bf16[192,288]{1,0:T(8,128)(2,1)S(1)}, u32[]{:S(2)}) copy-start(bf16[192,288]{1,0:T(8,128)(2,1)S(1)} %get-tuple-element.37.rest_mine) | copy-start | bytes 331780
  24.2 3.0 %copy-start.3 = (bf16[192,288]{1,0:T(8,128)(2,1)}, bf16[192,288]{1,0:T(8,128)(2,1)S(1)}, u32[]{:S(2)}) copy-start(bf16[192,288]{1,0:T(8,128)(2,1)S(1)} %get-tuple-element.38) | copy-start | bytes 331780
  24.2 8.1 %collective-permute-start = (bf16[864,128]{1,0:T(8,128)(2,1)S(1)}, bf16[864,128]{1,0:T(8,128)(2,1)S(1)}, u32[]{:S(2)}, u32[]{:S(2)}) collective-permute-start(bf16[864,128]{1,0:T(8,128)(2,1)S(1)} %get-tuple-element.25), channel_id=1, source_target_pairs={{2,0},{3,1},{0,2},{1,3},{6,4},{7,5},{4,6},{5,7},{10,8},{11,9},{8,1... | collective-permute-start | bytes 663560 | tf_op jit(solution)/shard_map/ppermute | solution.py:21
  27.2 10.2 %collective-permute-start.2 = (bf16[288,1152]{1,0:T(8,128)(2,1)}, bf16[288,1152]{1,0:T(8,128)(2,1)S(1)}, u32[]{:S(2)}, u32[]{:S(2)}) collective-permute-start(bf16[288,1152]{1,0:T(8,128)(2,1)} %get-tuple-element.45), channel_id=1, source_target_pairs={{1,0},{0,1},{3,2},{2,3},{5,4},{4,5},{7,6},{6,7},{9,8},{8,9},{11,10... | collective-permute-start | bytes 1990664 | tf_op jit(solution)/shard_map/ppermute | solution.py:21
  33.0 5.0 %collective-permute-start.1 = (bf16[384,576]{1,0:T(8,128)(2,1)S(1)}, bf16[384,576]{1,0:T(8,128)(2,1)S(1)}, u32[]{:S(2)}, u32[]{:S(2)}) collective-permute-start(bf16[384,576]{1,0:T(8,128)(2,1)S(1)} %shard_map.87.pair), channel_id=1, source_target_pairs={{1,0},{0,1},{3,2},{2,3},{5,4},{4,5},{7,6},{6,7},{9,8},{8,9},{11,10... | collective-permute-start | bytes 1327112 | tf_op jit(solution)/shard_map/ppermute | solution.py:21
  36.7 0.7 copy-start.8
  38.8 13.9 %collective-permute-start.3 = (bf16[96,1152]{1,0:T(8,128)(2,1)S(1)}, bf16[96,1152]{1,0:T(8,128)(2,1)}, u32[]{:S(2)}, u32[]{:S(2)}) collective-permute-start(bf16[96,1152]{1,0:T(8,128)(2,1)S(1)} %get-tuple-element.30), channel_id=1, source_target_pairs={{14,0},{1023,1},{4,2},{1013,3},{18,4},{3,5},{8,6},{1017,7},{22,8},... | collective-permute-start | bytes 663560 | tf_op jit(solution)/shard_map/ppermute | solution.py:21
  40.8 17.7 %collective-permute-start.4 = (bf16[96,1152]{1,0:T(8,128)(2,1)S(1)}, bf16[96,1152]{1,0:T(8,128)(2,1)}, u32[]{:S(2)}, u32[]{:S(2)}) collective-permute-start(bf16[96,1152]{1,0:T(8,128)(2,1)S(1)} %get-tuple-element.31.own_half), channel_id=1, source_target_pairs={{14,0},{1023,1},{4,2},{1013,3},{18,4},{3,5},{8,6},{1017,7},{22,8},... | collective-permute-start | bytes 663560 | tf_op jit(solution)/shard_map/ppermute | solution.py:21
  52.7 18.0 %collective-permute-start.5 = (bf16[96,1152]{1,0:T(8,128)(2,1)}, bf16[96,1152]{1,0:T(8,128)(2,1)}, u32[]{:S(2)}, u32[]{:S(2)}) collective-permute-start(bf16[96,1152]{1,0:T(8,128)(2,1)} %collective-permute-done.3.refs_0_), channel_id=1, source_target_pairs={{1020,0},{1021,1},{6,2},{7,3},{0,4},{1,5},{10,6},{11,7},{4,8},{5,9... | collective-permute-start | bytes 663560 | tf_op jit(solution)/shard_map/ppermute | solution.py:21
  54.6 18.1 %collective-permute-start.6 = (bf16[96,1152]{1,0:T(8,128)(2,1)S(1)}, bf16[96,1152]{1,0:T(8,128)(2,1)}, u32[]{:S(2)}, u32[]{:S(2)}) collective-permute-start(bf16[96,1152]{1,0:T(8,128)(2,1)S(1)} %get-tuple-element.31.own_half), channel_id=1, source_target_pairs={{16,0},{1009,1},{18,2},{1011,3},{20,4},{1013,5},{22,6},{1015,7},{2... | collective-permute-start | bytes 663560 | tf_op jit(solution)/shard_map/ppermute | solution.py:21
  56.6 16.2 %collective-permute-start.7 = (bf16[96,1152]{1,0:T(8,128)(2,1)}, bf16[96,1152]{1,0:T(8,128)(2,1)}, u32[]{:S(2)}, u32[]{:S(2)}) collective-permute-start(bf16[96,1152]{1,0:T(8,128)(2,1)} %collective-permute-done.3.refs_0_), channel_id=1, source_target_pairs={{16,0},{1009,1},{18,2},{1011,3},{20,4},{1013,5},{22,6},{1015,7},{2... | collective-permute-start | bytes 663560 | tf_op jit(solution)/shard_map/ppermute | solution.py:21
  58.5 16.3 %collective-permute-start.8 = (bf16[96,1152]{1,0:T(8,128)(2,1)}, bf16[96,1152]{1,0:T(8,128)(2,1)}, u32[]{:S(2)}, u32[]{:S(2)}) collective-permute-start(bf16[96,1152]{1,0:T(8,128)(2,1)} %collective-permute-done.4.refs_1_), channel_id=1, source_target_pairs={{16,0},{1009,1},{18,2},{1011,3},{20,4},{1013,5},{22,6},{1015,7},{2... | collective-permute-start | bytes 663560 | tf_op jit(solution)/shard_map/ppermute | solution.py:21
  70.7 10.3 %collective-permute-start.9 = (bf16[96,1152]{1,0:T(8,128)(2,1)}, bf16[96,1152]{1,0:T(8,128)(2,1)}, u32[]{:S(2)}, u32[]{:S(2)}) collective-permute-start(bf16[96,1152]{1,0:T(8,128)(2,1)} %collective-permute-done.5.refs_2_), channel_id=1, source_target_pairs={{16,0},{1009,1},{18,2},{1011,3},{20,4},{1013,5},{22,6},{1015,7},{2... | collective-permute-start | bytes 663560 | tf_op jit(solution)/shard_map/ppermute | solution.py:21
  77.4 7.5 %copy-start.4 = (bf16[192,288]{1,0:T(8,128)(2,1)S(1)}, bf16[192,288]{1,0:T(8,128)(2,1)}, u32[]{:S(2)}) copy-start(bf16[192,288]{1,0:T(8,128)(2,1)} %copy-done.3) | copy-start | bytes 331780
  77.4 14.0 %copy-start.2 = (bf16[192,288]{1,0:T(8,128)(2,1)S(1)}, bf16[192,288]{1,0:T(8,128)(2,1)}, u32[]{:S(2)}) copy-start(bf16[192,288]{1,0:T(8,128)(2,1)} %copy-done.1) | copy-start | bytes 331780
  83.0 8.5 %collective-permute-start.10 = (bf16[896,128]{1,0:T(8,128)(2,1)S(1)}, bf16[896,128]{1,0:T(8,128)(2,1)S(1)}, u32[]{:S(2)}, u32[]{:S(2)}) collective-permute-start(bf16[896,128]{1,0:T(8,128)(2,1)S(1)} %get-tuple-element.36), channel_id=1, source_target_pairs={{2,0},{3,1},{0,2},{1,3},{6,4},{7,5},{4,6},{5,7},{10,8},{11,9},{8,1... | collective-permute-start | bytes 688136 | tf_op jit(solution)/shard_map/ppermute | solution.py:21
  84.9 3.5 %collective-permute-start.11 = (bf16[192,288]{1,0:T(8,128)(2,1)S(1)}, bf16[192,288]{1,0:T(8,128)(2,1)S(1)}, u32[]{:S(2)}, u32[]{:S(2)}) collective-permute-start(bf16[192,288]{1,0:T(8,128)(2,1)S(1)} %copy-done.4), channel_id=1, source_target_pairs={{1,0},{0,1},{3,2},{2,3},{5,4},{4,5},{7,6},{6,7},{9,8},{8,9},{11,10... | collective-permute-start | bytes 331784 | tf_op jit(solution)/shard_map/ppermute | solution.py:21
  93.5 8.8 %collective-permute-start.12 = (bf16[432,128]{1,0:T(8,128)(2,1)S(1)}, bf16[432,128]{1,0:T(8,128)(2,1)S(1)}, u32[]{:S(2)}, u32[]{:S(2)}) collective-permute-start(bf16[432,128]{1,0:T(8,128)(2,1)S(1)} %get-tuple-element.40), channel_id=1, source_target_pairs={{2,0},{3,1},{0,2},{1,3},{6,4},{7,5},{4,6},{5,7},{10,8},{11,9},{8,1... | collective-permute-start | bytes 331784 | tf_op jit(solution)/shard_map/ppermute | solution.py:21
  95.7 7.9 %collective-permute-start.13 = (bf16[432,128]{1,0:T(8,128)(2,1)S(1)}, bf16[432,128]{1,0:T(8,128)(2,1)S(1)}, u32[]{:S(2)}, u32[]{:S(2)}) collective-permute-start(bf16[432,128]{1,0:T(8,128)(2,1)S(1)} %get-tuple-element.41), channel_id=1, source_target_pairs={{3,0},{2,1},{1,2},{0,3},{7,4},{6,5},{5,6},{4,7},{11,8},{10,9},{9,1... | collective-permute-start | bytes 331784 | tf_op jit(solution)/shard_map/ppermute | solution.py:21
  100.4 3.3 %collective-permute-start.14 = (bf16[432,128]{1,0:T(8,128)(2,1)S(1)}, bf16[432,128]{1,0:T(8,128)(2,1)S(1)}, u32[]{:S(2)}, u32[]{:S(2)}) collective-permute-start(bf16[432,128]{1,0:T(8,128)(2,1)S(1)} %get-tuple-element.42), channel_id=1, source_target_pairs={{1,0},{0,1},{3,2},{2,3},{5,4},{4,5},{7,6},{6,7},{9,8},{8,9},{11,10... | collective-permute-start | bytes 331784 | tf_op jit(solution)/shard_map/ppermute | solution.py:21

commit v3 on v2

--- a/solution.py
+++ b/solution.py
@@ -43,6 +43,11 @@
 
 def cross_swap(n, t):
     return (n, t ^ 3)
+
+
+def position():
+    t = lax.axis_index("tensor")
+    return lax.rem(t, 2), lax.div(t, 2)
 
 
 def call(kernel, outs, *operands, scratch=(), flops=0):
@@ -103,9 +108,10 @@
     )
 
 
-def unit_parts(place, img, txt, own, fixed, moving, rest_mine, rest_theirs):
+def unit_parts(img, txt, own, fixed, moving, rest_mine, rest_theirs):
+    core, chip = position()
     rows, span = img.shape
-    core0 = place[0] == 0
+    core0 = core == 0
     a, b = img[...], txt[...]
     keep, travel = jnp.where(core0, a, b), jnp.where(core0, b, a)
     keep_low, travel_low = keep.astype(BF16), travel.astype(BF16)
@@ -117,9 +123,10 @@
     pack(own, packed_rows(rows, span), travel_low)
 
 
-def pair_up(place, fixed, moving, got, pair):
+def pair_up(fixed, moving, got, pair):
+    core, chip = position()
     rows, span = fixed.shape
-    chip0 = place[1] == 0
+    chip0 = chip == 0
     second = packed_rows(rows, span)
     for i, ref in enumerate((fixed, moving)):
         own, other = ref[...], unpack(got, i * second, rows, span)
@@ -127,34 +134,44 @@
         pair[i * rows : (i + 1) * rows, :] = beside([first, last], 1)
 
 
-def whole_width(place, pair, peer, fixed, own_half, other_half):
+def widened(mine, theirs):
+    span = mine.shape[1] // 2
+    cut = span // LANES * LANES
+    end = cut + span
+    return jnp.concatenate(
+        [mine[:, :cut], theirs[:, :cut], mine[:, cut : 2 * cut], theirs[:, cut : 2 * cut]]
+        + [mine[:, 2 * cut : end], theirs[:, 2 * cut : end], mine[:, end:], theirs[:, end:]],
+        axis=1,
+    )
+
+
+def wide_half(own, pair, peer, out):
+    half = out.shape[0]
+    rows = 2 * half
+    _, chip = position()
+    for first in (True, False):
+
+        @pl.when((chip == 0) == (first == own))
+        def _(first=first):
+            at = 0 if first else half
+            mine, theirs = pair[rows + at : rows + at + half, :], peer[at : at + half, :]
+            out[...] = widened(mine, theirs)
+
+
+def relayed_half(pair, peer, other_half):
+    wide_half(False, pair, peer, other_half)
+
+
+def fixed_and_half(pair, peer, fixed, own_half):
     rows = fixed.shape[0]
-    half = rows // 2
-    span = pair.shape[1] // 2
-    cut = span // LANES * LANES
-    chip0 = place[1] == 0
-
-    def widened(i):
-        mine = pair[i * rows : (i + 1) * rows, :]
-        theirs = peer[(1 - i) * rows : (2 - i) * rows, :]
-        end = cut + span
-        return jnp.concatenate(
-            [mine[:, :cut], theirs[:, :cut], mine[:, cut : 2 * cut], theirs[:, cut : 2 * cut]]
-            + [mine[:, 2 * cut : end], theirs[:, 2 * cut : end], mine[:, end:], theirs[:, end:]],
-            axis=1,
-        )
-
-    fixed[...] = widened(0)
-    moving = widened(1)
-    top, bottom = moving[:half], moving[half:]
-    own_half[...] = jnp.where(chip0, top, bottom)
-    other_half[...] = jnp.where(chip0, bottom, top)
+    fixed[...] = widened(pair[:rows, :], peer[rows:, :])
+    wide_half(True, pair, peer, own_half)
 
 
 def pull(factors, fixed, block, sign=None):
-    logits = factors[0] * lax.dot_general(
+    logits = factors[0:1, 0:1] * lax.dot_general(
         fixed, block, BY_COLUMNS, preferred_element_type=F32
-    ) + factors[1]
+    ) + factors[1:2, 0:1]
     if sign is None:
         weight = 16.0 * jax.nn.sigmoid(logits)
     else:
@@ -176,15 +193,16 @@
     return lax.broadcasted_iota(jnp.int32, shape, 0) == lax.broadcasted_iota(jnp.int32, shape, 1)
 
 
-def last_sum(place, factors, fixed, before, far_opposite, inv, keep, inner_kept, give):
+def last_sum(factors, fixed, before, far_opposite, inv, keep, inner_kept, give):
+    core, chip = position()
     rows, width = fixed.shape
     span = width // 4
     cut = span // LANES * LANES
-    chip0 = place[1] == 0
+    chip0 = chip == 0
     a = fixed[...]
     total = before[...] + pull(factors, a, far_opposite[...])
     unit = a.astype(F32)
-    by_row = factors[0] * inv[...]
+    by_row = factors[0:1, 0:1] * inv[...]
     inner = jnp.sum(unit * total, axis=1, keepdims=True) * by_row
     across = total * by_row - unit * inner
     middle = 4 * cut + 2 * (span - cut)
@@ -213,8 +231,9 @@
 
 
 def through_matrix(
-    place, kept, inner_kept, got, rest_mine, rest_peer, mine, peer, to_chip, to_cross, to_core, keep, stacked
+    kept, inner_kept, got, rest_mine, rest_peer, mine, peer, to_chip, to_cross, to_core, keep, stacked
 ):
+    core, chip = position()
     rows, width = kept.shape
     span = width // 2
     finish_sum(kept, inner_kept, got, rest_mine, rest_peer, stacked)
@@ -224,7 +243,7 @@
     spans = [part[:, u * span : (u + 1) * span] for u in range(4)]
     for t in range(4):
 
-        @pl.when(2 * place[1] + place[0] == t)
+        @pl.when(2 * chip + core == t)
         def _(t=t):
             pack(to_chip, 0, spans[t ^ 2].astype(BF16))
             pack(to_cross, 0, spans[t ^ 3].astype(BF16))
@@ -232,9 +251,10 @@
             keep[...] = spans[t]
 
 
-def last_add(place, from_chip, from_cross, from_core, kept, img, txt):
+def last_add(from_chip, from_cross, from_core, kept, img, txt):
+    core, chip = position()
     rows, span = kept.shape
-    core0 = place[0] == 0
+    core0 = core == 0
     mine = kept[...] + unpack(from_chip, 0, rows, span).astype(F32)
     theirs = unpack(from_core, 0, rows, span).astype(F32)
     theirs = theirs + unpack(from_cross, 0, rows, span).astype(F32)
@@ -259,8 +279,8 @@
     t = lax.axis_index("tensor")
     core0 = t % 2 == 0
     chip0 = t < 2
-    place = jnp.stack([t % 2, t // 2]).astype(jnp.int32)
     factors = jnp.concatenate([sharpness_factor, offset_term])
+    factors = jnp.broadcast_to(factors[:, None], (2, LANES))
 
     img_emb = jnp.dot(
         picture_averaged_vectors, picture_mapping_matrix, preferred_element_type=F32
@@ -279,7 +299,6 @@
     own, fixed_own, moving_own, rest_mine, rest_theirs = call(
         unit_parts,
         [((2 * packed_rows(rows, span), LANES), BF16)] + [piece] * 4,
-        place,
         img_unit,
         txt_unit,
     )
@@ -291,17 +310,13 @@
     matrix_mine = jnp.where(core0, img_matrix, txt_matrix)
     matrix_theirs = jnp.where(core0, txt_matrix, img_matrix)
     matrix_peer = exchange(matrix_theirs, groups, core_swap)
-    (pair,) = call(pair_up, [((2 * rows, 2 * span), BF16)], place, fixed_own, moving_own, other)
+    (pair,) = call(pair_up, [((2 * rows, 2 * span), BF16)], fixed_own, moving_own, other)
     peer = exchange(pair, groups, core_swap)
     peer, matrix_peer = lax.optimization_barrier((peer, matrix_peer))
-    fixed, own_half, other_half = call(
-        whole_width,
-        [((rows, width), BF16), ((half, width), BF16), ((half, width), BF16)],
-        place,
-        pair,
-        peer,
-    )
-
+    half_width = ((half, width), BF16)
+    (other_half,) = call(relayed_half, [half_width], pair, peer)
+    pair, peer, other_half = lax.optimization_barrier((pair, peer, other_half))
+    fixed, own_half = call(fixed_and_half, [((rows, width), BF16), half_width], pair, peer)
     inv_fixed = jnp.where(core0, inv_img, inv_txt)[:, None]
 
     first_row = lax.axis_index("dp") * rows
@@ -336,7 +351,6 @@
             ((rows, 1), F32),
             ((packed_rows(rows, 2 * span) + 32, LANES), BF16),
         ],
-        place,
         factors,
         fixed,
         total,
@@ -349,7 +363,6 @@
     to_chip, to_cross, to_core, keep = call(
         through_matrix,
         [sent, sent, sent, part],
-        place,
         keep,
         inner_kept,
         got,
@@ -362,7 +375,7 @@
     from_chip = exchange(to_chip, groups, chip_swap)
     from_cross = exchange(to_cross, groups, cross_swap)
     from_core = exchange(to_core, groups, core_swap)
-    return tuple(call(last_add, [part, part], place, from_chip, from_cross, from_core, keep))
+    return tuple(call(last_add, [part, part], from_chip, from_cross, from_core, keep))
 
 
 def solution(mesh):

time: 106 us -> 102 us (0.962)
  waiting for transfers between devices: 32 us -> 24.9 us
  starting transfers between devices: 34.7 us -> 39 us
  Pallas kernels: 11.3 us -> 9.75 us
    ppermute x15, waiting for transfers between devices: 32 us -> 24.9 us  [exchange(): return lax.ppermute(block, AXES, route)]
    ppermute x15, starting transfers between devices: 34.7 us -> 39 us  [exchange(): return lax.ppermute(block, AXES, route)]
    pallas_call x8 -> x9, Pallas kernels: 11.3 us -> 9.75 us  [call(): pl.pallas_call(kernel, cost_estimate=pl.CostEstimate(flops=flops, bytes_a...]
  transfers between devices with their start and end apart: 15 -> 15, of which waited for: 9 -> 10; matrix products, arithmetic and copies ran while one was open for 1% -> 1% of each run, Pallas kernels for 4% -> 5%
where the time goes in v3:
time: 102 us; the launch traced here: 101 us
  starting transfers between devices  39 us (38%)
  waiting for transfers between devices  24.9 us (24%)
  blocking collectives  19.1 us (19%)
  Pallas kernels  9.75 us (10%)
  local copies, waits for them, and re-layouts  2.54 us (2%)
  matrix products  2.28 us (2%)
  between operations  2.21 us (2%)
  other arithmetic  1.53 us (2%)
    ppermute x15, starting transfers between devices, exchange(): return lax.ppermute(block, AXES, route)  39 us
    ppermute x15, waiting for transfers between devices, exchange(): return lax.ppermute(block, AXES, route)  24.9 us
    psum x1, blocking collectives, shards(): inv = lax.rsqrt(lax.psum(squares, 'tensor') + 1e-06)  19.1 us
    pallas_call x9, Pallas kernels, call(): pl.pallas_call(kernel, cost_estimate=pl.CostEstimate(flops=flops, bytes_a...  9.75 us
    unnamed x18, local copies, waits for them, and re-layouts  2.36 us
  transfers between devices with their start and end apart: 15, of which 10 were waited for; matrix products, arithmetic and copies ran while one was open for 1% of the time, Pallas kernels for 5%

profile of v3, /device:TPU:1, one launch (start us, length us, event | category | flops | bytes accessed | tf_op | source)
XLA Modules:
  0.0 101.3 jit_solution(7832727023460911787)
XLA Ops:
  0.7 1.0 copy-done
  1.7 1.7 %multiply_reduce_fusion = (f32[192]{0:T(256)S(1)}, f32[192,288]{1,0:T(8,128)S(1)}) fusion(bf16[192,1152]{1,0:T(8,128)(2,1)S(1)} %copy-done, bf16[1152,288]{0,1:T(8,128)(2,1)} %param.10), kind=kOutput, calls=%fused_computation.2 | convolution fusion | flops 127512384 | bytes 1327872 | tf_op jit(solution)/shard_map/dot_general | solution.py:288
  4.0 19.1 %psum.7 = f32[384]{0:T(512)S(1)} all-reduce(f32[384]{0:T(512)S(1)} %pad_maximum_fusion), channel_id=1, replica_groups=mesh['dp'=256,'tensor'=4] {'tensor'}, use_global_device_ids=true, to_apply=%region_2.3 | all-reduce | flops 384 | bytes 3072 | tf_op jit(solution)/shard_map/psum | solution.py:294
  24.2 2.0 %collective-permute-start = (bf16[864,128]{1,0:T(8,128)(2,1)S(1)}, bf16[864,128]{1,0:T(8,128)(2,1)S(1)}, u32[]{:S(2)}, u32[]{:S(2)}) collective-permute-start(bf16[864,128]{1,0:T(8,128)(2,1)S(1)} %get-tuple-element.27), channel_id=1, source_target_pairs={{2,0},{3,1},{0,2},{1,3},{6,4},{7,5},{4,6},{5,7},{10,8},{11,9},{8,1... | collective-permute-start | bytes 663560 | tf_op jit(solution)/shard_map/ppermute | solution.py:21
  26.3 1.0 broadcast_select_fusion
  27.2 2.5 %collective-permute-start.2 = (bf16[288,1152]{1,0:T(8,128)(2,1)}, bf16[288,1152]{1,0:T(8,128)(2,1)S(1)}, u32[]{:S(2)}, u32[]{:S(2)}) collective-permute-start(bf16[288,1152]{1,0:T(8,128)(2,1)} %get-tuple-element.49), channel_id=1, source_target_pairs={{1,0},{0,1},{3,2},{2,3},{5,4},{4,5},{7,6},{6,7},{9,8},{8,9},{11,10... | collective-permute-start | bytes 1990664 | tf_op jit(solution)/shard_map/ppermute | solution.py:21
  31.1 1.2 %collective-permute-done.got = bf16[864,128]{1,0:T(8,128)(2,1)S(1)} collective-permute-done((bf16[864,128]{1,0:T(8,128)(2,1)S(1)}, bf16[864,128]{1,0:T(8,128)(2,1)S(1)}, u32[]{:S(2)}, u32[]{:S(2)}) %collective-permute-start) | collective-permute-done | bytes 221216 | tf_op jit(solution)/shard_map/ppermute | solution.py:21
  32.5 3.5 %collective-permute-start.1 = (bf16[384,576]{1,0:T(8,128)(2,1)S(1)}, bf16[384,576]{1,0:T(8,128)(2,1)S(1)}, u32[]{:S(2)}, u32[]{:S(2)}) collective-permute-start(bf16[384,576]{1,0:T(8,128)(2,1)S(1)} %shard_map.87.pair), channel_id=1, source_target_pairs={{1,0},{0,1},{3,2},{2,3},{5,4},{4,5},{7,6},{6,7},{9,8},{8,9},{11,10... | collective-permute-start | bytes 1327112 | tf_op jit(solution)/shard_map/ppermute | solution.py:21
  37.6 1.9 %collective-permute-start.3 = (bf16[96,1152]{1,0:T(8,128)(2,1)S(1)}, bf16[96,1152]{1,0:T(8,128)(2,1)S(1)}, u32[]{:S(2)}, u32[]{:S(2)}) collective-permute-start(bf16[96,1152]{1,0:T(8,128)(2,1)S(1)} %shard_map.88), channel_id=1, source_target_pairs={{14,0},{1023,1},{4,2},{1013,3},{18,4},{3,5},{8,6},{1017,7},{22,8},... | collective-permute-start | bytes 663560 | tf_op jit(solution)/shard_map/ppermute | solution.py:21
  40.5 1.9 %collective-permute-start.4 = (bf16[96,1152]{1,0:T(8,128)(2,1)}, bf16[96,1152]{1,0:T(8,128)(2,1)}, u32[]{:S(2)}, u32[]{:S(2)}) collective-permute-start(bf16[96,1152]{1,0:T(8,128)(2,1)} %get-tuple-element.35.own_half), channel_id=1, source_target_pairs={{14,0},{1023,1},{4,2},{1013,3},{18,4},{3,5},{8,6},{1017,7},{22,8},... | collective-permute-start | bytes 663560 | tf_op jit(solution)/shard_map/ppermute | solution.py:21
  42.5 1.6 %shard_map.90.before = f32[192,1152]{1,0:T(8,128)S(1)} custom-call(f32[2,128]{1,0:T(2,128)S(1)} %broadcast_in_dim.10.factors, bf16[192,1152]{1,0:T(8,128)(2,1)S(1)} %get-tuple-element.33.fixed, f32[192,96]{1,0:T(8,128)S(1)} %select_select_fusion.sign, bf16[96,1152]{1,0:T(8,128)(2,1)} %get-tuple-element.35.own_half), custom_call_target="tpu_custom_call" | custom-call | bytes 738304 | tf_op jit(solution)/shard_map/pallas_call | solution.py:58
  44.1 7.4 %collective-permute-done.3.refs_0_ = bf16[96,1152]{1,0:T(8,128)(2,1)S(1)} collective-permute-done((bf16[96,1152]{1,0:T(8,128)(2,1)S(1)}, bf16[96,1152]{1,0:T(8,128)(2,1)S(1)}, u32[]{:S(2)}, u32[]{:S(2)}) %collective-permute-start.3) | collective-permute-done | bytes 221216 | tf_op jit(solution)/shard_map/ppermute | solution.py:21
  51.5 1.9 %collective-permute-start.5 = (bf16[96,1152]{1,0:T(8,128)(2,1)S(1)}, bf16[96,1152]{1,0:T(8,128)(2,1)}, u32[]{:S(2)}, u32[]{:S(2)}) collective-permute-start(bf16[96,1152]{1,0:T(8,128)(2,1)S(1)} %collective-permute-done.3.refs_0_), channel_id=1, source_target_pairs={{1020,0},{1021,1},{6,2},{7,3},{0,4},{1,5},{10,6},{11,7},{4,8},{5,9... | collective-permute-start | bytes 663560 | tf_op jit(solution)/shard_map/ppermute | solution.py:21
  53.4 1.9 %collective-permute-start.6 = (bf16[96,1152]{1,0:T(8,128)(2,1)}, bf16[96,1152]{1,0:T(8,128)(2,1)}, u32[]{:S(2)}, u32[]{:S(2)}) collective-permute-start(bf16[96,1152]{1,0:T(8,128)(2,1)} %get-tuple-element.35.own_half), channel_id=1, source_target_pairs={{16,0},{1009,1},{18,2},{1011,3},{20,4},{1013,5},{22,6},{1015,7},{2... | collective-permute-start | bytes 663560 | tf_op jit(solution)/shard_map/ppermute | solution.py:21
  55.3 1.9 %collective-permute-start.7 = (bf16[96,1152]{1,0:T(8,128)(2,1)S(1)}, bf16[96,1152]{1,0:T(8,128)(2,1)}, u32[]{:S(2)}, u32[]{:S(2)}) collective-permute-start(bf16[96,1152]{1,0:T(8,128)(2,1)S(1)} %collective-permute-done.3.refs_0_), channel_id=1, source_target_pairs={{16,0},{1009,1},{18,2},{1011,3},{20,4},{1013,5},{22,6},{1015,7},{2... | collective-permute-start | bytes 663560 | tf_op jit(solution)/shard_map/ppermute | solution.py:21
  57.2 1.9 %collective-permute-start.8 = (bf16[96,1152]{1,0:T(8,128)(2,1)}, bf16[96,1152]{1,0:T(8,128)(2,1)}, u32[]{:S(2)}, u32[]{:S(2)}) collective-permute-start(bf16[96,1152]{1,0:T(8,128)(2,1)} %collective-permute-done.4.refs_1_), channel_id=1, source_target_pairs={{16,0},{1009,1},{18,2},{1011,3},{20,4},{1013,5},{22,6},{1015,7},{2... | collective-permute-start | bytes 663560 | tf_op jit(solution)/shard_map/ppermute | solution.py:21
  59.2 7.7 %collective-permute-done.5.refs_2_ = bf16[96,1152]{1,0:T(8,128)(2,1)} collective-permute-done((bf16[96,1152]{1,0:T(8,128)(2,1)S(1)}, bf16[96,1152]{1,0:T(8,128)(2,1)}, u32[]{:S(2)}, u32[]{:S(2)}) %collective-permute-start.5) | collective-permute-done | bytes 221216 | tf_op jit(solution)/shard_map/ppermute | solution.py:21
  66.9 1.9 %collective-permute-start.9 = (bf16[96,1152]{1,0:T(8,128)(2,1)}, bf16[96,1152]{1,0:T(8,128)(2,1)}, u32[]{:S(2)}, u32[]{:S(2)}) collective-permute-start(bf16[96,1152]{1,0:T(8,128)(2,1)} %collective-permute-done.5.refs_2_), channel_id=1, source_target_pairs={{16,0},{1009,1},{18,2},{1011,3},{20,4},{1013,5},{22,6},{1015,7},{2... | collective-permute-start | bytes 663560 | tf_op jit(solution)/shard_map/ppermute | solution.py:21
  68.9 1.0 %collective-permute-done.7.refs_4_ = bf16[96,1152]{1,0:T(8,128)(2,1)} collective-permute-done((bf16[96,1152]{1,0:T(8,128)(2,1)S(1)}, bf16[96,1152]{1,0:T(8,128)(2,1)}, u32[]{:S(2)}, u32[]{:S(2)}) %collective-permute-start.7) | collective-permute-done | bytes 221216 | tf_op jit(solution)/shard_map/ppermute | solution.py:21
  70.0 3.2 %collective-permute-done.8.refs_5_ = bf16[96,1152]{1,0:T(8,128)(2,1)} collective-permute-done((bf16[96,1152]{1,0:T(8,128)(2,1)}, bf16[96,1152]{1,0:T(8,128)(2,1)}, u32[]{:S(2)}, u32[]{:S(2)}) %collective-permute-start.8) | collective-permute-done | bytes 221216 | tf_op jit(solution)/shard_map/ppermute | solution.py:21
  73.2 2.5 %shard_map.91.before = f32[192,1152]{1,0:T(8,128)S(1)} custom-call(f32[2,128]{1,0:T(2,128)S(1)} %broadcast_in_dim.10.factors, bf16[192,1152]{1,0:T(8,128)(2,1)S(1)} %get-tuple-element.33.fixed, f32[192,1152]{1,0:T(8,128)S(1)} %shard_map.90.before, bf16[96,1152]{1,0:T(8,128)(2,1)S(1)} %collective-permute-done.3.refs_0_, ...), custom_call_target="tpu_custom_call" | custom-call | bytes 2655232 | tf_op jit(solution)/shard_map/pallas_call | solution.py:58
  75.7 1.5 %collective-permute-done.9.far_opposite = bf16[96,1152]{1,0:T(8,128)(2,1)} collective-permute-done((bf16[96,1152]{1,0:T(8,128)(2,1)}, bf16[96,1152]{1,0:T(8,128)(2,1)}, u32[]{:S(2)}, u32[]{:S(2)}) %collective-permute-start.9) | collective-permute-done | bytes 221216 | tf_op jit(solution)/shard_map/ppermute | solution.py:21
  77.2 2.0 %shard_map.92 = (f32[192,576]{1,0:T(8,128)S(1)}, f32[192,1]{1,0:T(8,128)S(1)}, bf16[896,128]{1,0:T(8,128)(2,1)S(1)}) custom-call(f32[2,128]{1,0:T(2,128)S(1)} %broadcast_in_dim.10.factors, bf16[192,1152]{1,0:T(8,128)(2,1)S(1)} %get-tuple-element.33.fixed, f32[192,1152]{1,0:T(8,128)S(1)} %shard_map.91.before, ...), custom_call_target="tpu_custom_call" | custom-call | bytes 1550080 | tf_op jit(solution)/shard_map/pallas_call | solution.py:58
  79.2 1.9 %collective-permute-start.10 = (bf16[896,128]{1,0:T(8,128)(2,1)S(1)}, bf16[896,128]{1,0:T(8,128)(2,1)S(1)}, u32[]{:S(2)}, u32[]{:S(2)}) collective-permute-start(bf16[896,128]{1,0:T(8,128)(2,1)S(1)} %get-tuple-element.40), channel_id=1, source_target_pairs={{2,0},{3,1},{0,2},{1,3},{6,4},{7,5},{4,6},{5,7},{10,8},{11,9},{8,1... | collective-permute-start | bytes 688136 | tf_op jit(solution)/shard_map/ppermute | solution.py:21
  81.1 5.1 %collective-permute-start.11 = (bf16[192,288]{1,0:T(8,128)(2,1)S(1)}, bf16[192,288]{1,0:T(8,128)(2,1)S(1)}, u32[]{:S(2)}, u32[]{:S(2)}) collective-permute-start(bf16[192,288]{1,0:T(8,128)(2,1)S(1)} %copy-done.4), channel_id=1, source_target_pairs={{1,0},{0,1},{3,2},{2,3},{5,4},{4,5},{7,6},{6,7},{9,8},{8,9},{11,10... | collective-permute-start | bytes 331784 | tf_op jit(solution)/shard_map/ppermute | solution.py:21
  86.2 1.0 collective-permute-done.11.rest_peer
  87.2 1.5 %shard_map.93 = (bf16[432,128]{1,0:T(8,128)(2,1)S(1)}, bf16[432,128]{1,0:T(8,128)(2,1)S(1)}, bf16[432,128]{1,0:T(8,128)(2,1)S(1)}, f32[192,288]{1,0:T(8,128)S(1)}) custom-call(f32[192,576]{1,0:T(8,128)S(1)} %get-tuple-element.38.kept, f32[192,1]{1,0:T(8,128)S(1)} %get-tuple-element.39.inner_kept, bf16[896,128]{1,0:T(8,128)(2,1)S(1)} %collective-permute-done.10.got, ...), custom_call_target="tpu_custom_call" | custom-call | bytes 2220800 | tf_op jit(solution)/shard_map/pallas_call | solution.py:58
  88.7 3.6 %collective-permute-start.12 = (bf16[432,128]{1,0:T(8,128)(2,1)S(1)}, bf16[432,128]{1,0:T(8,128)(2,1)S(1)}, u32[]{:S(2)}, u32[]{:S(2)}) collective-permute-start(bf16[432,128]{1,0:T(8,128)(2,1)S(1)} %get-tuple-element.44), channel_id=1, source_target_pairs={{2,0},{3,1},{0,2},{1,3},{6,4},{7,5},{4,6},{5,7},{10,8},{11,9},{8,1... | collective-permute-start | bytes 331784 | tf_op jit(solution)/shard_map/ppermute | solution.py:21
  92.3 4.9 %collective-permute-start.13 = (bf16[432,128]{1,0:T(8,128)(2,1)S(1)}, bf16[432,128]{1,0:T(8,128)(2,1)S(1)}, u32[]{:S(2)}, u32[]{:S(2)}) collective-permute-start(bf16[432,128]{1,0:T(8,128)(2,1)S(1)} %get-tuple-element.45), channel_id=1, source_target_pairs={{3,0},{2,1},{1,2},{0,3},{7,4},{6,5},{5,6},{4,7},{11,8},{10,9},{9,1... | collective-permute-start | bytes 331784 | tf_op jit(solution)/shard_map/ppermute | solution.py:21
  97.2 1.9 %collective-permute-start.14 = (bf16[432,128]{1,0:T(8,128)(2,1)S(1)}, bf16[432,128]{1,0:T(8,128)(2,1)S(1)}, u32[]{:S(2)}, u32[]{:S(2)}) collective-permute-start(bf16[432,128]{1,0:T(8,128)(2,1)S(1)} %get-tuple-element.46), channel_id=1, source_target_pairs={{1,0},{0,1},{3,2},{2,3},{5,4},{4,5},{7,6},{6,7},{9,8},{8,9},{11,10... | collective-permute-start | bytes 331784 | tf_op jit(solution)/shard_map/ppermute | solution.py:21
  99.2 1.1 %collective-permute-done.13.from_cross = bf16[432,128]{1,0:T(8,128)(2,1)S(1)} collective-permute-done((bf16[432,128]{1,0:T(8,128)(2,1)S(1)}, bf16[432,128]{1,0:T(8,128)(2,1)S(1)}, u32[]{:S(2)}, u32[]{:S(2)}) %collective-permute-start.13) | collective-permute-done | bytes 110624 | tf_op jit(solution)/shard_map/ppermute | solution.py:21
  100.4 0.9 shard_map.94
  (39 shorter events, 4.8 us)
Async XLA Ops:
  0.6 1.0 %copy-start = (bf16[192,1152]{1,0:T(8,128)(2,1)S(1)}, bf16[192,1152]{1,0:T(8,128)(2,1)}, u32[]{:S(2)}) copy-start(bf16[192,1152]{1,0:T(8,128)(2,1)} %param.9) | copy-start | bytes 1327108
  1.6 1.7 %copy-start.6 = (bf16[1152,288]{0,1:T(8,128)(2,1)S(1)}, bf16[1152,288]{0,1:T(8,128)(2,1)}, u32[]{:S(2)}) copy-start(bf16[1152,288]{0,1:T(8,128)(2,1)} %param.8) | copy-start | bytes 1990660
  1.7 1.7 %copy-start.7 = (bf16[192,1152]{1,0:T(8,128)(2,1)S(1)}, bf16[192,1152]{1,0:T(8,128)(2,1)}, u32[]{:S(2)}) copy-start(bf16[192,1152]{1,0:T(8,128)(2,1)} %param.7) | copy-start | bytes 1327108
  23.3 3.0 %copy-start.5 = (bf16[1152,288]{0,1:T(8,128)(2,1)S(1)}, bf16[1152,288]{0,1:T(8,128)(2,1)}, u32[]{:S(2)}) copy-start(bf16[1152,288]{0,1:T(8,128)(2,1)} %param.10) | copy-start | bytes 1990660
  23.6 0.7 copy-start.3
  24.2 3.0 %copy-start.1 = (bf16[192,288]{1,0:T(8,128)(2,1)}, bf16[192,288]{1,0:T(8,128)(2,1)S(1)}, u32[]{:S(2)}) copy-start(bf16[192,288]{1,0:T(8,128)(2,1)S(1)} %get-tuple-element.41.rest_mine) | copy-start | bytes 331780
  24.2 8.1 %collective-permute-start = (bf16[864,128]{1,0:T(8,128)(2,1)S(1)}, bf16[864,128]{1,0:T(8,128)(2,1)S(1)}, u32[]{:S(2)}, u32[]{:S(2)}) collective-permute-start(bf16[864,128]{1,0:T(8,128)(2,1)S(1)} %get-tuple-element.27), channel_id=1, source_target_pairs={{2,0},{3,1},{0,2},{1,3},{6,4},{7,5},{4,6},{5,7},{10,8},{11,9},{8,1... | collective-permute-start | bytes 663560 | tf_op jit(solution)/shard_map/ppermute | solution.py:21
  27.2 9.6 %collective-permute-start.2 = (bf16[288,1152]{1,0:T(8,128)(2,1)}, bf16[288,1152]{1,0:T(8,128)(2,1)S(1)}, u32[]{:S(2)}, u32[]{:S(2)}) collective-permute-start(bf16[288,1152]{1,0:T(8,128)(2,1)} %get-tuple-element.49), channel_id=1, source_target_pairs={{1,0},{0,1},{3,2},{2,3},{5,4},{4,5},{7,6},{6,7},{9,8},{8,9},{11,10... | collective-permute-start | bytes 1990664 | tf_op jit(solution)/shard_map/ppermute | solution.py:21
  32.5 5.0 %collective-permute-start.1 = (bf16[384,576]{1,0:T(8,128)(2,1)S(1)}, bf16[384,576]{1,0:T(8,128)(2,1)S(1)}, u32[]{:S(2)}, u32[]{:S(2)}) collective-permute-start(bf16[384,576]{1,0:T(8,128)(2,1)S(1)} %shard_map.87.pair), channel_id=1, source_target_pairs={{1,0},{0,1},{3,2},{2,3},{5,4},{4,5},{7,6},{6,7},{9,8},{8,9},{11,10... | collective-permute-start | bytes 1327112 | tf_op jit(solution)/shard_map/ppermute | solution.py:21
  36.1 0.7 copy-start.8
  37.6 13.8 %collective-permute-start.3 = (bf16[96,1152]{1,0:T(8,128)(2,1)S(1)}, bf16[96,1152]{1,0:T(8,128)(2,1)S(1)}, u32[]{:S(2)}, u32[]{:S(2)}) collective-permute-start(bf16[96,1152]{1,0:T(8,128)(2,1)S(1)} %shard_map.88), channel_id=1, source_target_pairs={{14,0},{1023,1},{4,2},{1013,3},{18,4},{3,5},{8,6},{1017,7},{22,8},... | collective-permute-start | bytes 663560 | tf_op jit(solution)/shard_map/ppermute | solution.py:21
  40.5 16.7 %collective-permute-start.4 = (bf16[96,1152]{1,0:T(8,128)(2,1)}, bf16[96,1152]{1,0:T(8,128)(2,1)}, u32[]{:S(2)}, u32[]{:S(2)}) collective-permute-start(bf16[96,1152]{1,0:T(8,128)(2,1)} %get-tuple-element.35.own_half), channel_id=1, source_target_pairs={{14,0},{1023,1},{4,2},{1013,3},{18,4},{3,5},{8,6},{1017,7},{22,8},... | collective-permute-start | bytes 663560 | tf_op jit(solution)/shard_map/ppermute | solution.py:21
  51.5 15.4 %collective-permute-start.5 = (bf16[96,1152]{1,0:T(8,128)(2,1)S(1)}, bf16[96,1152]{1,0:T(8,128)(2,1)}, u32[]{:S(2)}, u32[]{:S(2)}) collective-permute-start(bf16[96,1152]{1,0:T(8,128)(2,1)S(1)} %collective-permute-done.3.refs_0_), channel_id=1, source_target_pairs={{1020,0},{1021,1},{6,2},{7,3},{0,4},{1,5},{10,6},{11,7},{4,8},{5,9... | collective-permute-start | bytes 663560 | tf_op jit(solution)/shard_map/ppermute | solution.py:21
  53.4 15.6 %collective-permute-start.6 = (bf16[96,1152]{1,0:T(8,128)(2,1)}, bf16[96,1152]{1,0:T(8,128)(2,1)}, u32[]{:S(2)}, u32[]{:S(2)}) collective-permute-start(bf16[96,1152]{1,0:T(8,128)(2,1)} %get-tuple-element.35.own_half), channel_id=1, source_target_pairs={{16,0},{1009,1},{18,2},{1011,3},{20,4},{1013,5},{22,6},{1015,7},{2... | collective-permute-start | bytes 663560 | tf_op jit(solution)/shard_map/ppermute | solution.py:21
  55.3 14.7 %collective-permute-start.7 = (bf16[96,1152]{1,0:T(8,128)(2,1)S(1)}, bf16[96,1152]{1,0:T(8,128)(2,1)}, u32[]{:S(2)}, u32[]{:S(2)}) collective-permute-start(bf16[96,1152]{1,0:T(8,128)(2,1)S(1)} %collective-permute-done.3.refs_0_), channel_id=1, source_target_pairs={{16,0},{1009,1},{18,2},{1011,3},{20,4},{1013,5},{22,6},{1015,7},{2... | collective-permute-start | bytes 663560 | tf_op jit(solution)/shard_map/ppermute | solution.py:21
  57.2 15.9 %collective-permute-start.8 = (bf16[96,1152]{1,0:T(8,128)(2,1)}, bf16[96,1152]{1,0:T(8,128)(2,1)}, u32[]{:S(2)}, u32[]{:S(2)}) collective-permute-start(bf16[96,1152]{1,0:T(8,128)(2,1)} %collective-permute-done.4.refs_1_), channel_id=1, source_target_pairs={{16,0},{1009,1},{18,2},{1011,3},{20,4},{1013,5},{22,6},{1015,7},{2... | collective-permute-start | bytes 663560 | tf_op jit(solution)/shard_map/ppermute | solution.py:21
  66.9 10.3 %collective-permute-start.9 = (bf16[96,1152]{1,0:T(8,128)(2,1)}, bf16[96,1152]{1,0:T(8,128)(2,1)}, u32[]{:S(2)}, u32[]{:S(2)}) collective-permute-start(bf16[96,1152]{1,0:T(8,128)(2,1)} %collective-permute-done.5.refs_2_), channel_id=1, source_target_pairs={{16,0},{1009,1},{18,2},{1011,3},{20,4},{1013,5},{22,6},{1015,7},{2... | collective-permute-start | bytes 663560 | tf_op jit(solution)/shard_map/ppermute | solution.py:21
  75.7 5.4 %copy-start.4 = (bf16[192,288]{1,0:T(8,128)(2,1)S(1)}, bf16[192,288]{1,0:T(8,128)(2,1)}, u32[]{:S(2)}) copy-start(bf16[192,288]{1,0:T(8,128)(2,1)} %copy-done.3) | copy-start | bytes 331780
  75.7 11.5 %copy-start.2 = (bf16[192,288]{1,0:T(8,128)(2,1)S(1)}, bf16[192,288]{1,0:T(8,128)(2,1)}, u32[]{:S(2)}) copy-start(bf16[192,288]{1,0:T(8,128)(2,1)} %copy-done.1) | copy-start | bytes 331780
  79.2 8.1 %collective-permute-start.10 = (bf16[896,128]{1,0:T(8,128)(2,1)S(1)}, bf16[896,128]{1,0:T(8,128)(2,1)S(1)}, u32[]{:S(2)}, u32[]{:S(2)}) collective-permute-start(bf16[896,128]{1,0:T(8,128)(2,1)S(1)} %get-tuple-element.40), channel_id=1, source_target_pairs={{2,0},{3,1},{0,2},{1,3},{6,4},{7,5},{4,6},{5,7},{10,8},{11,9},{8,1... | collective-permute-start | bytes 688136 | tf_op jit(solution)/shard_map/ppermute | solution.py:21
  81.1 6.1 %collective-permute-start.11 = (bf16[192,288]{1,0:T(8,128)(2,1)S(1)}, bf16[192,288]{1,0:T(8,128)(2,1)S(1)}, u32[]{:S(2)}, u32[]{:S(2)}) collective-permute-start(bf16[192,288]{1,0:T(8,128)(2,1)S(1)} %copy-done.4), channel_id=1, source_target_pairs={{1,0},{0,1},{3,2},{2,3},{5,4},{4,5},{7,6},{6,7},{9,8},{8,9},{11,10... | collective-permute-start | bytes 331784 | tf_op jit(solution)/shard_map/ppermute | solution.py:21
  88.7 10.5 %collective-permute-start.12 = (bf16[432,128]{1,0:T(8,128)(2,1)S(1)}, bf16[432,128]{1,0:T(8,128)(2,1)S(1)}, u32[]{:S(2)}, u32[]{:S(2)}) collective-permute-start(bf16[432,128]{1,0:T(8,128)(2,1)S(1)} %get-tuple-element.44), channel_id=1, source_target_pairs={{2,0},{3,1},{0,2},{1,3},{6,4},{7,5},{4,6},{5,7},{10,8},{11,9},{8,1... | collective-permute-start | bytes 331784 | tf_op jit(solution)/shard_map/ppermute | solution.py:21
  92.3 7.9 %collective-permute-start.13 = (bf16[432,128]{1,0:T(8,128)(2,1)S(1)}, bf16[432,128]{1,0:T(8,128)(2,1)S(1)}, u32[]{:S(2)}, u32[]{:S(2)}) collective-permute-start(bf16[432,128]{1,0:T(8,128)(2,1)S(1)} %get-tuple-element.45), channel_id=1, source_target_pairs={{3,0},{2,1},{1,2},{0,3},{7,4},{6,5},{5,6},{4,7},{11,8},{10,9},{9,1... | collective-permute-start | bytes 331784 | tf_op jit(solution)/shard_map/ppermute | solution.py:21
  97.2 3.2 %collective-permute-start.14 = (bf16[432,128]{1,0:T(8,128)(2,1)S(1)}, bf16[432,128]{1,0:T(8,128)(2,1)S(1)}, u32[]{:S(2)}, u32[]{:S(2)}) collective-permute-start(bf16[432,128]{1,0:T(8,128)(2,1)S(1)} %get-tuple-element.46), channel_id=1, source_target_pairs={{1,0},{0,1},{3,2},{2,3},{5,4},{4,5},{7,6},{6,7},{9,8},{8,9},{11,10... | collective-permute-start | bytes 331784 | tf_op jit(solution)/shard_map/ppermute | solution.py:21

commit v4 on v3

--- a/solution.py
+++ b/solution.py
@@ -8,7 +8,8 @@
 AXES = ("dp", "tensor")
 ROUND = 4
 LANES = 128
-F32, BF16 = jnp.float32, jnp.bfloat16
+F32, F16, BF16 = jnp.float32, jnp.float16, jnp.bfloat16
+RAISED = 32.0
 BY_COLUMNS = (((1,), (1,)), ((), ()))
 
 
@@ -108,41 +109,45 @@
     )
 
 
-def unit_parts(img, txt, own, fixed, moving, rest_mine, rest_theirs):
-    core, chip = position()
+def embedded(img, txt, own, fixed, moving):
+    core, _ = position()
     rows, span = img.shape
-    core0 = core == 0
     a, b = img[...], txt[...]
-    keep, travel = jnp.where(core0, a, b), jnp.where(core0, b, a)
-    keep_low, travel_low = keep.astype(BF16), travel.astype(BF16)
-    fixed[...] = keep_low
-    moving[...] = travel_low
-    rest_mine[...] = (keep - keep_low.astype(F32)).astype(BF16)
-    rest_theirs[...] = (travel - travel_low.astype(F32)).astype(BF16)
-    pack(own, 0, keep_low)
-    pack(own, packed_rows(rows, span), travel_low)
+    keep = jnp.where(core == 0, a, b) * RAISED
+    travel = jnp.where(core == 0, b, a) * RAISED
+    fixed[...] = keep
+    moving[...] = travel
+    pack(own, 0, keep)
+    pack(own, packed_rows(rows, span), travel)
 
 
 def pair_up(fixed, moving, got, pair):
-    core, chip = position()
+    _, chip = position()
     rows, span = fixed.shape
-    chip0 = chip == 0
     second = packed_rows(rows, span)
     for i, ref in enumerate((fixed, moving)):
         own, other = ref[...], unpack(got, i * second, rows, span)
-        first, last = jnp.where(chip0, own, other), jnp.where(chip0, other, own)
-        pair[i * rows : (i + 1) * rows, :] = beside([first, last], 1)
-
-
-def widened(mine, theirs):
-    span = mine.shape[1] // 2
+        first, last = jnp.where(chip == 0, own, other), jnp.where(chip == 0, other, own)
+        fill = jnp.zeros((rows, pair.shape[1] - 2 * span), F32)
+        pair[i * rows : (i + 1) * rows, :] = jnp.concatenate(
+            [beside([first, last], 1), fill], axis=1
+        )
+
+
+def widened(mine, theirs, span):
     cut = span // LANES * LANES
-    end = cut + span
+    middle, end = cut + span, 2 * span
     return jnp.concatenate(
         [mine[:, :cut], theirs[:, :cut], mine[:, cut : 2 * cut], theirs[:, cut : 2 * cut]]
-        + [mine[:, 2 * cut : end], theirs[:, 2 * cut : end], mine[:, end:], theirs[:, end:]],
+        + [mine[:, 2 * cut : middle], theirs[:, 2 * cut : middle]]
+        + [mine[:, middle:end], theirs[:, middle:end]],
         axis=1,
     )
+
+
+def unit_rows(emb):
+    inv = lax.rsqrt(jnp.sum(emb * emb, axis=1, keepdims=True) + 1e-06 * RAISED**2)
+    return emb * inv, inv * RAISED
 
 
 def wide_half(own, pair, peer, out):
@@ -155,16 +160,19 @@
         def _(first=first):
             at = 0 if first else half
             mine, theirs = pair[rows + at : rows + at + half, :], peer[at : at + half, :]
-            out[...] = widened(mine, theirs)
+            unit, _ = unit_rows(widened(mine, theirs, out.shape[1] // 4))
+            out[...] = unit.astype(BF16)
 
 
 def relayed_half(pair, peer, other_half):
     wide_half(False, pair, peer, other_half)
 
 
-def fixed_and_half(pair, peer, fixed, own_half):
-    rows = fixed.shape[0]
-    fixed[...] = widened(pair[:rows, :], peer[rows:, :])
+def fixed_and_half(pair, peer, fixed, own_half, unit, inv):
+    rows, width = fixed.shape
+    wide = widened(pair[:rows, :], peer[rows:, :], width // 4)
+    unit[...], inv[...] = unit_rows(wide)
+    fixed[...] = unit[...].astype(BF16)
     wide_half(True, pair, peer, own_half)
 
 
@@ -188,55 +196,29 @@
     refs[-1][...] = before[...] + pull(factors, fixed[...], block)
 
 
-def on_diagonal(rows):
-    shape = (rows, rows)
-    return lax.broadcasted_iota(jnp.int32, shape, 0) == lax.broadcasted_iota(jnp.int32, shape, 1)
-
-
-def last_sum(factors, fixed, before, far_opposite, inv, keep, inner_kept, give):
-    core, chip = position()
+def last_sum(factors, fixed, before, far_opposite, unit, inv, keep, give):
+    _, chip = position()
     rows, width = fixed.shape
     span = width // 4
     cut = span // LANES * LANES
-    chip0 = chip == 0
-    a = fixed[...]
-    total = before[...] + pull(factors, a, far_opposite[...])
-    unit = a.astype(F32)
-    by_row = factors[0:1, 0:1] * inv[...]
-    inner = jnp.sum(unit * total, axis=1, keepdims=True) * by_row
-    across = total * by_row - unit * inner
+    total = before[...] + pull(factors, fixed[...], far_opposite[...])
+    inner = jnp.sum(unit[...] * total, axis=1, keepdims=True)
+    across = (total - unit[...] * inner) * (factors[0:1, 0:1] * inv[...])
     middle = 4 * cut + 2 * (span - cut)
     first = jnp.concatenate([across[:, : 2 * cut], across[:, 4 * cut : middle]], axis=1)
     last = jnp.concatenate([across[:, 2 * cut : 4 * cut], across[:, middle:]], axis=1)
-    keep[...] = jnp.where(chip0, first, last)
-    inner_kept[...] = inner
-    pack(give, 0, jnp.where(chip0, last, first).astype(BF16))
-    at = packed_rows(rows, 2 * span)
-    line = jnp.sum(jnp.where(on_diagonal(rows), inner, 0.0), axis=0, keepdims=True)
-    give[at : at + 16, :] = jnp.broadcast_to(line[:, :LANES], (16, LANES)).astype(BF16)
-    give[at + 16 : at + 32, :] = jnp.broadcast_to(line[:, rows - LANES :], (16, LANES)).astype(BF16)
-
-
-def finish_sum(kept, inner_kept, got, rest_mine, rest_peer, stacked):
+    keep[...] = jnp.where(chip == 0, first, last)
+    pack(give, 0, jnp.where(chip == 0, last, first).astype(BF16))
+
+
+def through_matrix(kept, got, mine, peer, to_chip, to_cross, to_core, keep, stacked):
+    core, chip = position()
     rows, width = kept.shape
-    at = packed_rows(rows, width)
-    start, end = got[at : at + 1, :], got[at + 16 : at + 17, :]
-    line = jnp.concatenate([start, end[:, 2 * LANES - rows :]], axis=1).astype(F32)
-    other = jnp.sum(jnp.where(on_diagonal(rows), line, 0.0), axis=1, keepdims=True)
-    rest = beside([rest_mine[...], rest_peer[...]], 1).astype(F32)
-    demb = kept[...] + unpack(got, 0, rows, width).astype(F32) - rest * (inner_kept[...] + other)
+    span = width // 2
+    demb = kept[...] + unpack(got, 0, rows, width).astype(F32)
     high = demb.astype(BF16)
     stacked[:rows, :] = high
     stacked[rows:, :] = (demb - high.astype(F32)).astype(BF16)
-
-
-def through_matrix(
-    kept, inner_kept, got, rest_mine, rest_peer, mine, peer, to_chip, to_cross, to_core, keep, stacked
-):
-    core, chip = position()
-    rows, width = kept.shape
-    span = width // 2
-    finish_sum(kept, inner_kept, got, rest_mine, rest_peer, stacked)
     matrix = beside([mine[...], peer[...]], 0)
     part = jnp.dot(stacked[...], matrix, preferred_element_type=F32)
     part = part[:rows] + part[rows:]
@@ -288,36 +270,35 @@
     txt_emb = jnp.dot(
         caption_averaged_vectors, caption_mapping_matrix, preferred_element_type=F32
     )
-    squares = jnp.concatenate(
-        [jnp.sum(img_emb * img_emb, axis=1), jnp.sum(txt_emb * txt_emb, axis=1)]
-    )
-    inv = lax.rsqrt(lax.psum(squares, "tensor") + 1e-06)
-    inv_img, inv_txt = inv[:rows], inv[rows:]
-    img_unit = img_emb * inv_img[:, None]
-    txt_unit = txt_emb * inv_txt[:, None]
-    piece = ((rows, span), BF16)
-    own, fixed_own, moving_own, rest_mine, rest_theirs = call(
-        unit_parts,
-        [((2 * packed_rows(rows, span), LANES), BF16)] + [piece] * 4,
-        img_unit,
-        txt_unit,
-    )
-    other = exchange(own, groups, chip_swap)
-    rest_peer = exchange(rest_theirs, groups, core_swap)
+    emb_piece = ((rows, span), F32)
+    own, fixed_own, moving_own = call(
+        embedded,
+        [((2 * packed_rows(rows, span), LANES), F32), emb_piece, emb_piece],
+        img_emb,
+        txt_emb,
+    )
+    sent = own.astype(F16)
+    other = exchange(sent, groups, chip_swap).astype(F32)
     img_matrix, txt_matrix, _ = lax.optimization_barrier(
-        (picture_mapping_matrix.T, caption_mapping_matrix.T, own)
+        (picture_mapping_matrix.T, caption_mapping_matrix.T, sent)
     )
     matrix_mine = jnp.where(core0, img_matrix, txt_matrix)
     matrix_theirs = jnp.where(core0, txt_matrix, img_matrix)
     matrix_peer = exchange(matrix_theirs, groups, core_swap)
-    (pair,) = call(pair_up, [((2 * rows, 2 * span), BF16)], fixed_own, moving_own, other)
-    peer = exchange(pair, groups, core_swap)
+    pair_width = 2 * (span // LANES * LANES) + LANES
+    (pair,) = call(pair_up, [((2 * rows, pair_width), F32)], fixed_own, moving_own, other)
+    peer = exchange(pair.astype(F16), groups, core_swap)
     peer, matrix_peer = lax.optimization_barrier((peer, matrix_peer))
+    peer = peer.astype(F32)
     half_width = ((half, width), BF16)
     (other_half,) = call(relayed_half, [half_width], pair, peer)
     pair, peer, other_half = lax.optimization_barrier((pair, peer, other_half))
-    fixed, own_half = call(fixed_and_half, [((rows, width), BF16), half_width], pair, peer)
-    inv_fixed = jnp.where(core0, inv_img, inv_txt)[:, None]
+    fixed, own_half, unit, inv = call(
+        fixed_and_half,
+        [((rows, width), BF16), half_width, ((rows, width), F32), ((rows, 1), F32)],
+        pair,
+        peer,
+    )
 
     first_row = lax.axis_index("dp") * rows
     ids = first_row + jnp.arange(rows, dtype=jnp.int32)
@@ -344,18 +325,15 @@
     (total,) = call(
         next_sum, sums, factors, fixed, total, *nearer, far_own, far_relayed, far_other
     )
-    keep, inner_kept, give = call(
+    keep, give = call(
         last_sum,
-        [
-            ((rows, 2 * span), F32),
-            ((rows, 1), F32),
-            ((packed_rows(rows, 2 * span) + 32, LANES), BF16),
-        ],
+        [((rows, 2 * span), F32), ((packed_rows(rows, 2 * span), LANES), BF16)],
         factors,
         fixed,
         total,
         far_opposite,
-        inv_fixed,
+        unit,
+        inv,
     )
     got = exchange(give, groups, chip_swap)
     part = ((rows, span), F32)
@@ -364,10 +342,7 @@
         through_matrix,
         [sent, sent, sent, part],
         keep,
-        inner_kept,
         got,
-        rest_mine,
-        rest_peer,
         matrix_mine,
         matrix_peer,
         scratch=[((2 * rows, 2 * span), BF16)],

time: 102 us -> 97.8 us (0.959)
  blocking collectives: 19.1 us -> 0 us
  waiting for transfers between devices: 24.9 us -> 35.6 us
  starting transfers between devices: 39 us -> 46.4 us
  Pallas kernels: 9.75 us -> 6.07 us
  other arithmetic: 1.53 us -> 3.19 us
    psum x1 -> x0, blocking collectives: 19.1 us -> none  [shards(): inv = lax.rsqrt(lax.psum(squares, 'tensor') + 1e-06)]
    ppermute x15 -> x14, waiting for transfers between devices: 24.9 us -> 35.6 us  [exchange(): return lax.ppermute(block, AXES, route)]
    ppermute x15 -> x14, starting transfers between devices: 39 us -> 46.4 us  [exchange(): return lax.ppermute(block, AXES, route)]
    pallas_call x9, Pallas kernels: 9.75 us -> 6.07 us  [call(): pl.pallas_call(kernel, cost_estimate=pl.CostEstimate(flops=flops, bytes_a...]
    convert_element_type x0 -> x4, other arithmetic: none -> 1.93 us  [the longest x1 0.97 us: shards(): other = exchange(sent, groups, chip_swap).astype(F32)]
    dot_general x1, matrix products: 1.73 us -> 0.45 us  [shards(): jnp.dot(caption_averaged_vectors, caption_mapping_matrix, preferred_eleme...]
    unnamed x18 -> x10, local copies, waits for them, and re-layouts: 2.36 us -> 1.68 us
  transfers between devices with their start and end apart: 15 -> 14, of which waited for: 10 -> 6; matrix products, arithmetic and copies ran while one was open for 1% -> 3% of each run, Pallas kernels for 5% -> 3%
where the time goes in v4:
time: 97.8 us; the launch traced here: 97.2 us
  starting transfers between devices  46.4 us (47%)
  waiting for transfers between devices  35.6 us (36%)
  Pallas kernels  6.07 us (6%)
  other arithmetic  3.19 us (3%)
  between operations  2.25 us (2%)
  matrix products  1.99 us (2%)
  local copies, waits for them, and re-layouts  1.75 us (2%)
    ppermute x14, starting transfers between devices, exchange(): return lax.ppermute(block, AXES, route)  46.4 us
    ppermute x14, waiting for transfers between devices, exchange(): return lax.ppermute(block, AXES, route)  35.6 us
    pallas_call x9, Pallas kernels, call(): pl.pallas_call(kernel, cost_estimate=pl.CostEstimate(flops=flops, bytes_a...  6.07 us
  transfers between devices with their start and end apart: 14, of which 6 were waited for; matrix products, arithmetic and copies ran while one was open for 3% of the time, Pallas kernels for 3%

profile of v4, /device:TPU:1, one launch (start us, length us, event | category | flops | bytes accessed | tf_op | source)
XLA Modules:
  0.0 97.2 jit_solution(4337737653883213964)
XLA Ops:
  0.7 1.0 %copy-done = bf16[192,1152]{1,0:T(8,128)(2,1)S(1)} copy-done((bf16[192,1152]{1,0:T(8,128)(2,1)S(1)}, bf16[192,1152]{1,0:T(8,128)(2,1)}, u32[]{:S(2)}) %copy-start) | copy-done | bytes 442392
  1.6 1.5 %fusion.img = f32[192,288]{1,0:T(8,128)S(1)} fusion(bf16[192,1152]{1,0:T(8,128)(2,1)S(1)} %copy-done, bf16[1152,288]{0,1:T(8,128)(2,1)} %param.8), kind=kOutput, calls=%fused_computation.7 | convolution fusion | flops 127401984 | bytes 1327104 | tf_op jit(solution)/shard_map/dot_general | solution.py:267
  3.9 4.2 %collective-permute-start = (f16[864,128]{1,0:T(8,128)(2,1)S(1)}, f16[864,128]{1,0:T(8,128)(2,1)}, u32[]{:S(2)}, u32[]{:S(2)}) collective-permute-start(f16[864,128]{1,0:T(8,128)(2,1)S(1)} %convert_element_type.12), channel_id=1, source_target_pairs={{2,0},{3,1},{0,2},{1,3},{6,4},{7,5},{4,6},{5,7},{10,8},{11,9},{8,1... | collective-permute-start | bytes 663560 | tf_op jit(solution)/shard_map/ppermute | solution.py:22
  8.1 1.0 %broadcast_select_fusion = (bf16[288,1152]{1,0:T(8,128)(2,1)S(1)}, bf16[288,1152]{1,0:T(8,128)(2,1)}) fusion(bf16[288,1152]{1,0:T(8,128)(2,1)S(1)} %bitcast.6, bf16[288,1152]{1,0:T(8,128)(2,1)S(1)} %bitcast.7, pred[]{:T(512)S(6)} %eq.16), kind=kLoop, calls=%fused_computation | loop fusion | flops 663552 | bytes 2654209 | tf_op jit(solution)/shard_map/jit(_where)/select_n | solution.py:285
  9.1 13.8 %collective-permute-start.2 = (bf16[288,1152]{1,0:T(8,128)(2,1)}, bf16[288,1152]{1,0:T(8,128)(2,1)S(1)}, u32[]{:S(2)}, u32[]{:S(2)}) collective-permute-start(bf16[288,1152]{1,0:T(8,128)(2,1)} %get-tuple-element.47), channel_id=1, source_target_pairs={{1,0},{0,1},{3,2},{2,3},{5,4},{4,5},{7,6},{6,7},{9,8},{8,9},{11,10... | collective-permute-start | bytes 1990664 | tf_op jit(solution)/shard_map/ppermute | solution.py:22
  22.9 1.0 convert_element_type.13.got
  24.1 0.9 convert_element_type.14
  25.0 5.0 %collective-permute-start.1 = (f16[384,640]{1,0:T(8,128)(2,1)}, f16[384,640]{1,0:T(8,128)(2,1)S(1)}, u32[]{:S(2)}, u32[]{:S(2)}) collective-permute-start(f16[384,640]{1,0:T(8,128)(2,1)} %convert_element_type.14), channel_id=1, source_target_pairs={{1,0},{0,1},{3,2},{2,3},{5,4},{4,5},{7,6},{6,7},{9,8},{8,9},{11,10... | collective-permute-start | bytes 1474568 | tf_op jit(solution)/shard_map/ppermute | solution.py:22
  31.3 0.7 copy-done.4
  32.4 1.9 %collective-permute-start.3 = (bf16[96,1152]{1,0:T(8,128)(2,1)S(1)}, bf16[96,1152]{1,0:T(8,128)(2,1)S(1)}, u32[]{:S(2)}, u32[]{:S(2)}) collective-permute-start(bf16[96,1152]{1,0:T(8,128)(2,1)S(1)} %shard_map.88), channel_id=1, source_target_pairs={{14,0},{1023,1},{4,2},{1013,3},{18,4},{3,5},{8,6},{1017,7},{22,8},... | collective-permute-start | bytes 663560 | tf_op jit(solution)/shard_map/ppermute | solution.py:22
  34.5 0.5 shard_map.89
  35.0 1.9 %collective-permute-start.4 = (bf16[96,1152]{1,0:T(8,128)(2,1)S(1)}, bf16[96,1152]{1,0:T(8,128)(2,1)S(1)}, u32[]{:S(2)}, u32[]{:S(2)}) collective-permute-start(bf16[96,1152]{1,0:T(8,128)(2,1)S(1)} %get-tuple-element.34.own_half), channel_id=1, source_target_pairs={{14,0},{1023,1},{4,2},{1013,3},{18,4},{3,5},{8,6},{1017,7},{22,8},... | collective-permute-start | bytes 663560 | tf_op jit(solution)/shard_map/ppermute | solution.py:22
  37.0 0.6 shard_map.90.before
  37.6 9.8 %collective-permute-done.3.refs_0_ = bf16[96,1152]{1,0:T(8,128)(2,1)S(1)} collective-permute-done((bf16[96,1152]{1,0:T(8,128)(2,1)S(1)}, bf16[96,1152]{1,0:T(8,128)(2,1)S(1)}, u32[]{:S(2)}, u32[]{:S(2)}) %collective-permute-start.3) | collective-permute-done | bytes 221216 | tf_op jit(solution)/shard_map/ppermute | solution.py:22
  47.4 1.9 %collective-permute-start.5 = (bf16[96,1152]{1,0:T(8,128)(2,1)S(1)}, bf16[96,1152]{1,0:T(8,128)(2,1)S(1)}, u32[]{:S(2)}, u32[]{:S(2)}) collective-permute-start(bf16[96,1152]{1,0:T(8,128)(2,1)S(1)} %collective-permute-done.3.refs_0_), channel_id=1, source_target_pairs={{1020,0},{1021,1},{6,2},{7,3},{0,4},{1,5},{10,6},{11,7},{4,8},{5,9... | collective-permute-start | bytes 663560 | tf_op jit(solution)/shard_map/ppermute | solution.py:22
  49.4 1.9 %collective-permute-start.6 = (bf16[96,1152]{1,0:T(8,128)(2,1)S(1)}, bf16[96,1152]{1,0:T(8,128)(2,1)S(1)}, u32[]{:S(2)}, u32[]{:S(2)}) collective-permute-start(bf16[96,1152]{1,0:T(8,128)(2,1)S(1)} %get-tuple-element.34.own_half), channel_id=1, source_target_pairs={{16,0},{1009,1},{18,2},{1011,3},{20,4},{1013,5},{22,6},{1015,7},{2... | collective-permute-start | bytes 663560 | tf_op jit(solution)/shard_map/ppermute | solution.py:22
  51.3 1.9 %collective-permute-start.8 = (bf16[96,1152]{1,0:T(8,128)(2,1)S(1)}, bf16[96,1152]{1,0:T(8,128)(2,1)S(1)}, u32[]{:S(2)}, u32[]{:S(2)}) collective-permute-start(bf16[96,1152]{1,0:T(8,128)(2,1)S(1)} %collective-permute-done.4.refs_1_), channel_id=1, source_target_pairs={{16,0},{1009,1},{18,2},{1011,3},{20,4},{1013,5},{22,6},{1015,7},{2... | collective-permute-start | bytes 663560 | tf_op jit(solution)/shard_map/ppermute | solution.py:22
  53.2 1.9 %collective-permute-start.7 = (bf16[96,1152]{1,0:T(8,128)(2,1)S(1)}, bf16[96,1152]{1,0:T(8,128)(2,1)S(1)}, u32[]{:S(2)}, u32[]{:S(2)}) collective-permute-start(bf16[96,1152]{1,0:T(8,128)(2,1)S(1)} %collective-permute-done.3.refs_0_), channel_id=1, source_target_pairs={{16,0},{1009,1},{18,2},{1011,3},{20,4},{1013,5},{22,6},{1015,7},{2... | collective-permute-start | bytes 663560 | tf_op jit(solution)/shard_map/ppermute | solution.py:22
  55.2 10.5 %collective-permute-done.5.refs_2_ = bf16[96,1152]{1,0:T(8,128)(2,1)S(1)} collective-permute-done((bf16[96,1152]{1,0:T(8,128)(2,1)S(1)}, bf16[96,1152]{1,0:T(8,128)(2,1)S(1)}, u32[]{:S(2)}, u32[]{:S(2)}) %collective-permute-start.5) | collective-permute-done | bytes 221216 | tf_op jit(solution)/shard_map/ppermute | solution.py:22
  65.6 1.9 %collective-permute-start.9 = (bf16[96,1152]{1,0:T(8,128)(2,1)S(1)}, bf16[96,1152]{1,0:T(8,128)(2,1)S(1)}, u32[]{:S(2)}, u32[]{:S(2)}) collective-permute-start(bf16[96,1152]{1,0:T(8,128)(2,1)S(1)} %collective-permute-done.5.refs_2_), channel_id=1, source_target_pairs={{16,0},{1009,1},{18,2},{1011,3},{20,4},{1013,5},{22,6},{1015,7},{2... | collective-permute-start | bytes 663560 | tf_op jit(solution)/shard_map/ppermute | solution.py:22
  67.6 1.7 %collective-permute-done.7.refs_4_ = bf16[96,1152]{1,0:T(8,128)(2,1)S(1)} collective-permute-done((bf16[96,1152]{1,0:T(8,128)(2,1)S(1)}, bf16[96,1152]{1,0:T(8,128)(2,1)S(1)}, u32[]{:S(2)}, u32[]{:S(2)}) %collective-permute-start.7) | collective-permute-done | bytes 221216 | tf_op jit(solution)/shard_map/ppermute | solution.py:22
  69.2 1.2 %shard_map.91.before = f32[192,1152]{1,0:T(8,128)S(1)} custom-call(f32[2,128]{1,0:T(2,128)S(1)} %broadcast_in_dim.8.factors, bf16[192,1152]{1,0:T(8,128)(2,1)S(1)} %get-tuple-element.32.fixed, f32[192,1152]{1,0:T(8,128)S(1)} %shard_map.90.before, bf16[96,1152]{1,0:T(8,128)(2,1)S(1)} %collective-permute-done.3.refs_0_, ...), custom_call_target="tpu_custom_call" | custom-call | bytes 2655232 | tf_op jit(solution)/shard_map/pallas_call | solution.py:59
  70.4 5.2 %collective-permute-done.9.far_opposite = bf16[96,1152]{1,0:T(8,128)(2,1)S(1)} collective-permute-done((bf16[96,1152]{1,0:T(8,128)(2,1)S(1)}, bf16[96,1152]{1,0:T(8,128)(2,1)S(1)}, u32[]{:S(2)}, u32[]{:S(2)}) %collective-permute-start.9) | collective-permute-done | bytes 221216 | tf_op jit(solution)/shard_map/ppermute | solution.py:22
  75.6 1.0 %shard_map.92 = (f32[192,576]{1,0:T(8,128)S(1)}, bf16[864,128]{1,0:T(8,128)(2,1)S(1)}) custom-call(f32[2,128]{1,0:T(2,128)S(1)} %broadcast_in_dim.8.factors, bf16[192,1152]{1,0:T(8,128)(2,1)S(1)} %get-tuple-element.32.fixed, f32[192,1152]{1,0:T(8,128)S(1)} %shard_map.91.before, bf16[96,1152]{1,0:T(8,128)(2,1)S(1)} %collective-permute-done.9.far_opposite, ...), custom_call_target="tpu_custom_call" | custom-call | bytes 2434816 | tf_op jit(solution)/shard_map/pallas_call | solution.py:59
  76.6 1.9 %collective-permute-start.10 = (bf16[864,128]{1,0:T(8,128)(2,1)S(1)}, bf16[864,128]{1,0:T(8,128)(2,1)S(1)}, u32[]{:S(2)}, u32[]{:S(2)}) collective-permute-start(bf16[864,128]{1,0:T(8,128)(2,1)S(1)} %get-tuple-element.40), channel_id=1, source_target_pairs={{2,0},{3,1},{0,2},{1,3},{6,4},{7,5},{4,6},{5,7},{10,8},{11,9},{8,1... | collective-permute-start | bytes 663560 | tf_op jit(solution)/shard_map/ppermute | solution.py:22
  78.5 7.1 %collective-permute-done.10.got = bf16[864,128]{1,0:T(8,128)(2,1)S(1)} collective-permute-done((bf16[864,128]{1,0:T(8,128)(2,1)S(1)}, bf16[864,128]{1,0:T(8,128)(2,1)S(1)}, u32[]{:S(2)}, u32[]{:S(2)}) %collective-permute-start.10) | collective-permute-done | bytes 221216 | tf_op jit(solution)/shard_map/ppermute | solution.py:22
  85.6 1.2 %shard_map.93 = (bf16[432,128]{1,0:T(8,128)(2,1)S(1)}, bf16[432,128]{1,0:T(8,128)(2,1)S(1)}, bf16[432,128]{1,0:T(8,128)(2,1)S(1)}, f32[192,288]{1,0:T(8,128)S(1)}) custom-call(f32[192,576]{1,0:T(8,128)S(1)} %get-tuple-element.39.kept, bf16[864,128]{1,0:T(8,128)(2,1)S(1)} %collective-permute-done.10.got, bf16[288,1152]{1,0:T(8,128)(2,1)S(1)} %get-tuple-element.46.mine, ...), custom_call_target="tpu_custom_call" | custom-call | bytes 1990656 | tf_op jit(solution)/shard_map/pallas_call | solution.py:59
  86.8 2.1 %collective-permute-start.11 = (bf16[432,128]{1,0:T(8,128)(2,1)S(1)}, bf16[432,128]{1,0:T(8,128)(2,1)S(1)}, u32[]{:S(2)}, u32[]{:S(2)}) collective-permute-start(bf16[432,128]{1,0:T(8,128)(2,1)S(1)} %get-tuple-element.42), channel_id=1, source_target_pairs={{2,0},{3,1},{0,2},{1,3},{6,4},{7,5},{4,6},{5,7},{10,8},{11,9},{8,1... | collective-permute-start | bytes 331784 | tf_op jit(solution)/shard_map/ppermute | solution.py:22
  88.9 4.1 %collective-permute-start.12 = (bf16[432,128]{1,0:T(8,128)(2,1)S(1)}, bf16[432,128]{1,0:T(8,128)(2,1)S(1)}, u32[]{:S(2)}, u32[]{:S(2)}) collective-permute-start(bf16[432,128]{1,0:T(8,128)(2,1)S(1)} %get-tuple-element.43), channel_id=1, source_target_pairs={{3,0},{2,1},{1,2},{0,3},{7,4},{6,5},{5,6},{4,7},{11,8},{10,9},{9,1... | collective-permute-start | bytes 331784 | tf_op jit(solution)/shard_map/ppermute | solution.py:22
  93.0 1.9 %collective-permute-start.13 = (bf16[432,128]{1,0:T(8,128)(2,1)S(1)}, bf16[432,128]{1,0:T(8,128)(2,1)S(1)}, u32[]{:S(2)}, u32[]{:S(2)}) collective-permute-start(bf16[432,128]{1,0:T(8,128)(2,1)S(1)} %get-tuple-element.44), channel_id=1, source_target_pairs={{1,0},{0,1},{3,2},{2,3},{5,4},{4,5},{7,6},{6,7},{9,8},{8,9},{11,10... | collective-permute-start | bytes 331784 | tf_op jit(solution)/shard_map/ppermute | solution.py:22
  94.9 1.4 %collective-permute-done.12.from_cross = bf16[432,128]{1,0:T(8,128)(2,1)S(1)} collective-permute-done((bf16[432,128]{1,0:T(8,128)(2,1)S(1)}, bf16[432,128]{1,0:T(8,128)(2,1)S(1)}, u32[]{:S(2)}, u32[]{:S(2)}) %collective-permute-start.12) | collective-permute-done | bytes 110624 | tf_op jit(solution)/shard_map/ppermute | solution.py:22
  96.3 0.9 shard_map.94
  (27 shorter events, 1.5 us)
Async XLA Ops:
  0.6 1.0 %copy-start = (bf16[192,1152]{1,0:T(8,128)(2,1)S(1)}, bf16[192,1152]{1,0:T(8,128)(2,1)}, u32[]{:S(2)}) copy-start(bf16[192,1152]{1,0:T(8,128)(2,1)} %param.7) | copy-start | bytes 1327108
  0.6 2.5 %copy-start.2 = (bf16[1152,288]{0,1:T(8,128)(2,1)S(1)}, bf16[1152,288]{0,1:T(8,128)(2,1)}, u32[]{:S(2)}) copy-start(bf16[1152,288]{0,1:T(8,128)(2,1)} %param.10) | copy-start | bytes 1990660
  0.7 2.5 %copy-start.3 = (bf16[192,1152]{1,0:T(8,128)(2,1)S(1)}, bf16[192,1152]{1,0:T(8,128)(2,1)}, u32[]{:S(2)}) copy-start(bf16[192,1152]{1,0:T(8,128)(2,1)} %param.9) | copy-start | bytes 1327108
  3.7 4.4 %copy-start.1 = (bf16[1152,288]{0,1:T(8,128)(2,1)S(1)}, bf16[1152,288]{0,1:T(8,128)(2,1)}, u32[]{:S(2)}) copy-start(bf16[1152,288]{0,1:T(8,128)(2,1)} %param.8) | copy-start | bytes 1990660
  3.9 19.0 %collective-permute-start = (f16[864,128]{1,0:T(8,128)(2,1)S(1)}, f16[864,128]{1,0:T(8,128)(2,1)}, u32[]{:S(2)}, u32[]{:S(2)}) collective-permute-start(f16[864,128]{1,0:T(8,128)(2,1)S(1)} %convert_element_type.12), channel_id=1, source_target_pairs={{2,0},{3,1},{0,2},{1,3},{6,4},{7,5},{4,6},{5,7},{10,8},{11,9},{8,1... | collective-permute-start | bytes 663560 | tf_op jit(solution)/shard_map/ppermute | solution.py:22
  9.1 23.0 %collective-permute-start.2 = (bf16[288,1152]{1,0:T(8,128)(2,1)}, bf16[288,1152]{1,0:T(8,128)(2,1)S(1)}, u32[]{:S(2)}, u32[]{:S(2)}) collective-permute-start(bf16[288,1152]{1,0:T(8,128)(2,1)} %get-tuple-element.47), channel_id=1, source_target_pairs={{1,0},{0,1},{3,2},{2,3},{5,4},{4,5},{7,6},{6,7},{9,8},{8,9},{11,10... | collective-permute-start | bytes 1990664 | tf_op jit(solution)/shard_map/ppermute | solution.py:22
  25.0 7.1 %collective-permute-start.1 = (f16[384,640]{1,0:T(8,128)(2,1)}, f16[384,640]{1,0:T(8,128)(2,1)S(1)}, u32[]{:S(2)}, u32[]{:S(2)}) collective-permute-start(f16[384,640]{1,0:T(8,128)(2,1)} %convert_element_type.14), channel_id=1, source_target_pairs={{1,0},{0,1},{3,2},{2,3},{5,4},{4,5},{7,6},{6,7},{9,8},{8,9},{11,10... | collective-permute-start | bytes 1474568 | tf_op jit(solution)/shard_map/ppermute | solution.py:22
  31.3 0.7 copy-start.4
  32.4 15.0 %collective-permute-start.3 = (bf16[96,1152]{1,0:T(8,128)(2,1)S(1)}, bf16[96,1152]{1,0:T(8,128)(2,1)S(1)}, u32[]{:S(2)}, u32[]{:S(2)}) collective-permute-start(bf16[96,1152]{1,0:T(8,128)(2,1)S(1)} %shard_map.88), channel_id=1, source_target_pairs={{14,0},{1023,1},{4,2},{1013,3},{18,4},{3,5},{8,6},{1017,7},{22,8},... | collective-permute-start | bytes 663560 | tf_op jit(solution)/shard_map/ppermute | solution.py:22
  35.0 16.3 %collective-permute-start.4 = (bf16[96,1152]{1,0:T(8,128)(2,1)S(1)}, bf16[96,1152]{1,0:T(8,128)(2,1)S(1)}, u32[]{:S(2)}, u32[]{:S(2)}) collective-permute-start(bf16[96,1152]{1,0:T(8,128)(2,1)S(1)} %get-tuple-element.34.own_half), channel_id=1, source_target_pairs={{14,0},{1023,1},{4,2},{1013,3},{18,4},{3,5},{8,6},{1017,7},{22,8},... | collective-permute-start | bytes 663560 | tf_op jit(solution)/shard_map/ppermute | solution.py:22
  47.4 18.2 %collective-permute-start.5 = (bf16[96,1152]{1,0:T(8,128)(2,1)S(1)}, bf16[96,1152]{1,0:T(8,128)(2,1)S(1)}, u32[]{:S(2)}, u32[]{:S(2)}) collective-permute-start(bf16[96,1152]{1,0:T(8,128)(2,1)S(1)} %collective-permute-done.3.refs_0_), channel_id=1, source_target_pairs={{1020,0},{1021,1},{6,2},{7,3},{0,4},{1,5},{10,6},{11,7},{4,8},{5,9... | collective-permute-start | bytes 663560 | tf_op jit(solution)/shard_map/ppermute | solution.py:22
  49.4 18.2 %collective-permute-start.6 = (bf16[96,1152]{1,0:T(8,128)(2,1)S(1)}, bf16[96,1152]{1,0:T(8,128)(2,1)S(1)}, u32[]{:S(2)}, u32[]{:S(2)}) collective-permute-start(bf16[96,1152]{1,0:T(8,128)(2,1)S(1)} %get-tuple-element.34.own_half), channel_id=1, source_target_pairs={{16,0},{1009,1},{18,2},{1011,3},{20,4},{1013,5},{22,6},{1015,7},{2... | collective-permute-start | bytes 663560 | tf_op jit(solution)/shard_map/ppermute | solution.py:22
  51.3 16.3 %collective-permute-start.8 = (bf16[96,1152]{1,0:T(8,128)(2,1)S(1)}, bf16[96,1152]{1,0:T(8,128)(2,1)S(1)}, u32[]{:S(2)}, u32[]{:S(2)}) collective-permute-start(bf16[96,1152]{1,0:T(8,128)(2,1)S(1)} %collective-permute-done.4.refs_1_), channel_id=1, source_target_pairs={{16,0},{1009,1},{18,2},{1011,3},{20,4},{1013,5},{22,6},{1015,7},{2... | collective-permute-start | bytes 663560 | tf_op jit(solution)/shard_map/ppermute | solution.py:22
  53.2 16.0 %collective-permute-start.7 = (bf16[96,1152]{1,0:T(8,128)(2,1)S(1)}, bf16[96,1152]{1,0:T(8,128)(2,1)S(1)}, u32[]{:S(2)}, u32[]{:S(2)}) collective-permute-start(bf16[96,1152]{1,0:T(8,128)(2,1)S(1)} %collective-permute-done.3.refs_0_), channel_id=1, source_target_pairs={{16,0},{1009,1},{18,2},{1011,3},{20,4},{1013,5},{22,6},{1015,7},{2... | collective-permute-start | bytes 663560 | tf_op jit(solution)/shard_map/ppermute | solution.py:22
  65.6 10.0 %collective-permute-start.9 = (bf16[96,1152]{1,0:T(8,128)(2,1)S(1)}, bf16[96,1152]{1,0:T(8,128)(2,1)S(1)}, u32[]{:S(2)}, u32[]{:S(2)}) collective-permute-start(bf16[96,1152]{1,0:T(8,128)(2,1)S(1)} %collective-permute-done.5.refs_2_), channel_id=1, source_target_pairs={{16,0},{1009,1},{18,2},{1011,3},{20,4},{1013,5},{22,6},{1015,7},{2... | collective-permute-start | bytes 663560 | tf_op jit(solution)/shard_map/ppermute | solution.py:22
  76.6 9.0 %collective-permute-start.10 = (bf16[864,128]{1,0:T(8,128)(2,1)S(1)}, bf16[864,128]{1,0:T(8,128)(2,1)S(1)}, u32[]{:S(2)}, u32[]{:S(2)}) collective-permute-start(bf16[864,128]{1,0:T(8,128)(2,1)S(1)} %get-tuple-element.40), channel_id=1, source_target_pairs={{2,0},{3,1},{0,2},{1,3},{6,4},{7,5},{4,6},{5,7},{10,8},{11,9},{8,1... | collective-permute-start | bytes 663560 | tf_op jit(solution)/shard_map/ppermute | solution.py:22
  86.8 8.1 %collective-permute-start.11 = (bf16[432,128]{1,0:T(8,128)(2,1)S(1)}, bf16[432,128]{1,0:T(8,128)(2,1)S(1)}, u32[]{:S(2)}, u32[]{:S(2)}) collective-permute-start(bf16[432,128]{1,0:T(8,128)(2,1)S(1)} %get-tuple-element.42), channel_id=1, source_target_pairs={{2,0},{3,1},{0,2},{1,3},{6,4},{7,5},{4,6},{5,7},{10,8},{11,9},{8,1... | collective-permute-start | bytes 331784 | tf_op jit(solution)/shard_map/ppermute | solution.py:22
  88.9 7.4 %collective-permute-start.12 = (bf16[432,128]{1,0:T(8,128)(2,1)S(1)}, bf16[432,128]{1,0:T(8,128)(2,1)S(1)}, u32[]{:S(2)}, u32[]{:S(2)}) collective-permute-start(bf16[432,128]{1,0:T(8,128)(2,1)S(1)} %get-tuple-element.43), channel_id=1, source_target_pairs={{3,0},{2,1},{1,2},{0,3},{7,4},{6,5},{5,6},{4,7},{11,8},{10,9},{9,1... | collective-permute-start | bytes 331784 | tf_op jit(solution)/shard_map/ppermute | solution.py:22
  93.0 3.3 %collective-permute-start.13 = (bf16[432,128]{1,0:T(8,128)(2,1)S(1)}, bf16[432,128]{1,0:T(8,128)(2,1)S(1)}, u32[]{:S(2)}, u32[]{:S(2)}) collective-permute-start(bf16[432,128]{1,0:T(8,128)(2,1)S(1)} %get-tuple-element.44), channel_id=1, source_target_pairs={{1,0},{0,1},{3,2},{2,3},{5,4},{4,5},{7,6},{6,7},{9,8},{8,9},{11,10... | collective-permute-start | bytes 331784 | tf_op jit(solution)/shard_map/ppermute | solution.py:22

commit v5 on v4

--- a/solution.py
+++ b/solution.py
@@ -285,6 +285,17 @@
     matrix_mine = jnp.where(core0, img_matrix, txt_matrix)
     matrix_theirs = jnp.where(core0, txt_matrix, img_matrix)
     matrix_peer = exchange(matrix_theirs, groups, core_swap)
+    first_row = lax.axis_index("dp") * rows
+    ids = first_row + jnp.arange(rows, dtype=jnp.int32)
+    half_ids = jnp.where(chip0, ids[:half], ids[half:])
+    half_index = jnp.where(chip0, paired_caption_index[:half], paired_caption_index[half:])
+    matched = jnp.where(
+        core0,
+        paired_caption_index[:, None] == half_ids[None, :],
+        ids[:, None] == half_index[None, :],
+    )
+    sign = jnp.where(matched, 1.0, -1.0).astype(F32)
+    other, sign = lax.optimization_barrier((other, sign))
     pair_width = 2 * (span // LANES * LANES) + LANES
     (pair,) = call(pair_up, [((2 * rows, pair_width), F32)], fixed_own, moving_own, other)
     peer = exchange(pair.astype(F16), groups, core_swap)
@@ -300,31 +311,20 @@
         peer,
     )
 
-    first_row = lax.axis_index("dp") * rows
-    ids = first_row + jnp.arange(rows, dtype=jnp.int32)
-    half_ids = jnp.where(chip0, ids[:half], ids[half:])
-    half_index = jnp.where(chip0, paired_caption_index[:half], paired_caption_index[half:])
-    matched = jnp.where(
-        core0,
-        paired_caption_index[:, None] == half_ids[None, :],
-        ids[:, None] == half_index[None, :],
-    )
-    sign = jnp.where(matched, 1.0, -1.0).astype(F32)
-
     sums = [((rows, width), F32)]
     near_relayed = exchange(other_half, groups, neighbour)
+    far_own = exchange(own_half, groups, beyond)
     near_other = exchange(own_half, groups, neighbour)
     (total,) = call(first_sum, sums, factors, fixed, sign, own_half)
     near_relayed, total = lax.optimization_barrier((near_relayed, total))
     opposite = exchange(near_relayed, groups, relay)
-    far_own = exchange(own_half, groups, beyond)
-    far_relayed = exchange(near_relayed, groups, beyond)
+    far_own, near_sent = lax.optimization_barrier((far_own, near_relayed))
+    far_relayed = exchange(near_sent, groups, beyond)
     far_other = exchange(near_other, groups, beyond)
+    (total,) = call(next_sum, sums, factors, fixed, total, far_own, near_relayed, near_other)
+    opposite, total = lax.optimization_barrier((opposite, total))
     far_opposite = exchange(opposite, groups, beyond)
-    nearer = (near_relayed, near_other, opposite)
-    (total,) = call(
-        next_sum, sums, factors, fixed, total, *nearer, far_own, far_relayed, far_other
-    )
+    (total,) = call(next_sum, sums, factors, fixed, total, opposite, far_relayed, far_other)
     keep, give = call(
         last_sum,
         [((rows, 2 * span), F32), ((packed_rows(rows, 2 * span), LANES), BF16)],

time: 97.8 us -> 95 us (0.971)
  waiting for transfers between devices: 35.6 us -> 28.7 us
  starting transfers between devices: 46.4 us -> 51.5 us
  other arithmetic: 3.19 us -> 1.45 us
    ppermute x14, waiting for transfers between devices: 35.6 us -> 28.7 us  [exchange(): return lax.ppermute(block, AXES, route)]
    ppermute x14, starting transfers between devices: 46.4 us -> 51.5 us  [exchange(): return lax.ppermute(block, AXES, route)]
    pallas_call x9 -> x10, Pallas kernels: 6.07 us -> 6.76 us  [call(): pl.pallas_call(kernel, cost_estimate=pl.CostEstimate(flops=flops, bytes_a...]
  transfers between devices with their start and end apart: 14 -> 14, of which waited for: 6 -> 10; matrix products, arithmetic and copies ran while one was open for 3% -> 2% of each run, Pallas kernels for 3% -> 3%
where the time goes in v5:
time: 95 us; the launch traced here: 94.4 us
  starting transfers between devices  51.5 us (54%)
  waiting for transfers between devices  28.7 us (30%)
  Pallas kernels  6.76 us (7%)
  between operations  2.27 us (2%)
  matrix products  1.98 us (2%)
  local copies, waits for them, and re-layouts  1.74 us (2%)
  other arithmetic  1.45 us (2%)
    ppermute x14, starting transfers between devices, exchange(): return lax.ppermute(block, AXES, route)  51.5 us
    ppermute x14, waiting for transfers between devices, exchange(): return lax.ppermute(block, AXES, route)  28.7 us
    pallas_call x10, Pallas kernels, call(): pl.pallas_call(kernel, cost_estimate=pl.CostEstimate(flops=flops, bytes_a...  6.76 us
  transfers between devices with their start and end apart: 14, of which 10 were waited for; matrix products, arithmetic and copies ran while one was open for 2% of the time, Pallas kernels for 3%

profile of v5, /device:TPU:1, one launch (start us, length us, event | category | flops | bytes accessed | tf_op | source)
XLA Modules:
  0.0 94.4 jit_solution(13949125805569409135)
XLA Ops:
  0.7 1.0 %copy-done = bf16[192,1152]{1,0:T(8,128)(2,1)S(1)} copy-done((bf16[192,1152]{1,0:T(8,128)(2,1)S(1)}, bf16[192,1152]{1,0:T(8,128)(2,1)}, u32[]{:S(2)}) %copy-start) | copy-done | bytes 442392
  1.6 1.5 %fusion.img = f32[192,288]{1,0:T(8,128)S(1)} fusion(bf16[192,1152]{1,0:T(8,128)(2,1)S(1)} %copy-done, bf16[1152,288]{0,1:T(8,128)(2,1)} %param.8), kind=kOutput, calls=%fused_computation.7 | convolution fusion | flops 127401984 | bytes 1327104 | tf_op jit(solution)/shard_map/dot_general | solution.py:267
  3.9 4.1 %collective-permute-start = (f16[864,128]{1,0:T(8,128)(2,1)S(1)}, f16[864,128]{1,0:T(8,128)(2,1)S(1)}, u32[]{:S(2)}, u32[]{:S(2)}) collective-permute-start(f16[864,128]{1,0:T(8,128)(2,1)S(1)} %convert_element_type.12), channel_id=1, source_target_pairs={{2,0},{3,1},{0,2},{1,3},{6,4},{7,5},{4,6},{5,7},{10,8},{11,9},{8,1... | collective-permute-start | bytes 663560 | tf_op jit(solution)/shard_map/ppermute | solution.py:22
  8.1 1.0 %broadcast_select_fusion = (bf16[288,1152]{1,0:T(8,128)(2,1)S(1)}, bf16[288,1152]{1,0:T(8,128)(2,1)}) fusion(bf16[288,1152]{1,0:T(8,128)(2,1)S(1)} %bitcast.6, bf16[288,1152]{1,0:T(8,128)(2,1)S(1)} %bitcast.7, pred[]{:T(512)S(6)} %eq.16), kind=kLoop, calls=%fused_computation | loop fusion | flops 663552 | bytes 2654209 | tf_op jit(solution)/shard_map/jit(_where)/select_n | solution.py:285
  9.1 13.8 %collective-permute-start.2 = (bf16[288,1152]{1,0:T(8,128)(2,1)}, bf16[288,1152]{1,0:T(8,128)(2,1)S(1)}, u32[]{:S(2)}, u32[]{:S(2)}) collective-permute-start(bf16[288,1152]{1,0:T(8,128)(2,1)} %get-tuple-element.59), channel_id=1, source_target_pairs={{1,0},{0,1},{3,2},{2,3},{5,4},{4,5},{7,6},{6,7},{9,8},{8,9},{11,10... | collective-permute-start | bytes 1990664 | tf_op jit(solution)/shard_map/ppermute | solution.py:22
  22.9 0.7 copy-done.4
  24.1 4.0 %collective-permute-start.1 = (f16[384,640]{1,0:T(8,128)(2,1)S(1)}, f16[384,640]{1,0:T(8,128)(2,1)S(1)}, u32[]{:S(2)}, u32[]{:S(2)}) collective-permute-start(f16[384,640]{1,0:T(8,128)(2,1)S(1)} %convert_element_type.14), channel_id=1, source_target_pairs={{1,0},{0,1},{3,2},{2,3},{5,4},{4,5},{7,6},{6,7},{9,8},{8,9},{11,10... | collective-permute-start | bytes 1474568 | tf_op jit(solution)/shard_map/ppermute | solution.py:22
  28.1 1.5 %collective-permute-done.1 = f16[384,640]{1,0:T(8,128)(2,1)S(1)} collective-permute-done((f16[384,640]{1,0:T(8,128)(2,1)S(1)}, f16[384,640]{1,0:T(8,128)(2,1)S(1)}, u32[]{:S(2)}, u32[]{:S(2)}) %collective-permute-start.1) | collective-permute-done | bytes 491552 | tf_op jit(solution)/shard_map/ppermute | solution.py:22
  29.9 1.9 %collective-permute-start.3 = (bf16[96,1152]{1,0:T(8,128)(2,1)S(1)}, bf16[96,1152]{1,0:T(8,128)(2,1)S(1)}, u32[]{:S(2)}, u32[]{:S(2)}) collective-permute-start(bf16[96,1152]{1,0:T(8,128)(2,1)S(1)} %shard_map.88), channel_id=1, source_target_pairs={{14,0},{1023,1},{4,2},{1013,3},{18,4},{3,5},{8,6},{1017,7},{22,8},... | collective-permute-start | bytes 663560 | tf_op jit(solution)/shard_map/ppermute | solution.py:22
  33.7 1.9 %collective-permute-start.5 = (bf16[96,1152]{1,0:T(8,128)(2,1)S(1)}, bf16[96,1152]{1,0:T(8,128)(2,1)S(1)}, u32[]{:S(2)}, u32[]{:S(2)}) collective-permute-start(bf16[96,1152]{1,0:T(8,128)(2,1)S(1)} %get-tuple-element.42.own_half), channel_id=1, source_target_pairs={{16,0},{1009,1},{18,2},{1011,3},{20,4},{1013,5},{22,6},{1015,7},{2... | collective-permute-start | bytes 663560 | tf_op jit(solution)/shard_map/ppermute | solution.py:22
  35.6 1.9 %collective-permute-start.6 = (bf16[96,1152]{1,0:T(8,128)(2,1)S(1)}, bf16[96,1152]{1,0:T(8,128)(2,1)S(1)}, u32[]{:S(2)}, u32[]{:S(2)}) collective-permute-start(bf16[96,1152]{1,0:T(8,128)(2,1)S(1)} %get-tuple-element.42.own_half), channel_id=1, source_target_pairs={{14,0},{1023,1},{4,2},{1013,3},{18,4},{3,5},{8,6},{1017,7},{22,8},... | collective-permute-start | bytes 663560 | tf_op jit(solution)/shard_map/ppermute | solution.py:22
  37.6 0.6 shard_map.90.before
  38.3 6.7 %collective-permute-done.3.refs_1_ = bf16[96,1152]{1,0:T(8,128)(2,1)S(1)} collective-permute-done((bf16[96,1152]{1,0:T(8,128)(2,1)S(1)}, bf16[96,1152]{1,0:T(8,128)(2,1)S(1)}, u32[]{:S(2)}, u32[]{:S(2)}) %collective-permute-start.3) | collective-permute-done | bytes 221216 | tf_op jit(solution)/shard_map/ppermute | solution.py:22
  44.9 1.9 %collective-permute-start.4 = (bf16[96,1152]{1,0:T(8,128)(2,1)S(1)}, bf16[96,1152]{1,0:T(8,128)(2,1)S(1)}, u32[]{:S(2)}, u32[]{:S(2)}) collective-permute-start(bf16[96,1152]{1,0:T(8,128)(2,1)S(1)} %collective-permute-done.3.refs_1_), channel_id=1, source_target_pairs={{1020,0},{1021,1},{6,2},{7,3},{0,4},{1,5},{10,6},{11,7},{4,8},{5,9... | collective-permute-start | bytes 663560 | tf_op jit(solution)/shard_map/ppermute | solution.py:22
  46.9 2.3 %collective-permute-done.5.refs_0_ = bf16[96,1152]{1,0:T(8,128)(2,1)S(1)} collective-permute-done((bf16[96,1152]{1,0:T(8,128)(2,1)S(1)}, bf16[96,1152]{1,0:T(8,128)(2,1)S(1)}, u32[]{:S(2)}, u32[]{:S(2)}) %collective-permute-start.5) | collective-permute-done | bytes 221216 | tf_op jit(solution)/shard_map/ppermute | solution.py:22
  49.2 1.9 %collective-permute-start.7 = (bf16[96,1152]{1,0:T(8,128)(2,1)S(1)}, bf16[96,1152]{1,0:T(8,128)(2,1)S(1)}, u32[]{:S(2)}, u32[]{:S(2)}) collective-permute-start(bf16[96,1152]{1,0:T(8,128)(2,1)S(1)} %collective-permute-done.3.refs_1_), channel_id=1, source_target_pairs={{16,0},{1009,1},{18,2},{1011,3},{20,4},{1013,5},{22,6},{1015,7},{2... | collective-permute-start | bytes 663560 | tf_op jit(solution)/shard_map/ppermute | solution.py:22
  51.3 1.9 %collective-permute-start.8 = (bf16[96,1152]{1,0:T(8,128)(2,1)S(1)}, bf16[96,1152]{1,0:T(8,128)(2,1)S(1)}, u32[]{:S(2)}, u32[]{:S(2)}) collective-permute-start(bf16[96,1152]{1,0:T(8,128)(2,1)S(1)} %collective-permute-done.6.refs_2_), channel_id=1, source_target_pairs={{16,0},{1009,1},{18,2},{1011,3},{20,4},{1013,5},{22,6},{1015,7},{2... | collective-permute-start | bytes 663560 | tf_op jit(solution)/shard_map/ppermute | solution.py:22
  53.2 0.9 shard_map.91.before
  54.1 4.9 %collective-permute-done.4.refs_0_ = bf16[96,1152]{1,0:T(8,128)(2,1)S(1)} collective-permute-done((bf16[96,1152]{1,0:T(8,128)(2,1)S(1)}, bf16[96,1152]{1,0:T(8,128)(2,1)S(1)}, u32[]{:S(2)}, u32[]{:S(2)}) %collective-permute-start.4) | collective-permute-done | bytes 221216 | tf_op jit(solution)/shard_map/ppermute | solution.py:22
  59.1 1.9 %collective-permute-start.9 = (bf16[96,1152]{1,0:T(8,128)(2,1)S(1)}, bf16[96,1152]{1,0:T(8,128)(2,1)S(1)}, u32[]{:S(2)}, u32[]{:S(2)}) collective-permute-start(bf16[96,1152]{1,0:T(8,128)(2,1)S(1)} %collective-permute-done.4.refs_0_), channel_id=1, source_target_pairs={{16,0},{1009,1},{18,2},{1011,3},{20,4},{1013,5},{22,6},{1015,7},{2... | collective-permute-start | bytes 663560 | tf_op jit(solution)/shard_map/ppermute | solution.py:22
  61.0 2.4 %collective-permute-done.8.refs_2_ = bf16[96,1152]{1,0:T(8,128)(2,1)S(1)} collective-permute-done((bf16[96,1152]{1,0:T(8,128)(2,1)S(1)}, bf16[96,1152]{1,0:T(8,128)(2,1)S(1)}, u32[]{:S(2)}, u32[]{:S(2)}) %collective-permute-start.8) | collective-permute-done | bytes 221216 | tf_op jit(solution)/shard_map/ppermute | solution.py:22
  63.4 0.9 shard_map.92.before
  64.3 4.7 %collective-permute-done.9.far_opposite = bf16[96,1152]{1,0:T(8,128)(2,1)S(1)} collective-permute-done((bf16[96,1152]{1,0:T(8,128)(2,1)S(1)}, bf16[96,1152]{1,0:T(8,128)(2,1)S(1)}, u32[]{:S(2)}, u32[]{:S(2)}) %collective-permute-start.9) | collective-permute-done | bytes 221216 | tf_op jit(solution)/shard_map/ppermute | solution.py:22
  69.0 1.0 %shard_map.93 = (f32[192,576]{1,0:T(8,128)S(1)}, bf16[864,128]{1,0:T(8,128)(2,1)S(1)}) custom-call(f32[2,128]{1,0:T(2,128)S(1)} %broadcast_in_dim.8.factors, bf16[192,1152]{1,0:T(8,128)(2,1)S(1)} %get-tuple-element.39.fixed, f32[192,1152]{1,0:T(8,128)S(1)} %shard_map.92.before, bf16[96,1152]{1,0:T(8,128)(2,1)S(1)} %collective-permute-done.9.far_opposite, ...), custom_call_target="tpu_custom_call" | custom-call | bytes 2434816 | tf_op jit(solution)/shard_map/pallas_call | solution.py:59
  70.0 1.9 %collective-permute-start.10 = (bf16[864,128]{1,0:T(8,128)(2,1)S(1)}, bf16[864,128]{1,0:T(8,128)(2,1)S(1)}, u32[]{:S(2)}, u32[]{:S(2)}) collective-permute-start(bf16[864,128]{1,0:T(8,128)(2,1)S(1)} %get-tuple-element.52), channel_id=1, source_target_pairs={{2,0},{3,1},{0,2},{1,3},{6,4},{7,5},{4,6},{5,7},{10,8},{11,9},{8,1... | collective-permute-start | bytes 663560 | tf_op jit(solution)/shard_map/ppermute | solution.py:22
  72.0 4.7 %collective-permute-done.10.got = bf16[864,128]{1,0:T(8,128)(2,1)S(1)} collective-permute-done((bf16[864,128]{1,0:T(8,128)(2,1)S(1)}, bf16[864,128]{1,0:T(8,128)(2,1)S(1)}, u32[]{:S(2)}, u32[]{:S(2)}) %collective-permute-start.10) | collective-permute-done | bytes 221216 | tf_op jit(solution)/shard_map/ppermute | solution.py:22
  76.7 1.2 %shard_map.94 = (bf16[432,128]{1,0:T(8,128)(2,1)S(1)}, bf16[432,128]{1,0:T(8,128)(2,1)S(1)}, bf16[432,128]{1,0:T(8,128)(2,1)S(1)}, f32[192,288]{1,0:T(8,128)S(1)}) custom-call(f32[192,576]{1,0:T(8,128)S(1)} %get-tuple-element.51.kept, bf16[864,128]{1,0:T(8,128)(2,1)S(1)} %collective-permute-done.10.got, bf16[288,1152]{1,0:T(8,128)(2,1)S(1)} %get-tuple-element.58.mine, ...), custom_call_target="tpu_custom_call" | custom-call | bytes 1990656 | tf_op jit(solution)/shard_map/pallas_call | solution.py:59
  77.9 1.9 %collective-permute-start.11 = (bf16[432,128]{1,0:T(8,128)(2,1)S(1)}, bf16[432,128]{1,0:T(8,128)(2,1)S(1)}, u32[]{:S(2)}, u32[]{:S(2)}) collective-permute-start(bf16[432,128]{1,0:T(8,128)(2,1)S(1)} %get-tuple-element.54), channel_id=1, source_target_pairs={{2,0},{3,1},{0,2},{1,3},{6,4},{7,5},{4,6},{5,7},{10,8},{11,9},{8,1... | collective-permute-start | bytes 331784 | tf_op jit(solution)/shard_map/ppermute | solution.py:22
  79.9 10.4 %collective-permute-start.12 = (bf16[432,128]{1,0:T(8,128)(2,1)S(1)}, bf16[432,128]{1,0:T(8,128)(2,1)S(1)}, u32[]{:S(2)}, u32[]{:S(2)}) collective-permute-start(bf16[432,128]{1,0:T(8,128)(2,1)S(1)} %get-tuple-element.55), channel_id=1, source_target_pairs={{3,0},{2,1},{1,2},{0,3},{7,4},{6,5},{5,6},{4,7},{11,8},{10,9},{9,1... | collective-permute-start | bytes 331784 | tf_op jit(solution)/shard_map/ppermute | solution.py:22
  90.3 1.9 %collective-permute-start.13 = (bf16[432,128]{1,0:T(8,128)(2,1)S(1)}, bf16[432,128]{1,0:T(8,128)(2,1)S(1)}, u32[]{:S(2)}, u32[]{:S(2)}) collective-permute-start(bf16[432,128]{1,0:T(8,128)(2,1)S(1)} %get-tuple-element.56), channel_id=1, source_target_pairs={{1,0},{0,1},{3,2},{2,3},{5,4},{4,5},{7,6},{6,7},{9,8},{8,9},{11,10... | collective-permute-start | bytes 331784 | tf_op jit(solution)/shard_map/ppermute | solution.py:22
  92.2 1.1 %collective-permute-done.12.from_cross = bf16[432,128]{1,0:T(8,128)(2,1)S(1)} collective-permute-done((bf16[432,128]{1,0:T(8,128)(2,1)S(1)}, bf16[432,128]{1,0:T(8,128)(2,1)S(1)}, u32[]{:S(2)}, u32[]{:S(2)}) %collective-permute-start.12) | collective-permute-done | bytes 110624 | tf_op jit(solution)/shard_map/ppermute | solution.py:22
  93.5 0.9 shard_map.95
  (28 shorter events, 2.5 us)
Async XLA Ops:
  0.6 1.0 %copy-start = (bf16[192,1152]{1,0:T(8,128)(2,1)S(1)}, bf16[192,1152]{1,0:T(8,128)(2,1)}, u32[]{:S(2)}) copy-start(bf16[192,1152]{1,0:T(8,128)(2,1)} %param.7) | copy-start | bytes 1327108
  0.6 2.5 %copy-start.2 = (bf16[1152,288]{0,1:T(8,128)(2,1)S(1)}, bf16[1152,288]{0,1:T(8,128)(2,1)}, u32[]{:S(2)}) copy-start(bf16[1152,288]{0,1:T(8,128)(2,1)} %param.10) | copy-start | bytes 1990660
  0.7 2.5 %copy-start.3 = (bf16[192,1152]{1,0:T(8,128)(2,1)S(1)}, bf16[192,1152]{1,0:T(8,128)(2,1)}, u32[]{:S(2)}) copy-start(bf16[192,1152]{1,0:T(8,128)(2,1)} %param.9) | copy-start | bytes 1327108
  3.7 4.4 %copy-start.1 = (bf16[1152,288]{0,1:T(8,128)(2,1)S(1)}, bf16[1152,288]{0,1:T(8,128)(2,1)}, u32[]{:S(2)}) copy-start(bf16[1152,288]{0,1:T(8,128)(2,1)} %param.8) | copy-start | bytes 1990660
  3.9 19.9 %collective-permute-start = (f16[864,128]{1,0:T(8,128)(2,1)S(1)}, f16[864,128]{1,0:T(8,128)(2,1)S(1)}, u32[]{:S(2)}, u32[]{:S(2)}) collective-permute-start(f16[864,128]{1,0:T(8,128)(2,1)S(1)} %convert_element_type.12), channel_id=1, source_target_pairs={{2,0},{3,1},{0,2},{1,3},{6,4},{7,5},{4,6},{5,7},{10,8},{11,9},{8,1... | collective-permute-start | bytes 663560 | tf_op jit(solution)/shard_map/ppermute | solution.py:22
  9.1 19.1 %collective-permute-start.2 = (bf16[288,1152]{1,0:T(8,128)(2,1)}, bf16[288,1152]{1,0:T(8,128)(2,1)S(1)}, u32[]{:S(2)}, u32[]{:S(2)}) collective-permute-start(bf16[288,1152]{1,0:T(8,128)(2,1)} %get-tuple-element.59), channel_id=1, source_target_pairs={{1,0},{0,1},{3,2},{2,3},{5,4},{4,5},{7,6},{6,7},{9,8},{8,9},{11,10... | collective-permute-start | bytes 1990664 | tf_op jit(solution)/shard_map/ppermute | solution.py:22
  22.9 0.7 copy-start.4
  24.1 5.5 %collective-permute-start.1 = (f16[384,640]{1,0:T(8,128)(2,1)S(1)}, f16[384,640]{1,0:T(8,128)(2,1)S(1)}, u32[]{:S(2)}, u32[]{:S(2)}) collective-permute-start(f16[384,640]{1,0:T(8,128)(2,1)S(1)} %convert_element_type.14), channel_id=1, source_target_pairs={{1,0},{0,1},{3,2},{2,3},{5,4},{4,5},{7,6},{6,7},{9,8},{8,9},{11,10... | collective-permute-start | bytes 1474568 | tf_op jit(solution)/shard_map/ppermute | solution.py:22
  29.9 15.1 %collective-permute-start.3 = (bf16[96,1152]{1,0:T(8,128)(2,1)S(1)}, bf16[96,1152]{1,0:T(8,128)(2,1)S(1)}, u32[]{:S(2)}, u32[]{:S(2)}) collective-permute-start(bf16[96,1152]{1,0:T(8,128)(2,1)S(1)} %shard_map.88), channel_id=1, source_target_pairs={{14,0},{1023,1},{4,2},{1013,3},{18,4},{3,5},{8,6},{1017,7},{22,8},... | collective-permute-start | bytes 663560 | tf_op jit(solution)/shard_map/ppermute | solution.py:22
  33.7 15.5 %collective-permute-start.5 = (bf16[96,1152]{1,0:T(8,128)(2,1)S(1)}, bf16[96,1152]{1,0:T(8,128)(2,1)S(1)}, u32[]{:S(2)}, u32[]{:S(2)}) collective-permute-start(bf16[96,1152]{1,0:T(8,128)(2,1)S(1)} %get-tuple-element.42.own_half), channel_id=1, source_target_pairs={{16,0},{1009,1},{18,2},{1011,3},{20,4},{1013,5},{22,6},{1015,7},{2... | collective-permute-start | bytes 663560 | tf_op jit(solution)/shard_map/ppermute | solution.py:22
  35.6 15.7 %collective-permute-start.6 = (bf16[96,1152]{1,0:T(8,128)(2,1)S(1)}, bf16[96,1152]{1,0:T(8,128)(2,1)S(1)}, u32[]{:S(2)}, u32[]{:S(2)}) collective-permute-start(bf16[96,1152]{1,0:T(8,128)(2,1)S(1)} %get-tuple-element.42.own_half), channel_id=1, source_target_pairs={{14,0},{1023,1},{4,2},{1013,3},{18,4},{3,5},{8,6},{1017,7},{22,8},... | collective-permute-start | bytes 663560 | tf_op jit(solution)/shard_map/ppermute | solution.py:22
  44.9 14.1 %collective-permute-start.4 = (bf16[96,1152]{1,0:T(8,128)(2,1)S(1)}, bf16[96,1152]{1,0:T(8,128)(2,1)S(1)}, u32[]{:S(2)}, u32[]{:S(2)}) collective-permute-start(bf16[96,1152]{1,0:T(8,128)(2,1)S(1)} %collective-permute-done.3.refs_1_), channel_id=1, source_target_pairs={{1020,0},{1021,1},{6,2},{7,3},{0,4},{1,5},{10,6},{11,7},{4,8},{5,9... | collective-permute-start | bytes 663560 | tf_op jit(solution)/shard_map/ppermute | solution.py:22
  49.2 11.8 %collective-permute-start.7 = (bf16[96,1152]{1,0:T(8,128)(2,1)S(1)}, bf16[96,1152]{1,0:T(8,128)(2,1)S(1)}, u32[]{:S(2)}, u32[]{:S(2)}) collective-permute-start(bf16[96,1152]{1,0:T(8,128)(2,1)S(1)} %collective-permute-done.3.refs_1_), channel_id=1, source_target_pairs={{16,0},{1009,1},{18,2},{1011,3},{20,4},{1013,5},{22,6},{1015,7},{2... | collective-permute-start | bytes 663560 | tf_op jit(solution)/shard_map/ppermute | solution.py:22
  51.3 12.1 %collective-permute-start.8 = (bf16[96,1152]{1,0:T(8,128)(2,1)S(1)}, bf16[96,1152]{1,0:T(8,128)(2,1)S(1)}, u32[]{:S(2)}, u32[]{:S(2)}) collective-permute-start(bf16[96,1152]{1,0:T(8,128)(2,1)S(1)} %collective-permute-done.6.refs_2_), channel_id=1, source_target_pairs={{16,0},{1009,1},{18,2},{1011,3},{20,4},{1013,5},{22,6},{1015,7},{2... | collective-permute-start | bytes 663560 | tf_op jit(solution)/shard_map/ppermute | solution.py:22
  59.1 10.0 %collective-permute-start.9 = (bf16[96,1152]{1,0:T(8,128)(2,1)S(1)}, bf16[96,1152]{1,0:T(8,128)(2,1)S(1)}, u32[]{:S(2)}, u32[]{:S(2)}) collective-permute-start(bf16[96,1152]{1,0:T(8,128)(2,1)S(1)} %collective-permute-done.4.refs_0_), channel_id=1, source_target_pairs={{16,0},{1009,1},{18,2},{1011,3},{20,4},{1013,5},{22,6},{1015,7},{2... | collective-permute-start | bytes 663560 | tf_op jit(solution)/shard_map/ppermute | solution.py:22
  70.0 6.7 %collective-permute-start.10 = (bf16[864,128]{1,0:T(8,128)(2,1)S(1)}, bf16[864,128]{1,0:T(8,128)(2,1)S(1)}, u32[]{:S(2)}, u32[]{:S(2)}) collective-permute-start(bf16[864,128]{1,0:T(8,128)(2,1)S(1)} %get-tuple-element.52), channel_id=1, source_target_pairs={{2,0},{3,1},{0,2},{1,3},{6,4},{7,5},{4,6},{5,7},{10,8},{11,9},{8,1... | collective-permute-start | bytes 663560 | tf_op jit(solution)/shard_map/ppermute | solution.py:22
  77.9 14.3 %collective-permute-start.11 = (bf16[432,128]{1,0:T(8,128)(2,1)S(1)}, bf16[432,128]{1,0:T(8,128)(2,1)S(1)}, u32[]{:S(2)}, u32[]{:S(2)}) collective-permute-start(bf16[432,128]{1,0:T(8,128)(2,1)S(1)} %get-tuple-element.54), channel_id=1, source_target_pairs={{2,0},{3,1},{0,2},{1,3},{6,4},{7,5},{4,6},{5,7},{10,8},{11,9},{8,1... | collective-permute-start | bytes 331784 | tf_op jit(solution)/shard_map/ppermute | solution.py:22
  79.9 13.4 %collective-permute-start.12 = (bf16[432,128]{1,0:T(8,128)(2,1)S(1)}, bf16[432,128]{1,0:T(8,128)(2,1)S(1)}, u32[]{:S(2)}, u32[]{:S(2)}) collective-permute-start(bf16[432,128]{1,0:T(8,128)(2,1)S(1)} %get-tuple-element.55), channel_id=1, source_target_pairs={{3,0},{2,1},{1,2},{0,3},{7,4},{6,5},{5,6},{4,7},{11,8},{10,9},{9,1... | collective-permute-start | bytes 331784 | tf_op jit(solution)/shard_map/ppermute | solution.py:22
  90.3 3.2 %collective-permute-start.13 = (bf16[432,128]{1,0:T(8,128)(2,1)S(1)}, bf16[432,128]{1,0:T(8,128)(2,1)S(1)}, u32[]{:S(2)}, u32[]{:S(2)}) collective-permute-start(bf16[432,128]{1,0:T(8,128)(2,1)S(1)} %get-tuple-element.56), channel_id=1, source_target_pairs={{1,0},{0,1},{3,2},{2,3},{5,4},{4,5},{7,6},{6,7},{9,8},{8,9},{11,10... | collective-permute-start | bytes 331784 | tf_op jit(solution)/shard_map/ppermute | solution.py:22

commit v6 on v5

--- a/solution.py
+++ b/solution.py
@@ -187,8 +187,10 @@
     return jnp.dot(weight.astype(BF16), block, preferred_element_type=F32)
 
 
-def first_sum(factors, fixed, sign, own_half, total):
-    total[...] = pull(factors, fixed[...], own_half[...], sign[...])
+def first_sum(factors, fixed, sign, own_half, *refs):
+    a = fixed[...]
+    block = jnp.concatenate([x[...] for x in refs[:-1]], axis=0)
+    refs[-1][...] = pull(factors, a, own_half[...], sign[...]) + pull(factors, a, block)
 
 
 def next_sum(factors, fixed, before, *refs):
@@ -315,16 +317,14 @@
     near_relayed = exchange(other_half, groups, neighbour)
     far_own = exchange(own_half, groups, beyond)
     near_other = exchange(own_half, groups, neighbour)
-    (total,) = call(first_sum, sums, factors, fixed, sign, own_half)
-    near_relayed, total = lax.optimization_barrier((near_relayed, total))
     opposite = exchange(near_relayed, groups, relay)
+    (total,) = call(first_sum, sums, factors, fixed, sign, own_half, near_relayed)
     far_own, near_sent = lax.optimization_barrier((far_own, near_relayed))
     far_relayed = exchange(near_sent, groups, beyond)
+    near_other, total = lax.optimization_barrier((near_other, total))
     far_other = exchange(near_other, groups, beyond)
-    (total,) = call(next_sum, sums, factors, fixed, total, far_own, near_relayed, near_other)
-    opposite, total = lax.optimization_barrier((opposite, total))
     far_opposite = exchange(opposite, groups, beyond)
-    (total,) = call(next_sum, sums, factors, fixed, total, opposite, far_relayed, far_other)
+    (total,) = call(next_sum, sums, factors, fixed, total, far_own, near_other, opposite, far_relayed, far_other)
     keep, give = call(
         last_sum,
         [((rows, 2 * span), F32), ((packed_rows(rows, 2 * span), LANES), BF16)],

time: 95 us -> 93.7 us (0.986)
  starting transfers between devices: 51.5 us -> 49.3 us
  waiting for transfers between devices: 28.7 us -> 30.5 us
    ppermute x14, starting transfers between devices: 51.5 us -> 49.3 us  [exchange(): return lax.ppermute(block, AXES, route)]
    ppermute x14, waiting for transfers between devices: 28.7 us -> 30.5 us  [exchange(): return lax.ppermute(block, AXES, route)]
    pallas_call x10 -> x9, Pallas kernels: 6.76 us -> 5.92 us  [call(): pl.pallas_call(kernel, cost_estimate=pl.CostEstimate(flops=flops, bytes_a...]
  transfers between devices with their start and end apart: 14 -> 14, of which waited for: 10 -> 8; matrix products, arithmetic and copies ran while one was open for 2% -> 2% of each run, Pallas kernels for 3% -> 3%
where the time goes in v6:
time: 93.7 us; the launch traced here: 93.2 us
  starting transfers between devices  49.3 us (53%)
  waiting for transfers between devices  30.5 us (33%)
  Pallas kernels  5.92 us (6%)
  between operations  2.27 us (2%)
  matrix products  1.98 us (2%)
  local copies, waits for them, and re-layouts  1.74 us (2%)
  other arithmetic  1.45 us (2%)
    ppermute x14, starting transfers between devices, exchange(): return lax.ppermute(block, AXES, route)  49.3 us
    ppermute x14, waiting for transfers between devices, exchange(): return lax.ppermute(block, AXES, route)  30.5 us
    pallas_call x9, Pallas kernels, call(): pl.pallas_call(kernel, cost_estimate=pl.CostEstimate(flops=flops, bytes_a...  5.92 us
  transfers between devices with their start and end apart: 14, of which 8 were waited for; matrix products, arithmetic and copies ran while one was open for 2% of the time, Pallas kernels for 3%

profile of v6, /device:TPU:1, one launch (start us, length us, event | category | flops | bytes accessed | tf_op | source)
XLA Modules:
  0.0 93.2 jit_solution(15620697796556180547)
XLA Ops:
  0.7 1.0 %copy-done = bf16[192,1152]{1,0:T(8,128)(2,1)S(1)} copy-done((bf16[192,1152]{1,0:T(8,128)(2,1)S(1)}, bf16[192,1152]{1,0:T(8,128)(2,1)}, u32[]{:S(2)}) %copy-start) | copy-done | bytes 442392
  1.6 1.5 %fusion.img = f32[192,288]{1,0:T(8,128)S(1)} fusion(bf16[192,1152]{1,0:T(8,128)(2,1)S(1)} %copy-done, bf16[1152,288]{0,1:T(8,128)(2,1)} %param.8), kind=kOutput, calls=%fused_computation.7 | convolution fusion | flops 127401984 | bytes 1327104 | tf_op jit(solution)/shard_map/dot_general | solution.py:269
  3.2 0.4 fusion.1.txt
  3.9 4.1 %collective-permute-start = (f16[864,128]{1,0:T(8,128)(2,1)S(1)}, f16[864,128]{1,0:T(8,128)(2,1)S(1)}, u32[]{:S(2)}, u32[]{:S(2)}) collective-permute-start(f16[864,128]{1,0:T(8,128)(2,1)S(1)} %convert_element_type.12), channel_id=1, source_target_pairs={{2,0},{3,1},{0,2},{1,3},{6,4},{7,5},{4,6},{5,7},{10,8},{11,9},{8,1... | collective-permute-start | bytes 663560 | tf_op jit(solution)/shard_map/ppermute | solution.py:22
  8.1 1.0 %broadcast_select_fusion = (bf16[288,1152]{1,0:T(8,128)(2,1)S(1)}, bf16[288,1152]{1,0:T(8,128)(2,1)}) fusion(bf16[288,1152]{1,0:T(8,128)(2,1)S(1)} %bitcast.6, bf16[288,1152]{1,0:T(8,128)(2,1)S(1)} %bitcast.7, pred[]{:T(512)S(6)} %eq.16), kind=kLoop, calls=%fused_computation | loop fusion | flops 663552 | bytes 2654209 | tf_op jit(solution)/shard_map/jit(_where)/select_n | solution.py:287
  9.1 13.8 %collective-permute-start.2 = (bf16[288,1152]{1,0:T(8,128)(2,1)}, bf16[288,1152]{1,0:T(8,128)(2,1)S(1)}, u32[]{:S(2)}, u32[]{:S(2)}) collective-permute-start(bf16[288,1152]{1,0:T(8,128)(2,1)} %get-tuple-element.55), channel_id=1, source_target_pairs={{1,0},{0,1},{3,2},{2,3},{5,4},{4,5},{7,6},{6,7},{9,8},{8,9},{11,10... | collective-permute-start | bytes 1990664 | tf_op jit(solution)/shard_map/ppermute | solution.py:22
  22.9 0.7 copy-done.4
  24.1 4.0 %collective-permute-start.1 = (f16[384,640]{1,0:T(8,128)(2,1)S(1)}, f16[384,640]{1,0:T(8,128)(2,1)S(1)}, u32[]{:S(2)}, u32[]{:S(2)}) collective-permute-start(f16[384,640]{1,0:T(8,128)(2,1)S(1)} %convert_element_type.14), channel_id=1, source_target_pairs={{1,0},{0,1},{3,2},{2,3},{5,4},{4,5},{7,6},{6,7},{9,8},{8,9},{11,10... | collective-permute-start | bytes 1474568 | tf_op jit(solution)/shard_map/ppermute | solution.py:22
  28.1 1.5 %collective-permute-done.1 = f16[384,640]{1,0:T(8,128)(2,1)S(1)} collective-permute-done((f16[384,640]{1,0:T(8,128)(2,1)S(1)}, f16[384,640]{1,0:T(8,128)(2,1)S(1)}, u32[]{:S(2)}, u32[]{:S(2)}) %collective-permute-start.1) | collective-permute-done | bytes 491552 | tf_op jit(solution)/shard_map/ppermute | solution.py:22
  29.9 1.9 %collective-permute-start.4 = (bf16[96,1152]{1,0:T(8,128)(2,1)S(1)}, bf16[96,1152]{1,0:T(8,128)(2,1)S(1)}, u32[]{:S(2)}, u32[]{:S(2)}) collective-permute-start(bf16[96,1152]{1,0:T(8,128)(2,1)S(1)} %shard_map.88), channel_id=1, source_target_pairs={{14,0},{1023,1},{4,2},{1013,3},{18,4},{3,5},{8,6},{1017,7},{22,8},... | collective-permute-start | bytes 663560 | tf_op jit(solution)/shard_map/ppermute | solution.py:22
  31.8 0.5 shard_map.89
  32.3 1.9 %collective-permute-start.5 = (bf16[96,1152]{1,0:T(8,128)(2,1)S(1)}, bf16[96,1152]{1,0:T(8,128)(2,1)S(1)}, u32[]{:S(2)}, u32[]{:S(2)}) collective-permute-start(bf16[96,1152]{1,0:T(8,128)(2,1)S(1)} %get-tuple-element.38.own_half), channel_id=1, source_target_pairs={{16,0},{1009,1},{18,2},{1011,3},{20,4},{1013,5},{22,6},{1015,7},{2... | collective-permute-start | bytes 663560 | tf_op jit(solution)/shard_map/ppermute | solution.py:22
  34.3 1.9 %collective-permute-start.3 = (bf16[96,1152]{1,0:T(8,128)(2,1)S(1)}, bf16[96,1152]{1,0:T(8,128)(2,1)S(1)}, u32[]{:S(2)}, u32[]{:S(2)}) collective-permute-start(bf16[96,1152]{1,0:T(8,128)(2,1)S(1)} %get-tuple-element.38.own_half), channel_id=1, source_target_pairs={{14,0},{1023,1},{4,2},{1013,3},{18,4},{3,5},{8,6},{1017,7},{22,8},... | collective-permute-start | bytes 663560 | tf_op jit(solution)/shard_map/ppermute | solution.py:22
  36.2 8.7 %collective-permute-done.4.refs_0_ = bf16[96,1152]{1,0:T(8,128)(2,1)S(1)} collective-permute-done((bf16[96,1152]{1,0:T(8,128)(2,1)S(1)}, bf16[96,1152]{1,0:T(8,128)(2,1)S(1)}, u32[]{:S(2)}, u32[]{:S(2)}) %collective-permute-start.4) | collective-permute-done | bytes 221216 | tf_op jit(solution)/shard_map/ppermute | solution.py:22
  44.9 1.9 %collective-permute-start.6 = (bf16[96,1152]{1,0:T(8,128)(2,1)S(1)}, bf16[96,1152]{1,0:T(8,128)(2,1)S(1)}, u32[]{:S(2)}, u32[]{:S(2)}) collective-permute-start(bf16[96,1152]{1,0:T(8,128)(2,1)S(1)} %collective-permute-done.4.refs_0_), channel_id=1, source_target_pairs={{1020,0},{1021,1},{6,2},{7,3},{0,4},{1,5},{10,6},{11,7},{4,8},{5,9... | collective-permute-start | bytes 663560 | tf_op jit(solution)/shard_map/ppermute | solution.py:22
  48.2 1.9 %collective-permute-start.7 = (bf16[96,1152]{1,0:T(8,128)(2,1)S(1)}, bf16[96,1152]{1,0:T(8,128)(2,1)S(1)}, u32[]{:S(2)}, u32[]{:S(2)}) collective-permute-start(bf16[96,1152]{1,0:T(8,128)(2,1)S(1)} %collective-permute-done.4.refs_0_), channel_id=1, source_target_pairs={{16,0},{1009,1},{18,2},{1011,3},{20,4},{1013,5},{22,6},{1015,7},{2... | collective-permute-start | bytes 663560 | tf_op jit(solution)/shard_map/ppermute | solution.py:22
  50.2 0.8 shard_map.90.before
  51.0 1.9 %collective-permute-start.8 = (bf16[96,1152]{1,0:T(8,128)(2,1)S(1)}, bf16[96,1152]{1,0:T(8,128)(2,1)S(1)}, u32[]{:S(2)}, u32[]{:S(2)}) collective-permute-start(bf16[96,1152]{1,0:T(8,128)(2,1)S(1)} %collective-permute-done.3.refs_1_), channel_id=1, source_target_pairs={{16,0},{1009,1},{18,2},{1011,3},{20,4},{1013,5},{22,6},{1015,7},{2... | collective-permute-start | bytes 663560 | tf_op jit(solution)/shard_map/ppermute | solution.py:22
  52.9 7.1 %collective-permute-done.6.refs_2_ = bf16[96,1152]{1,0:T(8,128)(2,1)S(1)} collective-permute-done((bf16[96,1152]{1,0:T(8,128)(2,1)S(1)}, bf16[96,1152]{1,0:T(8,128)(2,1)S(1)}, u32[]{:S(2)}, u32[]{:S(2)}) %collective-permute-start.6) | collective-permute-done | bytes 221216 | tf_op jit(solution)/shard_map/ppermute | solution.py:22
  60.0 1.9 %collective-permute-start.9 = (bf16[96,1152]{1,0:T(8,128)(2,1)S(1)}, bf16[96,1152]{1,0:T(8,128)(2,1)S(1)}, u32[]{:S(2)}, u32[]{:S(2)}) collective-permute-start(bf16[96,1152]{1,0:T(8,128)(2,1)S(1)} %collective-permute-done.6.refs_2_), channel_id=1, source_target_pairs={{16,0},{1009,1},{18,2},{1011,3},{20,4},{1013,5},{22,6},{1015,7},{2... | collective-permute-start | bytes 663560 | tf_op jit(solution)/shard_map/ppermute | solution.py:22
  62.0 2.5 %collective-permute-done.8.refs_4_ = bf16[96,1152]{1,0:T(8,128)(2,1)S(1)} collective-permute-done((bf16[96,1152]{1,0:T(8,128)(2,1)S(1)}, bf16[96,1152]{1,0:T(8,128)(2,1)S(1)}, u32[]{:S(2)}, u32[]{:S(2)}) %collective-permute-start.8) | collective-permute-done | bytes 221216 | tf_op jit(solution)/shard_map/ppermute | solution.py:22
  64.4 0.9 shard_map.91.before
  65.3 4.7 %collective-permute-done.9.far_opposite = bf16[96,1152]{1,0:T(8,128)(2,1)S(1)} collective-permute-done((bf16[96,1152]{1,0:T(8,128)(2,1)S(1)}, bf16[96,1152]{1,0:T(8,128)(2,1)S(1)}, u32[]{:S(2)}, u32[]{:S(2)}) %collective-permute-start.9) | collective-permute-done | bytes 221216 | tf_op jit(solution)/shard_map/ppermute | solution.py:22
  70.0 1.0 %shard_map.92 = (f32[192,576]{1,0:T(8,128)S(1)}, bf16[864,128]{1,0:T(8,128)(2,1)S(1)}) custom-call(f32[2,128]{1,0:T(2,128)S(1)} %broadcast_in_dim.8.factors, bf16[192,1152]{1,0:T(8,128)(2,1)S(1)} %get-tuple-element.37.fixed, f32[192,1152]{1,0:T(8,128)S(1)} %shard_map.91.before, bf16[96,1152]{1,0:T(8,128)(2,1)S(1)} %collective-permute-done.9.far_opposite, ...), custom_call_target="tpu_custom_call" | custom-call | bytes 2434816 | tf_op jit(solution)/shard_map/pallas_call | solution.py:59
  71.0 1.9 %collective-permute-start.10 = (bf16[864,128]{1,0:T(8,128)(2,1)S(1)}, bf16[864,128]{1,0:T(8,128)(2,1)S(1)}, u32[]{:S(2)}, u32[]{:S(2)}) collective-permute-start(bf16[864,128]{1,0:T(8,128)(2,1)S(1)} %get-tuple-element.48), channel_id=1, source_target_pairs={{2,0},{3,1},{0,2},{1,3},{6,4},{7,5},{4,6},{5,7},{10,8},{11,9},{8,1... | collective-permute-start | bytes 663560 | tf_op jit(solution)/shard_map/ppermute | solution.py:22
  72.9 4.7 %collective-permute-done.10.got = bf16[864,128]{1,0:T(8,128)(2,1)S(1)} collective-permute-done((bf16[864,128]{1,0:T(8,128)(2,1)S(1)}, bf16[864,128]{1,0:T(8,128)(2,1)S(1)}, u32[]{:S(2)}, u32[]{:S(2)}) %collective-permute-start.10) | collective-permute-done | bytes 221216 | tf_op jit(solution)/shard_map/ppermute | solution.py:22
  77.7 1.2 %shard_map.93 = (bf16[432,128]{1,0:T(8,128)(2,1)S(1)}, bf16[432,128]{1,0:T(8,128)(2,1)S(1)}, bf16[432,128]{1,0:T(8,128)(2,1)S(1)}, f32[192,288]{1,0:T(8,128)S(1)}) custom-call(f32[192,576]{1,0:T(8,128)S(1)} %get-tuple-element.47.kept, bf16[864,128]{1,0:T(8,128)(2,1)S(1)} %collective-permute-done.10.got, bf16[288,1152]{1,0:T(8,128)(2,1)S(1)} %get-tuple-element.54.mine, ...), custom_call_target="tpu_custom_call" | custom-call | bytes 1990656 | tf_op jit(solution)/shard_map/pallas_call | solution.py:59
  78.9 1.9 %collective-permute-start.11 = (bf16[432,128]{1,0:T(8,128)(2,1)S(1)}, bf16[432,128]{1,0:T(8,128)(2,1)S(1)}, u32[]{:S(2)}, u32[]{:S(2)}) collective-permute-start(bf16[432,128]{1,0:T(8,128)(2,1)S(1)} %get-tuple-element.50), channel_id=1, source_target_pairs={{2,0},{3,1},{0,2},{1,3},{6,4},{7,5},{4,6},{5,7},{10,8},{11,9},{8,1... | collective-permute-start | bytes 331784 | tf_op jit(solution)/shard_map/ppermute | solution.py:22
  80.8 8.2 %collective-permute-start.12 = (bf16[432,128]{1,0:T(8,128)(2,1)S(1)}, bf16[432,128]{1,0:T(8,128)(2,1)S(1)}, u32[]{:S(2)}, u32[]{:S(2)}) collective-permute-start(bf16[432,128]{1,0:T(8,128)(2,1)S(1)} %get-tuple-element.51), channel_id=1, source_target_pairs={{3,0},{2,1},{1,2},{0,3},{7,4},{6,5},{5,6},{4,7},{11,8},{10,9},{9,1... | collective-permute-start | bytes 331784 | tf_op jit(solution)/shard_map/ppermute | solution.py:22
  89.0 1.9 %collective-permute-start.13 = (bf16[432,128]{1,0:T(8,128)(2,1)S(1)}, bf16[432,128]{1,0:T(8,128)(2,1)S(1)}, u32[]{:S(2)}, u32[]{:S(2)}) collective-permute-start(bf16[432,128]{1,0:T(8,128)(2,1)S(1)} %get-tuple-element.52), channel_id=1, source_target_pairs={{1,0},{0,1},{3,2},{2,3},{5,4},{4,5},{7,6},{6,7},{9,8},{8,9},{11,10... | collective-permute-start | bytes 331784 | tf_op jit(solution)/shard_map/ppermute | solution.py:22
  91.0 1.1 %collective-permute-done.12.from_cross = bf16[432,128]{1,0:T(8,128)(2,1)S(1)} collective-permute-done((bf16[432,128]{1,0:T(8,128)(2,1)S(1)}, bf16[432,128]{1,0:T(8,128)(2,1)S(1)}, u32[]{:S(2)}, u32[]{:S(2)}) %collective-permute-start.12) | collective-permute-done | bytes 110624 | tf_op jit(solution)/shard_map/ppermute | solution.py:22
  92.2 0.9 shard_map.94
  (27 shorter events, 1.4 us)
Async XLA Ops:
  0.6 1.0 %copy-start = (bf16[192,1152]{1,0:T(8,128)(2,1)S(1)}, bf16[192,1152]{1,0:T(8,128)(2,1)}, u32[]{:S(2)}) copy-start(bf16[192,1152]{1,0:T(8,128)(2,1)} %param.7) | copy-start | bytes 1327108
  0.6 2.5 %copy-start.2 = (bf16[1152,288]{0,1:T(8,128)(2,1)S(1)}, bf16[1152,288]{0,1:T(8,128)(2,1)}, u32[]{:S(2)}) copy-start(bf16[1152,288]{0,1:T(8,128)(2,1)} %param.10) | copy-start | bytes 1990660
  0.7 2.5 %copy-start.3 = (bf16[192,1152]{1,0:T(8,128)(2,1)S(1)}, bf16[192,1152]{1,0:T(8,128)(2,1)}, u32[]{:S(2)}) copy-start(bf16[192,1152]{1,0:T(8,128)(2,1)} %param.9) | copy-start | bytes 1327108
  3.7 4.4 %copy-start.1 = (bf16[1152,288]{0,1:T(8,128)(2,1)S(1)}, bf16[1152,288]{0,1:T(8,128)(2,1)}, u32[]{:S(2)}) copy-start(bf16[1152,288]{0,1:T(8,128)(2,1)} %param.8) | copy-start | bytes 1990660
  3.9 19.9 %collective-permute-start = (f16[864,128]{1,0:T(8,128)(2,1)S(1)}, f16[864,128]{1,0:T(8,128)(2,1)S(1)}, u32[]{:S(2)}, u32[]{:S(2)}) collective-permute-start(f16[864,128]{1,0:T(8,128)(2,1)S(1)} %convert_element_type.12), channel_id=1, source_target_pairs={{2,0},{3,1},{0,2},{1,3},{6,4},{7,5},{4,6},{5,7},{10,8},{11,9},{8,1... | collective-permute-start | bytes 663560 | tf_op jit(solution)/shard_map/ppermute | solution.py:22
  9.1 19.1 %collective-permute-start.2 = (bf16[288,1152]{1,0:T(8,128)(2,1)}, bf16[288,1152]{1,0:T(8,128)(2,1)S(1)}, u32[]{:S(2)}, u32[]{:S(2)}) collective-permute-start(bf16[288,1152]{1,0:T(8,128)(2,1)} %get-tuple-element.55), channel_id=1, source_target_pairs={{1,0},{0,1},{3,2},{2,3},{5,4},{4,5},{7,6},{6,7},{9,8},{8,9},{11,10... | collective-permute-start | bytes 1990664 | tf_op jit(solution)/shard_map/ppermute | solution.py:22
  22.9 0.7 copy-start.4
  24.1 5.5 %collective-permute-start.1 = (f16[384,640]{1,0:T(8,128)(2,1)S(1)}, f16[384,640]{1,0:T(8,128)(2,1)S(1)}, u32[]{:S(2)}, u32[]{:S(2)}) collective-permute-start(f16[384,640]{1,0:T(8,128)(2,1)S(1)} %convert_element_type.14), channel_id=1, source_target_pairs={{1,0},{0,1},{3,2},{2,3},{5,4},{4,5},{7,6},{6,7},{9,8},{8,9},{11,10... | collective-permute-start | bytes 1474568 | tf_op jit(solution)/shard_map/ppermute | solution.py:22
  29.9 15.1 %collective-permute-start.4 = (bf16[96,1152]{1,0:T(8,128)(2,1)S(1)}, bf16[96,1152]{1,0:T(8,128)(2,1)S(1)}, u32[]{:S(2)}, u32[]{:S(2)}) collective-permute-start(bf16[96,1152]{1,0:T(8,128)(2,1)S(1)} %shard_map.88), channel_id=1, source_target_pairs={{14,0},{1023,1},{4,2},{1013,3},{18,4},{3,5},{8,6},{1017,7},{22,8},... | collective-permute-start | bytes 663560 | tf_op jit(solution)/shard_map/ppermute | solution.py:22
  32.3 15.9 %collective-permute-start.5 = (bf16[96,1152]{1,0:T(8,128)(2,1)S(1)}, bf16[96,1152]{1,0:T(8,128)(2,1)S(1)}, u32[]{:S(2)}, u32[]{:S(2)}) collective-permute-start(bf16[96,1152]{1,0:T(8,128)(2,1)S(1)} %get-tuple-element.38.own_half), channel_id=1, source_target_pairs={{16,0},{1009,1},{18,2},{1011,3},{20,4},{1013,5},{22,6},{1015,7},{2... | collective-permute-start | bytes 663560 | tf_op jit(solution)/shard_map/ppermute | solution.py:22
  34.3 16.7 %collective-permute-start.3 = (bf16[96,1152]{1,0:T(8,128)(2,1)S(1)}, bf16[96,1152]{1,0:T(8,128)(2,1)S(1)}, u32[]{:S(2)}, u32[]{:S(2)}) collective-permute-start(bf16[96,1152]{1,0:T(8,128)(2,1)S(1)} %get-tuple-element.38.own_half), channel_id=1, source_target_pairs={{14,0},{1023,1},{4,2},{1013,3},{18,4},{3,5},{8,6},{1017,7},{22,8},... | collective-permute-start | bytes 663560 | tf_op jit(solution)/shard_map/ppermute | solution.py:22
  44.9 15.1 %collective-permute-start.6 = (bf16[96,1152]{1,0:T(8,128)(2,1)S(1)}, bf16[96,1152]{1,0:T(8,128)(2,1)S(1)}, u32[]{:S(2)}, u32[]{:S(2)}) collective-permute-start(bf16[96,1152]{1,0:T(8,128)(2,1)S(1)} %collective-permute-done.4.refs_0_), channel_id=1, source_target_pairs={{1020,0},{1021,1},{6,2},{7,3},{0,4},{1,5},{10,6},{11,7},{4,8},{5,9... | collective-permute-start | bytes 663560 | tf_op jit(solution)/shard_map/ppermute | solution.py:22
  48.2 13.7 %collective-permute-start.7 = (bf16[96,1152]{1,0:T(8,128)(2,1)S(1)}, bf16[96,1152]{1,0:T(8,128)(2,1)S(1)}, u32[]{:S(2)}, u32[]{:S(2)}) collective-permute-start(bf16[96,1152]{1,0:T(8,128)(2,1)S(1)} %collective-permute-done.4.refs_0_), channel_id=1, source_target_pairs={{16,0},{1009,1},{18,2},{1011,3},{20,4},{1013,5},{22,6},{1015,7},{2... | collective-permute-start | bytes 663560 | tf_op jit(solution)/shard_map/ppermute | solution.py:22
  51.0 13.4 %collective-permute-start.8 = (bf16[96,1152]{1,0:T(8,128)(2,1)S(1)}, bf16[96,1152]{1,0:T(8,128)(2,1)S(1)}, u32[]{:S(2)}, u32[]{:S(2)}) collective-permute-start(bf16[96,1152]{1,0:T(8,128)(2,1)S(1)} %collective-permute-done.3.refs_1_), channel_id=1, source_target_pairs={{16,0},{1009,1},{18,2},{1011,3},{20,4},{1013,5},{22,6},{1015,7},{2... | collective-permute-start | bytes 663560 | tf_op jit(solution)/shard_map/ppermute | solution.py:22
  60.0 10.0 %collective-permute-start.9 = (bf16[96,1152]{1,0:T(8,128)(2,1)S(1)}, bf16[96,1152]{1,0:T(8,128)(2,1)S(1)}, u32[]{:S(2)}, u32[]{:S(2)}) collective-permute-start(bf16[96,1152]{1,0:T(8,128)(2,1)S(1)} %collective-permute-done.6.refs_2_), channel_id=1, source_target_pairs={{16,0},{1009,1},{18,2},{1011,3},{20,4},{1013,5},{22,6},{1015,7},{2... | collective-permute-start | bytes 663560 | tf_op jit(solution)/shard_map/ppermute | solution.py:22
  71.0 6.7 %collective-permute-start.10 = (bf16[864,128]{1,0:T(8,128)(2,1)S(1)}, bf16[864,128]{1,0:T(8,128)(2,1)S(1)}, u32[]{:S(2)}, u32[]{:S(2)}) collective-permute-start(bf16[864,128]{1,0:T(8,128)(2,1)S(1)} %get-tuple-element.48), channel_id=1, source_target_pairs={{2,0},{3,1},{0,2},{1,3},{6,4},{7,5},{4,6},{5,7},{10,8},{11,9},{8,1... | collective-permute-start | bytes 663560 | tf_op jit(solution)/shard_map/ppermute | solution.py:22
  78.9 12.1 %collective-permute-start.11 = (bf16[432,128]{1,0:T(8,128)(2,1)S(1)}, bf16[432,128]{1,0:T(8,128)(2,1)S(1)}, u32[]{:S(2)}, u32[]{:S(2)}) collective-permute-start(bf16[432,128]{1,0:T(8,128)(2,1)S(1)} %get-tuple-element.50), channel_id=1, source_target_pairs={{2,0},{3,1},{0,2},{1,3},{6,4},{7,5},{4,6},{5,7},{10,8},{11,9},{8,1... | collective-permute-start | bytes 331784 | tf_op jit(solution)/shard_map/ppermute | solution.py:22
  80.8 11.3 %collective-permute-start.12 = (bf16[432,128]{1,0:T(8,128)(2,1)S(1)}, bf16[432,128]{1,0:T(8,128)(2,1)S(1)}, u32[]{:S(2)}, u32[]{:S(2)}) collective-permute-start(bf16[432,128]{1,0:T(8,128)(2,1)S(1)} %get-tuple-element.51), channel_id=1, source_target_pairs={{3,0},{2,1},{1,2},{0,3},{7,4},{6,5},{5,6},{4,7},{11,8},{10,9},{9,1... | collective-permute-start | bytes 331784 | tf_op jit(solution)/shard_map/ppermute | solution.py:22
  89.0 3.2 %collective-permute-start.13 = (bf16[432,128]{1,0:T(8,128)(2,1)S(1)}, bf16[432,128]{1,0:T(8,128)(2,1)S(1)}, u32[]{:S(2)}, u32[]{:S(2)}) collective-permute-start(bf16[432,128]{1,0:T(8,128)(2,1)S(1)} %get-tuple-element.52), channel_id=1, source_target_pairs={{1,0},{0,1},{3,2},{2,3},{5,4},{4,5},{7,6},{6,7},{9,8},{8,9},{11,10... | collective-permute-start | bytes 331784 | tf_op jit(solution)/shard_map/ppermute | solution.py:22
